TPU v7x, 32 devices: a whole 2x2x4 slice. The times are simulated.
32 devices in a mesh: fsdp: 4 (over y, x), seq: 8 (over z, core).
Axes of the slice: x: 2, y: 2, z: 4, core: 2. Of those that a mesh axis runs over, the one named last changes fastest.
Arguments:
- tokens: bfloat16 [4096, 1024], P(('fsdp', 'seq')), may hold values from -6 to 6
- condition: bfloat16 [4, 1024], P('fsdp'), may hold values from -6 to 6
- block_image: int32 [32], P('fsdp'), may hold values from 0 to 3, as said below
- cotangent: bfloat16 [4096, 1024], P(('fsdp', 'seq')), may hold values from -6 to 6
- modul_weight: float32 [1024, 6144], P(('fsdp', 'seq')), may hold values from -0.1875 to 0.1875
- qkv_weight: float32 [1024, 3072], P(('fsdp', 'seq')), may hold values from -0.1875 to 0.1875
- proj_weight: float32 [1024, 1024], P(('fsdp', 'seq')), may hold values from -0.75 to 0.75
- widen_weight: float32 [1024, 4096], P(('fsdp', 'seq')), may hold values from -0.1875 to 0.1875
- narrow_weight: float32 [4096, 1024], P(('fsdp', 'seq')), may hold values from -0.09375 to 0.09375
- bias_vector: float32 [14336], P(('fsdp', 'seq')), may hold values from -1.5 to 1.5
- modul_mean: float32 [1024, 6144], P(('fsdp', 'seq')), may hold values from -20 to 20
- qkv_mean: float32 [1024, 3072], P(('fsdp', 'seq')), may hold values from -20 to 20
- proj_mean: float32 [1024, 1024], P(('fsdp', 'seq')), may hold values from -20 to 20
- widen_mean: float32 [1024, 4096], P(('fsdp', 'seq')), may hold values from -20 to 20
- narrow_mean: float32 [4096, 1024], P(('fsdp', 'seq')), may hold values from -20 to 20
- bias_mean: float32 [14336], P(('fsdp', 'seq')), may hold values from -20 to 20
- modul_square: float32 [1024, 6144], P(('fsdp', 'seq')), may hold values from 53.248 to 212.992
- qkv_square: float32 [1024, 3072], P(('fsdp', 'seq')), may hold values from 53.248 to 212.992
- proj_square: float32 [1024, 1024], P(('fsdp', 'seq')), may hold values from 53.248 to 212.992
- widen_square: float32 [1024, 4096], P(('fsdp', 'seq')), may hold values from 53.248 to 212.992
- narrow_square: float32 [4096, 1024], P(('fsdp', 'seq')), may hold values from 53.248 to 212.992
- bias_square: float32 [14336], P(('fsdp', 'seq')), may hold values from 2048 to 8192
Outputs:
- block_output: bfloat16 [4096, 1024], P(('fsdp', 'seq'))
- tokens_grad: bfloat16 [4096, 1024], P(('fsdp', 'seq'))
- condition_grad: float32 [4, 1024], P('fsdp')
- modul_updated: float32 [1024, 6144], P(('fsdp', 'seq'))
- qkv_updated: float32 [1024, 3072], P(('fsdp', 'seq'))
- proj_updated: float32 [1024, 1024], P(('fsdp', 'seq'))
- widen_updated: float32 [1024, 4096], P(('fsdp', 'seq'))
- narrow_updated: float32 [4096, 1024], P(('fsdp', 'seq'))
- bias_updated: float32 [14336], P(('fsdp', 'seq'))
- modul_momentum: float32 [1024, 6144], P(('fsdp', 'seq'))
- qkv_momentum: float32 [1024, 3072], P(('fsdp', 'seq'))
- proj_momentum: float32 [1024, 1024], P(('fsdp', 'seq'))
- widen_momentum: float32 [1024, 4096], P(('fsdp', 'seq'))
- narrow_momentum: float32 [4096, 1024], P(('fsdp', 'seq'))
- bias_momentum: float32 [14336], P(('fsdp', 'seq'))
- modul_variance: float32 [1024, 6144], P(('fsdp', 'seq'))
- qkv_variance: float32 [1024, 3072], P(('fsdp', 'seq'))
- proj_variance: float32 [1024, 1024], P(('fsdp', 'seq'))
- widen_variance: float32 [1024, 4096], P(('fsdp', 'seq'))
- narrow_variance: float32 [4096, 1024], P(('fsdp', 'seq'))
- bias_variance: float32 [14336], P(('fsdp', 'seq'))
Inputs may be any that keep to these rules, and one draw needn't show every extreme that they name: `block_image`: every image is named by exactly 8 entries; the blocks held by fsdp index f (entries f * 8 * 1 to (f + 1) * 8 - 1) name only images f * 1 to (f + 1) - 1.
All inputs are finite; a program needn't handle non-finite values.
Results may differ from a plain program's by a relative error of at most 0.017.
The roundings to bfloat16 on the way count: a program that leaves them out, or rounds other values in their place, can miss the bound.
Values may be sent and summed in bfloat16 or wider, within the bound.
No kernel may reach another device: no remote copies, remote signals or barrier semaphores. Data moves between devices by JAX's collectives and lax.ppermute only.
A program may use at most 256 MiB of HBM per device.

v0:
```python
import math

import jax
import jax.numpy as jnp
from jax import lax
from jax.sharding import PartitionSpec as P

D = 1024
HEADS = 16
HEAD = 64
FF = 4096
BLOCK = 128
SEQ_LEN = 1024
STEP = 10


norm_eps = 1e-06
beta_first = 0.9
beta_second = 0.95
adam_eps = 1e-08
decay_rate = 0.01


def layer_norm(values):
    center = values - jnp.mean(values, axis=-1, keepdims=True)
    spread = jnp.mean(center * center, axis=-1, keepdims=True)
    return center * lax.rsqrt(spread + norm_eps)


def modulate(values, shift, scale):
    return layer_norm(values) * (1.0 + scale[:, None, :]) + shift[:, None, :]


def adam_step(weight, grad, first, second, rate):
    first = beta_first * first + (1.0 - beta_first) * grad
    second = beta_second * second + (1.0 - beta_second) * grad * grad
    fix_first = 1.0 - beta_first**STEP
    fix_second = 1.0 - beta_second**STEP
    weight = weight - rate * (
        first / fix_first / (jnp.sqrt(second / fix_second) + adam_eps) + decay_rate * weight
    )
    return (weight, first, second)


def column_sums(values):
    return jnp.sum(values.astype(jnp.float32), axis=0)


def shards(
    tokens,
    condition,
    block_image,
    cotangent,
    modul_weight,
    qkv_weight,
    proj_weight,
    widen_weight,
    narrow_weight,
    bias_vector,
    modul_mean,
    qkv_mean,
    proj_mean,
    widen_mean,
    narrow_mean,
    bias_mean,
    modul_square,
    qkv_square,
    proj_square,
    widen_square,
    narrow_square,
    bias_square,
):
    tok_count = tokens.shape[0]
    block_count = tok_count // BLOCK
    group_blocks = block_image.shape[0]
    images_group = condition.shape[0]
    per_image = SEQ_LEN // BLOCK
    head_scale = HEAD ** (-0.5)
    modul_low = modul_weight.astype(jnp.bfloat16)
    qkv_low = qkv_weight.astype(jnp.bfloat16)
    proj_low = proj_weight.astype(jnp.bfloat16)
    widen_low = widen_weight.astype(jnp.bfloat16)
    narrow_low = narrow_weight.astype(jnp.bfloat16)
    bias_low = bias_vector.astype(jnp.bfloat16)
    modul_full, qkv_full, proj_full, widen_full, narrow_full, bias_full = (
        lax.all_gather(modul_low, ("fsdp", "seq"), axis=0, tiled=True),
        lax.all_gather(qkv_low, ("fsdp", "seq"), axis=0, tiled=True),
        lax.all_gather(proj_low, ("fsdp", "seq"), axis=0, tiled=True),
        lax.all_gather(widen_low, ("fsdp", "seq"), axis=0, tiled=True),
        lax.all_gather(narrow_low, ("fsdp", "seq"), axis=0, tiled=True),
        lax.all_gather(bias_low, ("fsdp", "seq"), axis=0, tiled=True),
    )
    bias_all = bias_full.astype(jnp.float32)
    bias_mod = bias_all[: 6 * D]
    bias_query = bias_all[6 * D : 7 * D]
    bias_value = bias_all[7 * D : 8 * D]
    bias_proj = bias_all[8 * D : 9 * D]
    bias_widen = bias_all[9 * D : 9 * D + FF]
    bias_narrow = bias_all[9 * D + FF :]
    local_ids = block_image - lax.axis_index("fsdp") * images_group
    own_images = lax.dynamic_slice_in_dim(
        local_ids, lax.axis_index("seq") * block_count, block_count
    )
    image_pick = (own_images[:, None] == jnp.arange(images_group, dtype=jnp.int32)[None, :]).astype(
        jnp.float32
    )

    def blocks_of(image):
        return jnp.argsort((local_ids != image).astype(jnp.int32), stable=True)[:per_image]

    key_blocks = jax.vmap(blocks_of)(own_images)

    def pick_rows(whole):
        width = whole.shape[1]
        rows = whole.reshape(group_blocks, BLOCK, width)[key_blocks]
        return rows.reshape(block_count, SEQ_LEN, width)

    cond_float = condition.astype(jnp.float32)
    cond_act = jax.nn.silu(cond_float).astype(jnp.bfloat16)
    modulation = jnp.dot(cond_act, modul_full, preferred_element_type=jnp.float32) + bias_mod
    per_block = jnp.sum(image_pick[:, :, None] * modulation[None, :, :], axis=1)
    shift_a, scale_a, gate_a, shift_b, scale_b, gate_b = jnp.split(per_block, 6, axis=1)
    inputs = tokens.astype(jnp.float32).reshape(block_count, BLOCK, D)
    normed_a = modulate(inputs, shift_a, scale_a).astype(jnp.bfloat16).reshape(tok_count, D)
    qkv_bias = jnp.concatenate([bias_query, jnp.zeros((D,), jnp.float32), bias_value])
    qkv = (jnp.dot(normed_a, qkv_full, preferred_element_type=jnp.float32) + qkv_bias).astype(
        jnp.bfloat16
    )
    query_flat = qkv[:, :D]
    queries = query_flat.reshape(block_count, BLOCK, HEADS, HEAD)
    key_values = qkv[:, D:]
    group_pairs = lax.all_gather(key_values, "seq", axis=0, tiled=True)

    def select(whole):
        rows = pick_rows(whole).reshape(block_count, SEQ_LEN, 2, HEADS, HEAD)
        return (rows[:, :, 0], rows[:, :, 1])

    def scores_of(keys):
        return (
            jnp.einsum("bqhd,bkhd->bhqk", queries, keys, preferred_element_type=jnp.float32)
            * head_scale
        )

    keys_fwd, values_fwd = select(group_pairs)
    scores = scores_of(keys_fwd)
    log_total = jax.nn.logsumexp(scores, axis=-1, keepdims=True)
    probs_low = jnp.exp(scores - log_total).astype(jnp.bfloat16)
    attended = jnp.einsum(
        "bhqk,bkhd->bqhd", probs_low, values_fwd, preferred_element_type=jnp.float32
    )
    attended = attended.astype(jnp.bfloat16).reshape(tok_count, D)
    branch_a = (
        jnp.dot(attended, proj_full, preferred_element_type=jnp.float32) + bias_proj
    ).reshape(block_count, BLOCK, D)
    middle = inputs + gate_a[:, None, :] * branch_a
    normed_b = modulate(middle, shift_b, scale_b).astype(jnp.bfloat16).reshape(tok_count, D)
    widened = jnp.dot(normed_b, widen_full, preferred_element_type=jnp.float32) + bias_widen
    activated = jax.nn.gelu(widened, approximate=True).astype(jnp.bfloat16)
    branch_b = (
        jnp.dot(activated, narrow_full, preferred_element_type=jnp.float32) + bias_narrow
    ).reshape(block_count, BLOCK, D)
    block_output = (
        (middle + gate_b[:, None, :] * branch_b).reshape(tok_count, D).astype(jnp.bfloat16)
    )
    modul_back, qkv_back, proj_back, widen_back, narrow_back = (
        lax.all_gather(modul_low, ("fsdp", "seq"), axis=0, tiled=True),
        lax.all_gather(qkv_low, ("fsdp", "seq"), axis=0, tiled=True),
        lax.all_gather(proj_low, ("fsdp", "seq"), axis=0, tiled=True),
        lax.all_gather(widen_low, ("fsdp", "seq"), axis=0, tiled=True),
        lax.all_gather(narrow_low, ("fsdp", "seq"), axis=0, tiled=True),
    )
    pairs_back = lax.all_gather(key_values, "seq", axis=0, tiled=True)
    grad_out = cotangent.astype(jnp.float32).reshape(block_count, BLOCK, D)
    d_gate_b = jnp.sum(grad_out * branch_b, axis=1)
    d_narrow = (gate_b[:, None, :] * grad_out).astype(jnp.bfloat16).reshape(tok_count, D)
    grad_narrow = jnp.einsum("tf,td->fd", activated, d_narrow, preferred_element_type=jnp.float32)
    bias_g_narrow = column_sums(d_narrow)
    d_activated = jnp.einsum("td,fd->tf", d_narrow, narrow_back, preferred_element_type=jnp.float32)
    gelu_pull = jax.vjp(lambda values: jax.nn.gelu(values, approximate=True), widened)[1]
    d_widened = gelu_pull(d_activated)[0].astype(jnp.bfloat16)
    grad_widen = jnp.einsum("td,tf->df", normed_b, d_widened, preferred_element_type=jnp.float32)
    bias_g_widen = column_sums(d_widened)
    widen_sum, narrow_sum = (
        lax.psum_scatter(grad_widen, ("fsdp", "seq"), scatter_dimension=0, tiled=True),
        lax.psum_scatter(grad_narrow, ("fsdp", "seq"), scatter_dimension=0, tiled=True),
    )
    d_normed_b = jnp.einsum(
        "tf,df->td", d_widened, widen_back, preferred_element_type=jnp.float32
    ).reshape(block_count, BLOCK, D)
    mlp_pull = jax.vjp(modulate, middle, shift_b, scale_b)[1]
    d_middle_norm, d_shift_b, d_scale_b = mlp_pull(d_normed_b)
    d_middle = grad_out + d_middle_norm
    d_gate_a = jnp.sum(d_middle * branch_a, axis=1)
    d_branch = (gate_a[:, None, :] * d_middle).astype(jnp.bfloat16).reshape(tok_count, D)
    grad_proj = jnp.einsum("td,te->de", attended, d_branch, preferred_element_type=jnp.float32)
    bias_g_proj = column_sums(d_branch)
    d_attended = jnp.einsum("te,de->td", d_branch, proj_back, preferred_element_type=jnp.float32)
    d_att_flat = d_attended.astype(jnp.bfloat16)
    d_attended = d_att_flat.reshape(block_count, BLOCK, HEADS, HEAD)
    keys_back, values_back = select(pairs_back)
    probs = jnp.exp(scores_of(keys_back) - log_total)
    d_probs = jnp.einsum(
        "bqhd,bkhd->bhqk", d_attended, values_back, preferred_element_type=jnp.float32
    )
    row_term = jnp.sum(probs * d_probs, axis=-1, keepdims=True)
    d_scores = (probs * (d_probs - row_term)).astype(jnp.bfloat16)
    d_queries = (
        jnp.einsum("bhqk,bkhd->bqhd", d_scores, keys_back, preferred_element_type=jnp.float32)
        * head_scale
    )
    d_values = jnp.einsum(
        "bhqk,bqhd->bkhd",
        probs.astype(jnp.bfloat16),
        d_attended,
        preferred_element_type=jnp.float32,
    )
    d_keys = (
        jnp.einsum("bhqk,bqhd->bkhd", d_scores, queries, preferred_element_type=jnp.float32)
        * head_scale
    )
    d_selected = jnp.stack([d_keys, d_values], axis=2).reshape(block_count, per_image, BLOCK, 2 * D)
    d_group = jnp.zeros((group_blocks, BLOCK, 2 * D), jnp.float32).at[key_blocks].add(d_selected)
    d_pairs = lax.psum_scatter(
        d_group.reshape(group_blocks * BLOCK, 2 * D), "seq", scatter_dimension=0, tiled=True
    )
    d_qkv = jnp.concatenate([d_queries.reshape(tok_count, D), d_pairs], axis=1).astype(jnp.bfloat16)
    grad_qkv = jnp.einsum("td,te->de", normed_a, d_qkv, preferred_element_type=jnp.float32)
    bias_g_query = column_sums(d_qkv[:, :D])
    bias_g_value = column_sums(d_qkv[:, 2 * D :])
    d_normed_a = jnp.einsum(
        "te,de->td", d_qkv, qkv_back, preferred_element_type=jnp.float32
    ).reshape(block_count, BLOCK, D)
    attn_pull = jax.vjp(modulate, inputs, shift_a, scale_a)[1]
    d_inputs_norm, d_shift_a, d_scale_a = attn_pull(d_normed_a)
    tokens_grad = (d_middle + d_inputs_norm).reshape(tok_count, D).astype(jnp.bfloat16)
    d_block = jnp.concatenate(
        [d_shift_a, d_scale_a, d_gate_a, d_shift_b, d_scale_b, d_gate_b], axis=1
    )
    d_modulation = jnp.sum(image_pick[:, :, None] * d_block[:, None, :], axis=0)
    grad_modul = jnp.dot(
        cond_act.astype(jnp.float32).T, d_modulation, precision=lax.Precision.HIGHEST
    )
    bias_g_mod = jnp.sum(d_modulation, axis=0)
    d_cond_part = jnp.einsum(
        "im,dm->id",
        d_modulation,
        modul_back,
        precision=lax.Precision.HIGHEST,
        preferred_element_type=jnp.float32,
    )
    bias_grad = jnp.concatenate(
        [bias_g_mod, bias_g_query, bias_g_value, bias_g_proj, bias_g_widen, bias_g_narrow]
    )
    proj_sum, qkv_sum, modul_sum, bias_sum = (
        lax.psum_scatter(grad_proj, ("fsdp", "seq"), scatter_dimension=0, tiled=True),
        lax.psum_scatter(grad_qkv, ("fsdp", "seq"), scatter_dimension=0, tiled=True),
        lax.psum_scatter(grad_modul, ("fsdp", "seq"), scatter_dimension=0, tiled=True),
        lax.psum_scatter(bias_grad, ("fsdp", "seq"), scatter_dimension=0, tiled=True),
    )
    d_cond_act = lax.psum(d_cond_part, "seq")
    silu_pull = jax.vjp(jax.nn.silu, cond_float)[1]
    condition_grad = silu_pull(d_cond_act)[0]
    rate_wide = 2.0 / math.sqrt(D)
    modul_updated, modul_momentum, modul_variance = adam_step(
        modul_weight, modul_sum, modul_mean, modul_square, rate_wide
    )
    qkv_updated, qkv_momentum, qkv_variance = adam_step(
        qkv_weight, qkv_sum, qkv_mean, qkv_square, rate_wide
    )
    proj_updated, proj_momentum, proj_variance = adam_step(
        proj_weight, proj_sum, proj_mean, proj_square, 2.0 / math.sqrt(D // 16)
    )
    widen_updated, widen_momentum, widen_variance = adam_step(
        widen_weight, widen_sum, widen_mean, widen_square, rate_wide
    )
    narrow_updated, narrow_momentum, narrow_variance = adam_step(
        narrow_weight, narrow_sum, narrow_mean, narrow_square, 2.0 / math.sqrt(FF)
    )
    bias_updated, bias_momentum, bias_variance = adam_step(
        bias_vector, bias_sum, bias_mean, bias_square, 0.5
    )
    return (
        block_output,
        tokens_grad,
        condition_grad,
        modul_updated,
        qkv_updated,
        proj_updated,
        widen_updated,
        narrow_updated,
        bias_updated,
        modul_momentum,
        qkv_momentum,
        proj_momentum,
        widen_momentum,
        narrow_momentum,
        bias_momentum,
        modul_variance,
        qkv_variance,
        proj_variance,
        widen_variance,
        narrow_variance,
        bias_variance,
    )


def solution(mesh):
    placed = (
        P(("fsdp", "seq"), None),
        P("fsdp", None),
        P("fsdp"),
        P(("fsdp", "seq"), None),
        P(("fsdp", "seq"), None),
        P(("fsdp", "seq"), None),
        P(("fsdp", "seq"), None),
        P(("fsdp", "seq"), None),
        P(("fsdp", "seq"), None),
        P(("fsdp", "seq")),
        P(("fsdp", "seq"), None),
        P(("fsdp", "seq"), None),
        P(("fsdp", "seq"), None),
        P(("fsdp", "seq"), None),
        P(("fsdp", "seq"), None),
        P(("fsdp", "seq")),
        P(("fsdp", "seq"), None),
        P(("fsdp", "seq"), None),
        P(("fsdp", "seq"), None),
        P(("fsdp", "seq"), None),
        P(("fsdp", "seq"), None),
        P(("fsdp", "seq")),
    )
    return jax.shard_map(
        shards,
        mesh=mesh,
        in_specs=placed,
        out_specs=(
            P(("fsdp", "seq"), None),
            P(("fsdp", "seq"), None),
            P("fsdp", None),
            P(("fsdp", "seq"), None),
            P(("fsdp", "seq"), None),
            P(("fsdp", "seq"), None),
            P(("fsdp", "seq"), None),
            P(("fsdp", "seq"), None),
            P(("fsdp", "seq")),
            P(("fsdp", "seq"), None),
            P(("fsdp", "seq"), None),
            P(("fsdp", "seq"), None),
            P(("fsdp", "seq"), None),
            P(("fsdp", "seq"), None),
            P(("fsdp", "seq")),
            P(("fsdp", "seq"), None),
            P(("fsdp", "seq"), None),
            P(("fsdp", "seq"), None),
            P(("fsdp", "seq"), None),
            P(("fsdp", "seq"), None),
            P(("fsdp", "seq")),
        ),
        check_vma=False,
    )
```

profile of v0, /device:TPU:0, one launch (start us, length us, event | category | flops | bytes accessed | tf_op | source)
XLA Modules:
  0.0 1564.8 jit_solution(16607978279763247215)
XLA Ops:
  11.9 42.7 %all-reduce = bf16[14336]{0:T(1024)(128)(2,1)S(1)} all-reduce(bf16[14336]{0:T(1024)(128)(2,1)S(1)} %dynamic-update-slice), channel_id=1, replica_groups=mesh['fsdp'=4,'seq'=8] {'fsdp','seq'}, use_global_device_ids=true, to_apply=%add | all-reduce | flops 14336 | bytes 57344
  60.7 50.8 %all-gather.7.cloned.1.call-done = bf16[1024,6144]{1,0:T(8,128)(2,1)} async-done(((bf16[32,6144]{1,0:T(8,128)(2,1)}), bf16[1024,6144]{1,0:T(8,128)(2,1)}) %all-gather.7.cloned.1.call-update) | async-done | bytes 12582928 | tf_op jit(solution)/shard_map/all_gather | solution.py:86
  111.5 6.4 fusion.48
  118.5 64.3 %all-gather.9.cloned.1.call-done = bf16[1024,3072]{1,0:T(8,128)(2,1)} async-done(((bf16[32,3072]{1,0:T(8,128)(2,1)}), bf16[1024,3072]{1,0:T(8,128)(2,1)}) %all-gather.9.cloned.1.call-update) | async-done | bytes 6291472 | tf_op jit(solution)/shard_map/all_gather | solution.py:87
  191.8 41.7 %all-gather.11.cloned.1.call-done = bf16[1024,2048]{1,0:T(8,128)(2,1)} async-done(((bf16[128,2048]{1,0:T(8,128)(2,1)}), bf16[1024,2048]{1,0:T(8,128)(2,1)}) %all-gather.11.cloned.1.call-update) | async-done | bytes 4194320 | tf_op jit(solution)/shard_map/all_gather | solution.py:132
  238.4 6.8 copy.62
  245.1 7.4 reshape_reshape.4
  262.7 29.4 %all-gather.13.cloned.1.call-done = bf16[1024,1024]{1,0:T(8,128)(2,1)} async-done(((bf16[32,1024]{1,0:T(8,128)(2,1)}), bf16[1024,1024]{1,0:T(8,128)(2,1)}) %all-gather.13.cloned.1.call-update) | async-done | bytes 2097168 | tf_op jit(solution)/shard_map/all_gather | solution.py:88
  295.7 75.9 %all-gather.15.cloned.1.call-done = bf16[1024,4096]{1,0:T(8,128)(2,1)} async-done(((bf16[32,4096]{1,0:T(8,128)(2,1)}), bf16[1024,4096]{1,0:T(8,128)(2,1)}) %all-gather.15.cloned.1.call-update) | async-done | bytes 8388624 | tf_op jit(solution)/shard_map/all_gather | solution.py:89
  376.5 8.2 fusion.37
  384.7 185.3 %reduce-scatter.17.cloned.1.call-done = f32[128,1024]{1,0:T(8,128)} async-done(((f32[4096,1024]{1,0:T(8,128)}), f32[128,1024]{1,0:T(8,128)}) %reduce-scatter.17.cloned.1.call-update) | async-done | bytes 524304 | tf_op jit(solution)/shard_map/reduce_scatter | solution.py:185
  573.6 75.1 %all-gather.17.cloned.1.call-done = bf16[4096,1024]{1,0:T(8,128)(2,1)} async-done(((bf16[128,1024]{1,0:T(8,128)(2,1)}), bf16[4096,1024]{1,0:T(8,128)(2,1)}) %all-gather.17.cloned.1.call-update) | async-done | bytes 8388624 | tf_op jit(solution)/shard_map/all_gather | solution.py:90
  648.7 7.8 convert_reduce_fusion
  656.6 7.4 multiply_reduce_fusion.2
  669.4 7.3 convolution_bitcast_fusion
  676.6 5.8 multiply_reduce_fusion
  690.0 5.3 copy.67
  695.3 9.3 copy.65
  708.9 17.4 %scatter_fusion = f32[8,128,2048]{2,1,0:T(8,128)} fusion(f32[8,128,2048]{2,1,0:T(8,128)} %broadcast_in_dim.23, s32[8]{0:T(128)S(1)} %copy-done.49, f32[8,128,2048]{2,1,0:T(8,128)} %copy.65), kind=kCustom, calls=%fused_computation.1 | custom fusion | flops 2097152 | bytes 25165856 | tf_op jit(solution)/shard_map/scatter-add | solution.py:222
  730.0 5.1 fusion.14
  735.3 79.4 %reduce-scatter.7.cloned.1.call-done = f32[128,2048]{1,0:T(8,128)} async-done(((f32[1024,2048]{1,0:T(8,128)}), f32[128,2048]{1,0:T(8,128)}) %reduce-scatter.7.cloned.1.call-update) | async-done | bytes 1048592 | tf_op jit(solution)/shard_map/reduce_scatter | solution.py:223
  816.0 6.4 fusion.34
  823.6 8.2 fusion.62
  832.5 5.1 fusion.29
  838.1 11.6 broadcast_multiply_fusion
  849.9 107.9 %reduce-scatter.13.cloned.1.call-done = f32[32,1024]{1,0:T(8,128)} async-done(((f32[1024,1024]{1,0:T(8,128)}), f32[32,1024]{1,0:T(8,128)}) %reduce-scatter.13.cloned.1.call-update) | async-done | bytes 131088 | tf_op jit(solution)/shard_map/reduce_scatter | solution.py:255
  959.6 12.8 fusion.73
  972.5 13.7 psum.7
  986.4 38.0 %all-reduce.1 = f32[14336]{0:T(1024)S(1)} all-reduce(f32[14336]{0:T(1024)S(1)} %constant_dynamic-update-slice_fusion.5), channel_id=8, replica_groups=mesh['fsdp'=4,'seq'=8] {'fsdp','seq'}, use_global_device_ids=true, to_apply=%region_31.32.clone | all-reduce | flops 14336 | bytes 114688
  1026.6 89.3 %reduce-scatter.11.cloned.1.call-done = f32[32,3072]{1,0:T(8,128)} async-done(((f32[1024,3072]{1,0:T(8,128)}), f32[32,3072]{1,0:T(8,128)}) %reduce-scatter.11.cloned.1.call-update) | async-done | bytes 393232 | tf_op jit(solution)/shard_map/reduce_scatter | solution.py:256
  1118.4 185.8 %reduce-scatter.15.cloned.1.call-done = f32[32,4096]{1,0:T(8,128)} async-done(((f32[1024,4096]{1,0:T(8,128)}), f32[32,4096]{1,0:T(8,128)}) %reduce-scatter.15.cloned.1.call-update) | async-done | bytes 524304 | tf_op jit(solution)/shard_map/reduce_scatter | solution.py:184
  1306.9 247.9 %reduce-scatter.9.cloned.1.call-done = f32[32,6144]{1,0:T(8,128)} async-done(((f32[1024,6144]{1,0:T(8,128)}), f32[32,6144]{1,0:T(8,128)}) %reduce-scatter.9.cloned.1.call-update) | async-done | bytes 786448 | tf_op jit(solution)/shard_map/reduce_scatter | solution.py:257
  (240 shorter events, 83.4 us)
Async XLA Ops:
  7.2 104.3 %all-gather.7.cloned.1.call-start = ((), (), s32[]{:S(2)}) async-start(), calls=%async_computation.6 | async-start | bytes 12976128 | tf_op jit(solution)/shard_map/all_gather | solution.py:86
  9.2 173.6 %all-gather.9.cloned.1.call-start = ((), (), s32[]{:S(2)}) async-start(), calls=%async_computation.7 | async-start | bytes 6488064 | tf_op jit(solution)/shard_map/all_gather | solution.py:87
  11.0 222.5 %all-gather.11.cloned.1.call-start = ((), (), s32[]{:S(2)}) async-start(), calls=%async_computation.8 | async-start | bytes 4718592 | tf_op jit(solution)/shard_map/all_gather | solution.py:132
  58.2 124.6 %copy-start.30 = (f32[128]{0:T(128)}, f32[128]{0:T(128)S(1)}, u32[]{:S(2)}) copy-start(f32[128]{0:T(128)S(1)} %broadcast_multiply_fusion.3) | copy-start | bytes 1540
  59.4 123.4 %copy-start.35 = (f32[128]{0:T(128)}, f32[128]{0:T(128)S(1)}, u32[]{:S(2)}) copy-start(f32[128]{0:T(128)S(1)} %fusion.53) | copy-start | bytes 1540
  111.5 71.3 %copy-start.4 = (bf16[128,1024]{1,0:T(8,128)(2,1)S(1)}, bf16[128,1024]{1,0:T(8,128)(2,1)}, u32[]{:S(2)}) copy-start(bf16[128,1024]{1,0:T(8,128)(2,1)} %param.22) | copy-start | bytes 786436
  118.5 173.6 %copy-start.44 = (f32[1,1024]{1,0:T(1,128)}, f32[1,1024]{1,0:T(1,128)S(1)}, u32[]{:S(2)}) copy-start(f32[1,1024]{1,0:T(1,128)S(1)} %get-tuple-element.73) | copy-start | bytes 12292
  187.6 104.5 %all-gather.13.cloned.1.call-start = ((), (), s32[]{:S(2)}) async-start(), calls=%async_computation.9 | async-start | bytes 2162688 | tf_op jit(solution)/shard_map/all_gather | solution.py:88
  188.3 183.3 %all-gather.15.cloned.1.call-start = ((), (), s32[]{:S(2)}) async-start(), calls=%async_computation.10 | async-start | bytes 8650752 | tf_op jit(solution)/shard_map/all_gather | solution.py:89
  189.2 380.9 %reduce-scatter.17.cloned.1.call-start = ((), (), s32[]{:S(2)}) async-start(), calls=%async_computation.17 | async-start | bytes 17301504 | tf_op jit(solution)/shard_map/reduce_scatter | solution.py:185
  295.0 76.7 %copy-start.32 = (f32[128]{0:T(128)}, f32[128]{0:T(128)S(1)}, u32[]{:S(2)}) copy-start(f32[128]{0:T(128)S(1)} %broadcast_multiply_fusion.2) | copy-start | bytes 1540
  295.2 76.5 %copy-start.62 = (f32[128]{0:T(128)}, f32[128]{0:T(128)S(1)}, u32[]{:S(2)}) copy-start(f32[128]{0:T(128)S(1)} %multiply_reduce_fusion.5) | copy-start | bytes 1540
  384.7 264.1 %all-gather.17.cloned.1.call-start = ((), (), s32[]{:S(2)}) async-start(), calls=%async_computation.11 | async-start | bytes 8650752 | tf_op jit(solution)/shard_map/all_gather | solution.py:90
  573.3 241.4 %reduce-scatter.7.cloned.1.call-start = ((), (), s32[]{:S(2)}) async-start(), calls=%async_computation.12 | async-start | bytes 9437184 | tf_op jit(solution)/shard_map/reduce_scatter | solution.py:223
  726.3 231.5 %reduce-scatter.13.cloned.1.call-start = ((), (), s32[]{:S(2)}) async-start(), calls=%async_computation.15 | async-start | bytes 4325376 | tf_op jit(solution)/shard_map/reduce_scatter | solution.py:255
  730.0 86.0 %copy-start.31 = (f32[128]{0:T(128)S(1)}, f32[128]{0:T(128)}, u32[]{:S(2)}) copy-start(f32[128]{0:T(128)} %copy-done.30) | copy-start | bytes 1540
  730.0 86.0 %copy-start.36 = (f32[128]{0:T(128)S(1)}, f32[128]{0:T(128)}, u32[]{:S(2)}) copy-start(f32[128]{0:T(128)} %copy-done.35) | copy-start | bytes 1540
  730.0 386.0 %reduce-scatter.11.cloned.1.call-start = ((), (), s32[]{:S(2)}) async-start(), calls=%async_computation.14 | async-start | bytes 12976128 | tf_op jit(solution)/shard_map/reduce_scatter | solution.py:256
  822.4 481.7 %reduce-scatter.15.cloned.1.call-start = ((), (), s32[]{:S(2)}) async-start(), calls=%async_computation.16 | async-start | bytes 17301504 | tf_op jit(solution)/shard_map/reduce_scatter | solution.py:184
  831.8 723.0 %reduce-scatter.9.cloned.1.call-start = ((), (), s32[]{:S(2)}) async-start(), calls=%async_computation.13 | async-start | bytes 25952256 | tf_op jit(solution)/shard_map/reduce_scatter | solution.py:257
  849.7 108.1 %copy-start.25 = (f32[32,1024]{1,0:T(8,128)S(1)}, f32[32,1024]{1,0:T(8,128)}, u32[]{:S(2)}) copy-start(f32[32,1024]{1,0:T(8,128)} %param.34) | copy-start | bytes 393220
  849.7 108.1 %copy-start.26 = (f32[32,1024]{1,0:T(8,128)S(1)}, f32[32,1024]{1,0:T(8,128)}, u32[]{:S(2)}) copy-start(f32[32,1024]{1,0:T(8,128)} %param.40) | copy-start | bytes 393220
  959.6 65.5 %copy-start.27 = (bf16[1,1024]{1,0:T(2,128)(2,1)S(1)}, bf16[1,1024]{1,0:T(2,128)(2,1)}, u32[]{:S(2)}) copy-start(bf16[1,1024]{1,0:T(2,128)(2,1)} %param.23) | copy-start | bytes 6148
  959.6 65.5 %copy-start.29 = (f32[1,1024]{1,0:T(1,128)S(1)}, f32[1,1024]{1,0:T(1,128)}, u32[]{:S(2)}) copy-start(f32[1,1024]{1,0:T(1,128)} %copy-done.28) | copy-start | bytes 12292
  959.6 66.0 %copy-start.12 = (f32[128,1024]{1,0:T(8,128)S(1)}, f32[128,1024]{1,0:T(8,128)}, u32[]{:S(2)}) copy-start(f32[128,1024]{1,0:T(8,128)} %copy-done.11) | copy-start | bytes 1572868
  959.6 66.0 %copy-start.16 = (bf16[128,1024]{1,0:T(8,128)(2,1)S(1)}, bf16[128,1024]{1,0:T(8,128)(2,1)}, u32[]{:S(2)}) copy-start(bf16[128,1024]{1,0:T(8,128)(2,1)} %param.25) | copy-start | bytes 786436
  959.6 66.0 %copy-start.60 = (f32[128]{0:T(128)S(1)}, f32[128]{0:T(128)}, u32[]{:S(2)}) copy-start(f32[128]{0:T(128)} %copy-done.59) | copy-start | bytes 1540
  959.6 156.3 %copy-start.13 = (f32[32,3072]{1,0:T(8,128)S(1)}, f32[32,3072]{1,0:T(8,128)}, u32[]{:S(2)}) copy-start(f32[32,3072]{1,0:T(8,128)} %param.27) | copy-start | bytes 1179652
  972.5 331.7 %copy-start.10 = (f32[32,4096]{1,0:T(8,128)S(1)}, f32[32,4096]{1,0:T(8,128)}, u32[]{:S(2)}) copy-start(f32[32,4096]{1,0:T(8,128)} %param.29) | copy-start | bytes 1572868
  986.3 568.5 %copy-start.8 = (f32[32,6144]{1,0:T(8,128)S(1)}, f32[32,6144]{1,0:T(8,128)}, u32[]{:S(2)}) copy-start(f32[32,6144]{1,0:T(8,128)} %param.26) | copy-start | bytes 2359300
  1026.6 528.2 %copy-start.19 = (f32[32,6144]{1,0:T(8,128)S(1)}, f32[32,6144]{1,0:T(8,128)}, u32[]{:S(2)}) copy-start(f32[32,6144]{1,0:T(8,128)} %param.32) | copy-start | bytes 2359300
  1118.4 436.4 %copy-start.20 = (f32[32,6144]{1,0:T(8,128)S(1)}, f32[32,6144]{1,0:T(8,128)}, u32[]{:S(2)}) copy-start(f32[32,6144]{1,0:T(8,128)} %param.38) | copy-start | bytes 2359300
  (47 other events, 637.6 us)
Sparse Core Ops, SparseCore 0:
  11.6 99.8 all-gather.6
  115.1 67.6 all-gather.8
  187.7 45.6 all-gather.10
  236.8 55.1 all-gather.12
  295.5 76.1 all-gather.14
  384.8 185.2 reduce-scatter.16
  573.6 75.0 all-gather.16
  726.5 88.1 reduce-scatter.6
  817.0 140.7 reduce-scatter.12
  963.7 152.2 reduce-scatter.10
  1118.4 185.7 reduce-scatter.14
  1311.6 243.1 reduce-scatter.8
where the time goes:
time: 1570 us; the launch traced here: 1560 us
  waiting for transfers between devices  1230 us (78%)
  matrix products  104 us (7%)
  blocking collectives  94.3 us (6%)
  other arithmetic  66.4 us (4%)
  local copies, waits for them, and re-layouts  49.4 us (3%)
  between operations  16 us (1%)
    reduce_scatter x1, waiting for transfers between devices, shards(): lax.psum_scatter(grad_modul, ('fsdp', 'seq'), scatter_dimension=0, tiled=...  248 us
    reduce_scatter x1, waiting for transfers between devices, shards(): lax.psum_scatter(grad_widen, ('fsdp', 'seq'), scatter_dimension=0, tiled=...  186 us
    reduce_scatter x1, waiting for transfers between devices, shards(): lax.psum_scatter(grad_narrow, ('fsdp', 'seq'), scatter_dimension=0, tiled...  185 us
    reduce_scatter x1, waiting for transfers between devices, shards(): lax.psum_scatter(grad_proj, ('fsdp', 'seq'), scatter_dimension=0, tiled=T...  108 us
    reduce_scatter x1, waiting for transfers between devices, shards(): lax.psum_scatter(grad_qkv, ('fsdp', 'seq'), scatter_dimension=0, tiled=True)  89.3 us
    unnamed x2, blocking collectives  80.6 us
    reduce_scatter x1, waiting for transfers between devices, shards(): lax.psum_scatter(d_group.reshape(group_blocks * BLOCK, 2 * D), 'seq', sca...  79.4 us
    all_gather x1, waiting for transfers between devices, shards(): lax.all_gather(widen_low, ('fsdp', 'seq'), axis=0, tiled=True)  75.9 us
  transfers between devices with their start and end apart: 12, of which 12 were waited for; matrix products, arithmetic and copies ran while one was open for 7% of the time, Pallas kernels for 0%

commit v1 on v0

v1 whole, which is shorter than its diff:
```python
import math

import jax
import jax.numpy as jnp
from jax import lax
from jax.sharding import PartitionSpec as P

D = 1024
HEADS = 16
HEAD = 64
FF = 4096
BLOCK = 128
SEQ_LEN = 1024
STEP = 10

CORES = 2

norm_eps = 1e-06
beta_first = 0.9
beta_second = 0.95
adam_eps = 1e-08
decay_rate = 0.01

f32 = jnp.float32
bf16 = jnp.bfloat16


def adam_step(weight, grad, first, second, rate):
    first = beta_first * first + (1.0 - beta_first) * grad
    second = beta_second * second + (1.0 - beta_second) * grad * grad
    fix_first = 1.0 - beta_first**STEP
    fix_second = 1.0 - beta_second**STEP
    weight = weight - rate * (
        first / fix_first / (jnp.sqrt(second / fix_second) + adam_eps) + decay_rate * weight
    )
    return (weight, first, second)


def normalize(values):
    center = values - jnp.mean(values, axis=-1, keepdims=True)
    spread = jnp.mean(center * center, axis=-1, keepdims=True)
    scale = lax.rsqrt(spread + norm_eps)
    return center * scale, scale


def norm_back(grad, normed, scale):
    mean_g = jnp.mean(grad, axis=-1, keepdims=True)
    mean_gn = jnp.mean(grad * normed, axis=-1, keepdims=True)
    return (grad - mean_g - normed * mean_gn) * scale


def matmul(left, right):
    return jnp.dot(left, right, preferred_element_type=f32)


def column_sums(values):
    return jnp.sum(values.astype(f32), axis=0)


def tree_sum(parts):
    while len(parts) > 1:
        parts = [parts[i] + parts[i + 1] for i in range(0, len(parts), 2)]
    return parts[0]


def xor_take(values, mask):
    order = jnp.arange(values.shape[0], dtype=jnp.int32) ^ mask
    return jnp.take(values, order, axis=0, mode="clip")


def xor_parts(parts, mask):
    step = 1
    while step < len(parts):
        turned = (mask & step) != 0
        parts = [jnp.where(turned, parts[i ^ step], parts[i]) for i in range(len(parts))]
        step *= 2
    return parts


def make_shards(n_f, n_z):
    n_s = n_z * CORES
    n_g = n_f * n_s
    heads_dev = HEADS // n_s
    hd = heads_dev * HEAD
    ub = FF // n_g
    rows = D // n_g
    units = n_z * ub

    def swap(values, axis, size, k):
        if k == 0:
            return values
        return lax.ppermute(values, axis, [(i, i ^ k) for i in range(size)])

    def swap_f(values, k):
        return swap(values, "fsdp", n_f, k)

    def swap_z(values, k):
        return swap(values, "z", n_z, k)

    def swap_c(values):
        return swap(values, "core", CORES, 1)

    def all_z(values):
        return [swap_z(values, k) for k in range(n_z)]

    def all_f(values):
        return [swap_f(values, k) for k in range(n_f)]

    def swap_rows_seq(values):
        both = jnp.stack([values[:, 0], swap_c(values[:, 1])], axis=1)
        return jnp.stack([swap_z(both[k], k) for k in range(n_z)])

    def reduce_seq(values):
        values = values + swap_c(values)
        return tree_sum(all_z(values))

    def shards(
        tokens,
        condition,
        block_image,
        cotangent,
        modul_weight,
        qkv_weight,
        proj_weight,
        widen_weight,
        narrow_weight,
        bias_vector,
        modul_mean,
        qkv_mean,
        proj_mean,
        widen_mean,
        narrow_mean,
        bias_mean,
        modul_square,
        qkv_square,
        proj_square,
        widen_square,
        narrow_square,
        bias_square,
    ):
        images_group = condition.shape[0]
        tok_group = n_s * BLOCK
        head_scale = HEAD ** (-0.5)
        at_f = lax.axis_index("fsdp")
        at_z = lax.axis_index("z")
        at_c = lax.axis_index("core")
        at_s = at_z * CORES + at_c
        at_g = at_f * n_s + at_s
        first_core = at_c == 0
        local_ids = block_image - at_f * images_group

        def own_other(values, axis):
            zero = lax.index_in_dim(values, 0, axis, keepdims=False)
            one = lax.index_in_dim(values, 1, axis, keepdims=False)
            return jnp.where(first_core, zero, one), jnp.where(first_core, one, zero)

        width = bias_vector.shape[0]
        pad = -(-width // 1024) * 1024
        small = jnp.concatenate(
            [
                jnp.pad(bias_vector.astype(bf16), (0, pad - width)).reshape(-1, 128),
                condition.reshape(-1, 128),
            ]
        )
        small = lax.all_gather(small, ("fsdp", "z", "core"), axis=0, tiled=False)
        bias_all = small[:, : pad // 128].reshape(n_g, pad)[:, :width].reshape(-1).astype(f32)
        cond_all = small.reshape(n_f, n_s, -1, 128)[:, 0, pad // 128 :]
        cond_all = cond_all.reshape(n_f * images_group, D).astype(f32)
        bias_mod = bias_all[: 6 * D]
        bias_query = bias_all[6 * D : 7 * D].reshape(n_s, hd)
        bias_value = bias_all[7 * D : 8 * D].reshape(n_s, hd)
        bias_proj = bias_all[8 * D : 9 * D]
        bias_widen = bias_all[9 * D : 9 * D + FF].reshape(n_f, n_z, CORES, ub)
        bias_narrow = bias_all[9 * D + FF :]

        modul_low = modul_weight.astype(bf16)
        modul_rows = lax.all_gather(modul_low, "fsdp", axis=0, tiled=True)

        tokens_z = jnp.stack(all_z(tokens))
        tokens_group = jnp.stack([tokens_z, swap_c(tokens_z)], axis=1).reshape(n_s, BLOCK, D)

        qkv_low = qkv_weight.astype(bf16).reshape(rows, 3, n_s, hd)
        qkv_out = xor_take(qkv_low.transpose(2, 0, 1, 3), at_s).reshape(n_z, CORES, rows, 3 * hd)
        qkv_mine = swap_rows_seq(qkv_out).reshape(n_s, rows, 3 * hd)
        qkv_in = jnp.stack(all_f(qkv_mine)).reshape(n_g, rows, 3 * hd)
        qkv_full = xor_take(qkv_in, at_g).reshape(D, 3 * hd)

        proj_full = lax.all_gather(
            proj_weight.astype(bf16), ("fsdp", "z", "core"), axis=0, tiled=True
        )
        narrow_full = lax.all_gather(narrow_weight.astype(bf16), "z", axis=0, tiled=True)
        widen_low = widen_weight.astype(bf16).reshape(rows, n_f, n_z, CORES, ub)
        widen_out = widen_low.transpose(1, 3, 0, 2, 4).reshape(n_f * CORES, rows, units)
        widen_mine = lax.all_to_all(widen_out, ("fsdp", "core"), 0, 0)
        widen_in = lax.all_gather(widen_mine.reshape(-1, units), "z", axis=0, tiled=False)
        widen_full = (
            widen_in.reshape(n_z, n_f, CORES, rows, units).transpose(1, 0, 2, 3, 4).reshape(D, units)
        )

        cond_float = condition.astype(f32)
        cond_act = jax.nn.silu(cond_float).astype(bf16).reshape(images_group, n_f, n_s, rows)
        cond_rows = lax.dynamic_index_in_dim(cond_act, at_s, 2, keepdims=False)
        modul_part = matmul(cond_rows.reshape(images_group, n_f * rows), modul_rows)
        modulation = reduce_seq(modul_part) + bias_mod

        own_id = lax.dynamic_index_in_dim(local_ids, at_s, keepdims=False)
        image_pick = (own_id == jnp.arange(images_group, dtype=jnp.int32)).astype(f32)
        if images_group == 1:
            own_row = modulation[0]
            group_rows = modulation
        else:
            own_row = jnp.sum(image_pick[:, None] * modulation, axis=0)
            rel_ids = xor_take(local_ids, at_s)
            rel_pick = (
                rel_ids[:, None] == jnp.arange(images_group, dtype=jnp.int32)[None, :]
            ).astype(f32)
            group_rows = jnp.sum(rel_pick[:, :, None] * modulation[None, :, :], axis=1)
            arrange = jnp.argsort(rel_ids, stable=True)
            restore = jnp.argsort(arrange, stable=True)
        shift_a, scale_a, gate_a, shift_b, scale_b, gate_b = [
            own_row[i * D : (i + 1) * D] for i in range(6)
        ]

        def by_image(values):
            if images_group > 1:
                values = values.reshape(n_s, BLOCK, hd)[arrange]
            values = values.reshape(images_group, SEQ_LEN, heads_dev, HEAD)
            return values.transpose(0, 2, 1, 3)

        def by_block(values):
            values = values.transpose(0, 2, 1, 3).reshape(tok_group, hd)
            if images_group > 1:
                values = values.reshape(n_s, BLOCK, hd)[restore].reshape(tok_group, hd)
            return values

        normed_group, _ = normalize(tokens_group.astype(f32))
        h_a = (
            normed_group * (1.0 + group_rows[:, None, D : 2 * D]) + group_rows[:, None, :D]
        ).astype(bf16)
        h_a = h_a.reshape(tok_group, D)
        query_bias = lax.dynamic_index_in_dim(bias_query, at_s, keepdims=False)
        value_bias = lax.dynamic_index_in_dim(bias_value, at_s, keepdims=False)
        qkv_bias = jnp.concatenate([query_bias, jnp.zeros((hd,), f32), value_bias])
        qkv = (matmul(h_a, qkv_full) + qkv_bias).astype(bf16)
        queries = by_image(qkv[:, :hd])
        keys = by_image(qkv[:, hd : 2 * hd])
        values = by_image(qkv[:, 2 * hd :])
        scores = (
            jnp.einsum("ihqd,ihkd->ihqk", queries, keys, preferred_element_type=f32) * head_scale
        )
        log_total = jax.nn.logsumexp(scores, axis=-1, keepdims=True)
        probs = jnp.exp(scores - log_total)
        probs_low = probs.astype(bf16)
        attended = by_block(
            jnp.einsum("ihqk,ihkd->ihqd", probs_low, values, preferred_element_type=f32).astype(
                bf16
            )
        )
        att_in = swap_rows_seq(attended.reshape(n_z, CORES, BLOCK, hd)).reshape(n_s, BLOCK, hd)
        att_own = xor_take(att_in, at_s).transpose(1, 0, 2).reshape(BLOCK, D)

        branch_a = matmul(att_own, proj_full) + bias_proj
        inputs = tokens.astype(f32)
        middle = inputs + gate_a * branch_a
        normed_b, spread_b = normalize(middle)
        h_b_own = (normed_b * (1.0 + scale_b) + shift_b).astype(bf16)
        grad_out = cotangent.astype(f32)
        d_b_own = (gate_b * grad_out).astype(bf16)

        d_b_f = lax.all_gather(d_b_own, "fsdp", axis=0, tiled=False)
        d_b = jnp.stack([d_b_f, swap_c(d_b_f)], axis=1).reshape(-1, D)
        h_b_f = jnp.stack(xor_parts(all_f(h_b_own), at_f))
        h_b = jnp.stack([h_b_f, swap_c(h_b_f)], axis=1).reshape(-1, D)
        bias_units = lax.dynamic_index_in_dim(bias_widen, at_f, 0, keepdims=False)
        bias_units = lax.dynamic_index_in_dim(bias_units, at_c, 1, keepdims=False).reshape(units)
        widened = matmul(h_b, widen_full) + bias_units
        activated, gelu_pull = jax.vjp(lambda u: jax.nn.gelu(u, approximate=True), widened)
        activated = activated.astype(bf16)
        d_act = jnp.einsum("td,fd->tf", d_b, narrow_full, preferred_element_type=f32)
        d_wide = gelu_pull(d_act)[0].astype(bf16)
        d_hb_part = jnp.einsum("tf,df->td", d_wide, widen_full, preferred_element_type=f32)

        def join_cores(values):
            return values[:, 0] + swap_c(values[:, 1].astype(bf16)).astype(f32)

        d_hb_f = join_cores(d_hb_part.reshape(n_f, CORES, BLOCK, D))
        d_hb_rel = [
            lax.dynamic_index_in_dim(d_hb_f, at_f ^ k, keepdims=False) for k in range(n_f)
        ]
        d_hb = tree_sum(
            [d_hb_rel[0]]
            + [swap_f(d_hb_rel[k].astype(bf16), k).astype(f32) for k in range(1, n_f)]
        )
        branch_part = join_cores(matmul(activated, narrow_full).reshape(n_f, CORES, BLOCK, D))
        branch_b = (
            lax.psum_scatter(branch_part, "fsdp", scatter_dimension=0, tiled=False) + bias_narrow
        )
        block_output = (middle + gate_b * branch_b).astype(bf16)
        d_gate_b = jnp.sum(grad_out * branch_b, axis=0)
        grad_narrow = jnp.einsum("tf,td->fd", activated, d_b, preferred_element_type=f32)
        narrow_sum = lax.psum_scatter(grad_narrow, "z", scatter_dimension=0, tiled=True)
        grad_widen = jnp.einsum("td,tf->df", h_b, d_wide, preferred_element_type=f32)
        grad_widen = grad_widen.reshape(n_f, n_z, CORES * rows, units).transpose(1, 0, 2, 3)
        widen_mid = lax.psum_scatter(
            grad_widen.reshape(n_z, -1, units), "z", scatter_dimension=0, tiled=False
        )
        widen_back = lax.all_to_all(
            widen_mid.astype(bf16).reshape(n_f * CORES, rows, units), ("fsdp", "core"), 0, 0
        )
        widen_sum = widen_back.reshape(n_f, CORES, rows, n_z, ub).transpose(2, 0, 3, 1, 4)
        widen_sum = widen_sum.reshape(rows, FF).astype(f32)

        d_shift_b = jnp.sum(d_hb, axis=0)
        d_scale_b = jnp.sum(d_hb * normed_b, axis=0)
        d_middle = grad_out + norm_back(d_hb * (1.0 + scale_b), normed_b, spread_b)
        d_gate_a = jnp.sum(d_middle * branch_a, axis=0)
        d_a = (gate_a * d_middle).astype(bf16)
        d_att_own = jnp.einsum("te,de->td", d_a, proj_full, preferred_element_type=f32)
        d_att_own = d_att_own.astype(bf16).reshape(BLOCK, n_s, hd).transpose(1, 0, 2)
        d_att_out = xor_take(d_att_own, at_s).reshape(n_z, CORES, BLOCK, hd)
        d_att = by_image(swap_rows_seq(d_att_out).reshape(tok_group, hd))
        grad_proj = jnp.einsum("td,te->de", att_own, d_a, preferred_element_type=f32)
        proj_own, proj_other = own_other(grad_proj.reshape(n_f * n_z, CORES, rows, D), 1)
        proj_both = proj_own + swap_c(proj_other.astype(bf16)).astype(f32)
        proj_sum = lax.psum_scatter(
            proj_both.reshape(-1, D), ("fsdp", "z"), scatter_dimension=0, tiled=True
        )

        d_values = jnp.einsum("ihqk,ihqd->ihkd", probs_low, d_att, preferred_element_type=f32)
        d_probs = jnp.einsum("ihqd,ihkd->ihqk", d_att, values, preferred_element_type=f32)
        row_term = jnp.sum(probs * d_probs, axis=-1, keepdims=True)
        d_scores = (probs * (d_probs - row_term)).astype(bf16)
        d_queries = (
            jnp.einsum("ihqk,ihkd->ihqd", d_scores, keys, preferred_element_type=f32) * head_scale
        )
        d_keys = (
            jnp.einsum("ihqk,ihqd->ihkd", d_scores, queries, preferred_element_type=f32)
            * head_scale
        )
        d_qkv = jnp.concatenate(
            [by_block(part.astype(bf16)) for part in (d_queries, d_keys, d_values)], axis=1
        )
        d_ha_part = jnp.einsum("te,de->td", d_qkv, qkv_full, preferred_element_type=f32)
        d_ha_z = join_cores(d_ha_part.reshape(n_z, CORES, BLOCK, D))
        d_ha = tree_sum(
            [d_ha_z[0]] + [swap_z(d_ha_z[k].astype(bf16), k).astype(f32) for k in range(1, n_z)]
        )
        grad_qkv = jnp.einsum("td,te->de", h_a, d_qkv, preferred_element_type=f32)
        grad_qkv = xor_take(grad_qkv.reshape(n_g, rows, 3 * hd), at_g)
        grad_qkv = grad_qkv.reshape(n_f, n_s, rows, 3 * hd)
        qkv_mid = tree_sum(
            [grad_qkv[0]]
            + [swap_f(grad_qkv[k].astype(bf16), k).astype(f32) for k in range(1, n_f)]
        )
        qkv_back = swap_rows_seq(qkv_mid.reshape(n_z, CORES, rows, 3 * hd))
        qkv_sum = xor_take(qkv_back.reshape(n_s, rows, 3, hd), at_s)
        qkv_sum = qkv_sum.transpose(1, 2, 0, 3).reshape(rows, 3 * D)
        normed_a, spread_a = normalize(inputs)
        d_shift_a = jnp.sum(d_ha, axis=0)
        d_scale_a = jnp.sum(d_ha * normed_a, axis=0)
        tokens_grad = (
            d_middle + norm_back(d_ha * (1.0 + scale_a), normed_a, spread_a)
        ).astype(bf16)

        pick_f = (jnp.arange(n_f) == at_f).astype(f32)
        pick_c = (jnp.arange(CORES) == at_c).astype(f32)
        pick_s = (jnp.arange(n_s) == at_s).astype(f32)
        units_sum = column_sums(d_wide).reshape(n_z, ub)
        bias_g_widen = (
            pick_f[:, None, None, None] * pick_c[None, None, :, None] * units_sum[None, :, None, :]
        ).reshape(FF)
        heads_sum = column_sums(d_qkv)
        bias_g_query = (pick_s[:, None] * heads_sum[None, :hd]).reshape(D)
        bias_g_value = (pick_s[:, None] * heads_sum[None, 2 * hd :]).reshape(D)
        d_block = jnp.concatenate([d_shift_a, d_scale_a, d_gate_a, d_shift_b, d_scale_b, d_gate_b])
        per_image = (image_pick[:, None] * d_block[None, :]).reshape(-1)
        sums = reduce_seq(
            jnp.concatenate(
                [
                    per_image,
                    bias_g_query,
                    bias_g_value,
                    column_sums(d_a),
                    bias_g_widen,
                    column_sums(d_b_own),
                ]
            )
        )
        split = images_group * 6 * D
        whole = jnp.stack(xor_parts(all_f(sums), at_f))
        d_modulation = whole[:, :split].reshape(n_f * images_group, 6 * D)
        all_act = jax.nn.silu(cond_all).astype(bf16).astype(f32)
        act_cols = lax.dynamic_slice_in_dim(all_act, at_g * rows, rows, axis=1)
        modul_sum = sum(
            act_cols[i][:, None] * d_modulation[i][None, :] for i in range(n_f * images_group)
        )
        bias_grad = jnp.concatenate(
            [jnp.sum(d_modulation, axis=0), jnp.sum(whole[:, split:], axis=0)]
        )
        bias_sum = lax.dynamic_slice_in_dim(bias_grad, at_g * width, width)
        d_own = sums[:split].reshape(images_group, 6 * D)
        d_cond_rows = jnp.einsum(
            "im,dm->id",
            d_own,
            modul_rows.astype(f32),
            precision=lax.Precision.HIGHEST,
            preferred_element_type=f32,
        )
        d_cond_z = jnp.stack(all_z(d_cond_rows))
        d_cond = jnp.stack([d_cond_z, swap_c(d_cond_z)], axis=1)
        d_cond = xor_take(d_cond.reshape(n_s, images_group, n_f, rows), at_s)
        d_cond_act = d_cond.transpose(1, 2, 0, 3).reshape(images_group, D)
        silu_pull = jax.vjp(jax.nn.silu, cond_float)[1]
        condition_grad = silu_pull(d_cond_act)[0]

        rate_wide = 2.0 / math.sqrt(D)
        modul_new = adam_step(modul_weight, modul_sum, modul_mean, modul_square, rate_wide)
        qkv_new = adam_step(qkv_weight, qkv_sum, qkv_mean, qkv_square, rate_wide)
        proj_new = adam_step(
            proj_weight, proj_sum, proj_mean, proj_square, 2.0 / math.sqrt(D // 16)
        )
        widen_new = adam_step(widen_weight, widen_sum, widen_mean, widen_square, rate_wide)
        narrow_new = adam_step(
            narrow_weight, narrow_sum, narrow_mean, narrow_square, 2.0 / math.sqrt(FF)
        )
        bias_new = adam_step(bias_vector, bias_sum, bias_mean, bias_square, 0.5)
        news = (modul_new, qkv_new, proj_new, widen_new, narrow_new, bias_new)
        return (
            block_output,
            tokens_grad,
            condition_grad,
            *[new[0] for new in news],
            *[new[1] for new in news],
            *[new[2] for new in news],
        )

    return shards


def solution(mesh):
    n_f, n_s = mesh.shape["fsdp"], mesh.shape["seq"]
    n_z = n_s // CORES
    cores = jax.sharding.Mesh(mesh.devices.reshape(n_f, n_z, CORES), ("fsdp", "z", "core"))
    both = P(("fsdp", "z", "core"), None)
    flat = P(("fsdp", "z", "core"))
    params = (both, both, both, both, both, flat)
    return jax.shard_map(
        make_shards(n_f, n_z),
        mesh=cores,
        in_specs=(both, P("fsdp", None), P("fsdp"), both) + params * 3,
        out_specs=(both, both, P("fsdp", None)) + params * 3,
        check_vma=False,
    )
```

time: 1570 us -> 534 us (0.34)
  waiting for transfers between devices: 1230 us -> 224 us
  starting transfers between devices: 1.14 us -> 68.5 us
  matrix products: 104 us -> 52.3 us
  blocking collectives: 94.3 us -> 43 us
    reduce_scatter x6 -> x3, waiting for transfers between devices: 896 us -> 99.6 us  [the longest x1 56.2 us: shards(): lax.psum_scatter(proj_both.reshape(-1, D), ('fsdp', 'z'), scatter_dimensi...]
    all_gather x6 -> x5, waiting for transfers between devices: 337 us -> 25.6 us  [the longest x1 23.2 us: shards(): lax.all_gather(narrow_weight.astype(bf16), 'z', axis=0, tiled=True)]
    unnamed x2 -> x0, blocking collectives: 80.6 us -> none
    ppermute x0 -> x56, waiting for transfers between devices: none -> 76.5 us  [swap(): return lax.ppermute(values, axis, [(i, i ^ k) for i in range(size)])]
    ppermute x0 -> x56, starting transfers between devices: none -> 59.7 us  [swap(): return lax.ppermute(values, axis, [(i, i ^ k) for i in range(size)])]
    dot_general x20, matrix products: 104 us -> 52.3 us  [the longest x5 10.8 us: matmul(): return jnp.dot(left, right, preferred_element_type=f32)]
    all_gather x0 -> x1, blocking collectives: none -> 43 us  [shards(): small = lax.all_gather(small, ('fsdp', 'z', 'core'), axis=0, tiled=False)]
    scatter-add x1 -> x0, other arithmetic: 17.4 us -> none  [shards(): jnp.zeros((group_blocks, BLOCK, 2 * D), jnp.float32).at[key_blocks]]
  transfers between devices with their start and end apart: 12 -> 67, of which waited for: 12 -> 32; matrix products, arithmetic and copies ran while one was open for 7% -> 23% of each run, Pallas kernels for 0% -> 0%
where the time goes in v1:
time: 534 us; the launch traced here: 526 us
  waiting for transfers between devices  224 us (42%)
  other arithmetic  73.8 us (14%)
  starting transfers between devices  68.5 us (13%)
  matrix products  52.3 us (10%)
  local copies, waits for them, and re-layouts  47.7 us (9%)
  blocking collectives  43 us (8%)
  between operations  16.4 us (3%)
    ppermute x56, waiting for transfers between devices, swap(): return lax.ppermute(values, axis, [(i, i ^ k) for i in range(size)])  76.5 us
    ppermute x56, starting transfers between devices, swap(): return lax.ppermute(values, axis, [(i, i ^ k) for i in range(size)])  59.7 us
    reduce_scatter x1, waiting for transfers between devices, shards(): lax.psum_scatter(proj_both.reshape(-1, D), ('fsdp', 'z'), scatter_dimensi...  56.2 us
    reduce_scatter x1, waiting for transfers between devices, shards(): lax.psum_scatter(grad_narrow, 'z', scatter_dimension=0, tiled=True)  43.5 us
    all_gather x1, blocking collectives, shards(): small = lax.all_gather(small, ('fsdp', 'z', 'core'), axis=0, tiled=False)  43 us
    all_gather x1, waiting for transfers between devices, shards(): lax.all_gather(narrow_weight.astype(bf16), 'z', axis=0, tiled=True)  23.2 us
    unnamed x10, waiting for transfers between devices  14.3 us
    sub x6, other arithmetic, adam_step(): weight - rate * (first / fix_first / (jnp.sqrt(second / fix_second) + ada...  12.7 us
  transfers between devices with their start and end apart: 67, of which 32 were waited for; matrix products, arithmetic and copies ran while one was open for 23% of the time, Pallas kernels for 0%

profile of v1, /device:TPU:0, one launch (start us, length us, event | category | flops | bytes accessed | tf_op | source)
XLA Modules:
  0.0 526.1 jit_solution(3741964116385981806)
XLA Ops:
  9.2 3.1 collective-permute-start.4
  19.3 4.0 all-to-all-start
  24.8 43.0 %all-gather = bf16[512,128]{1,0:T(8,128)(2,1)S(1)} all-gather(bf16[16,128]{1,0:T(8,128)(2,1)S(1)} %pad_maximum_fusion.20), channel_id=2, replica_groups=mesh['fsdp'=4,'z'=4,'core'=2] {'fsdp','z','core'}, dimensions={0}, use_global_device_ids=true | all-gather | bytes 135168 | tf_op jit(solution)/shard_map/all_gather | solution.py:165
  82.2 4.8 collective-permute-done.14
  107.4 4.6 multiply_reduce_fusion.1
  113.8 4.9 exponential_reduce_fusion
  139.7 3.4 fusion.127
  147.7 6.1 %collective-permute-done.21 = bf16[128,1024]{1,0:T(8,128)(2,1)} collective-permute-done((bf16[128,1024]{1,0:T(8,128)(2,1)}, bf16[128,1024]{1,0:T(8,128)(2,1)}, u32[]{:S(2)}, u32[]{:S(2)}) %collective-permute-start.21) | collective-permute-done | bytes 262176 | tf_op jit(solution)/shard_map/ppermute | solution.py:92
  153.8 4.9 collective-permute-done.19
  179.0 43.5 %reduce-scatter.11.cloned.1.call-done = f32[128,1024]{1,0:T(8,128)} async-done(((f32[512,1024]{1,0:T(8,128)}), f32[128,1024]{1,0:T(8,128)}) %reduce-scatter.11.cloned.1.call-update) | async-done | bytes 524304 | tf_op jit(solution)/shard_map/reduce_scatter | solution.py:301
  222.5 3.3 multiply_subtract_fusion.1
  226.1 3.9 copy.339
  230.1 23.2 %all-gather.14.cloned.1.call-done = bf16[512,1024]{1,0:T(8,128)(2,1)} async-done(((bf16[128,1024]{1,0:T(8,128)(2,1)}), bf16[512,1024]{1,0:T(8,128)(2,1)}) %all-gather.14.cloned.1.call-update) | async-done | bytes 1048592 | tf_op jit(solution)/shard_map/all_gather | solution.py:191
  253.3 5.8 %convert_reduce_fusion.1 = (f32[512]{0:T(512)}, bf16[1024,512]{1,0:T(8,128)(2,1)S(1)}) fusion(f32[1024,512]{1,0:T(8,128)} %copy-done.81, f32[512]{0:T(512)} %bitcast.558, bf16[1024,1024]{1,0:T(8,128)(2,1)} %bitcast.468, bf16[512,1024]{1,0:T(8,128)(2,1)} %all-gather.14.cloned.1.call-done), kind=kOutput, calls=%fused_computation.46 | convolution fusion | flops 1085799936 | bytes 6295552 | tf_op jit(solution)/shard_map/td,fd->tf/dot_general | solution.py:279
  261.9 3.4 fusion.111
  271.4 3.6 fusion.14
  288.0 3.9 copy.331
  299.1 4.4 collective-permute-done.26
  303.5 6.1 %collective-permute-done.28 = bf16[128,1024]{1,0:T(8,128)(2,1)S(1)} collective-permute-done((bf16[128,1024]{1,0:T(8,128)(2,1)S(1)}, bf16[128,1024]{1,0:T(8,128)(2,1)S(1)}, u32[]{:S(2)}, u32[]{:S(2)}) %collective-permute-start.28) | collective-permute-done | bytes 262176 | tf_op jit(solution)/shard_map/ppermute | solution.py:92
  314.4 3.4 all-to-all-start.1
  319.4 8.5 %all-to-all-done.1 = bf16[8,32,512]{2,1,0:T(8,128)(2,1)S(1)} async-done(((bf16[8,32,512]{2,1,0:T(8,128)(2,1)}), bf16[8,32,512]{2,1,0:T(8,128)(2,1)S(1)}, u32[]{:S(2)}, u32[]{:S(2)}) %all-to-all-start.1) | async-done | bytes 262176 | tf_op jit(solution)/shard_map/all_to_all | solution.py:307
  331.6 14.1 %reduce-scatter.13.cloned.1.call-done = f32[1,128,1024]{2,1,0:T(8,128)} async-done(((f32[4,128,1024]{2,1,0:T(8,128)}), f32[1,128,1024]{2,1,0:T(8,128)}) %reduce-scatter.13.cloned.1.call-update) | async-done | bytes 524304
  345.7 3.1 fusion.48
  364.3 5.1 convolution_convert_fusion.1
  369.4 5.2 multiply_reduce_fusion
  385.5 4.0 fusion.29
  405.7 7.5 %collective-permute-done.36 = bf16[128,1024]{1,0:T(8,128)(2,1)S(1)} collective-permute-done((bf16[128,1024]{1,0:T(8,128)(2,1)S(1)}, bf16[128,1024]{1,0:T(8,128)(2,1)S(1)}, u32[]{:S(2)}, u32[]{:S(2)}) %collective-permute-start.36) | collective-permute-done | bytes 262176 | tf_op jit(solution)/shard_map/ppermute | solution.py:92
  413.2 10.0 %collective-permute-done.35 = bf16[128,1024]{1,0:T(8,128)(2,1)S(1)} collective-permute-done((bf16[128,1024]{1,0:T(8,128)(2,1)S(1)}, bf16[128,1024]{1,0:T(8,128)(2,1)S(1)}, u32[]{:S(2)}, u32[]{:S(2)}) %collective-permute-start.35) | collective-permute-done | bytes 262176 | tf_op jit(solution)/shard_map/ppermute | solution.py:92
  432.4 3.1 fusion.16
  435.5 4.1 collective-permute-start.53
  454.9 3.4 collective-permute-done.46
  461.5 56.2 %reduce-scatter.7.cloned.1.call-done = f32[32,1024]{1,0:T(8,128)} async-done(((f32[512,1024]{1,0:T(8,128)}), f32[32,1024]{1,0:T(8,128)}) %reduce-scatter.7.cloned.1.call-update) | async-done | bytes 131088 | tf_op jit(solution)/shard_map/reduce_scatter | solution.py:325
  (483 shorter events, 202.1 us)
Async XLA Ops:
  7.2 86.5 %all-gather.8.cloned.1.call-start = ((), (), s32[]{:S(2)}) async-start(), calls=%async_computation.6 | async-start | bytes 1966080 | tf_op jit(solution)/shard_map/all_gather | solution.py:177
  9.2 58.7 %collective-permute-start.4 = (bf16[128,1024]{1,0:T(8,128)(2,1)}, bf16[128,1024]{1,0:T(8,128)(2,1)S(1)}, u32[]{:S(2)}, u32[]{:S(2)}) collective-permute-start(bf16[128,1024]{1,0:T(8,128)(2,1)} %param.22), channel_id=1, source_target_pairs={{0,2},{2,0},{4,6},{6,4},{1,3},{3,1},{5,7},{7,5},{8,10},{10,8},{12,... | collective-permute-start | bytes 786440 | tf_op jit(solution)/shard_map/ppermute | solution.py:92
  12.3 55.6 %collective-permute-start.6 = (bf16[128,1024]{1,0:T(8,128)(2,1)}, bf16[128,1024]{1,0:T(8,128)(2,1)S(1)}, u32[]{:S(2)}, u32[]{:S(2)}) collective-permute-start(bf16[128,1024]{1,0:T(8,128)(2,1)} %param.22), channel_id=1, source_target_pairs={{0,6},{2,4},{4,2},{6,0},{1,7},{3,5},{5,3},{7,1},{8,14},{10,12},{12... | collective-permute-start | bytes 786440 | tf_op jit(solution)/shard_map/ppermute | solution.py:92
  14.7 53.1 %collective-permute-start.5 = (bf16[128,1024]{1,0:T(8,128)(2,1)}, bf16[128,1024]{1,0:T(8,128)(2,1)S(1)}, u32[]{:S(2)}, u32[]{:S(2)}) collective-permute-start(bf16[128,1024]{1,0:T(8,128)(2,1)} %param.22), channel_id=1, source_target_pairs={{0,4},{2,6},{4,0},{6,2},{1,5},{3,7},{5,1},{7,3},{8,12},{10,14},{12... | collective-permute-start | bytes 786440 | tf_op jit(solution)/shard_map/ppermute | solution.py:92
  18.2 51.9 %collective-permute-start.8 = (bf16[4,32,384]{2,1,0:T(8,128)(2,1)}, bf16[4,32,384]{2,1,0:T(8,128)(2,1)S(1)}, u32[]{:S(2)}, u32[]{:S(2)}) collective-permute-start(bf16[4,32,384]{2,1,0:T(8,128)(2,1)} %get-tuple-element.119), channel_id=1, source_target_pairs={{0,1},{1,0},{2,3},{3,2},{4,5},{5,4},{6,7},{7,6},{8,9},{9,8},{10,11... | collective-permute-start | bytes 294920 | tf_op jit(solution)/shard_map/ppermute | solution.py:92
  19.3 112.0 %all-to-all-start = ((bf16[8,32,512]{2,1,0:T(8,128)(2,1)}), bf16[8,32,512]{2,1,0:T(8,128)(2,1)}, u32[]{:S(2)}, u32[]{:S(2)}) async-start(bf16[8,32,512]{2,1,0:T(8,128)(2,1)} %reshape.623), calls=%async_computation | async-start | bytes 524288 | tf_op jit(solution)/shard_map/all_to_all | solution.py:194
  23.4 116.4 %all-gather.10.cloned.1.call-start = ((), (), s32[]{:S(2)}) async-start(), calls=%async_computation.7 | async-start | bytes 2162688 | tf_op jit(solution)/shard_map/all_gather | solution.py:188
  24.1 123.6 %all-gather.16.cloned.1.call-start = ((), (), s32[]{:S(2)}) async-start(), calls=%async_computation.13 | async-start | bytes 1310720 | tf_op jit(solution)/shard_map/all_gather | solution.py:270
  69.0 24.2 %collective-permute-start.7 = (bf16[4,128,1024]{2,1,0:T(8,128)(2,1)}, bf16[4,128,1024]{2,1,0:T(8,128)(2,1)S(1)}, u32[]{:S(2)}, u32[]{:S(2)}) collective-permute-start(bf16[4,128,1024]{2,1,0:T(8,128)(2,1)} %get-tuple-element.76), channel_id=1, source_target_pairs={{0,1},{1,0},{2,3},{3,2},{4,5},{5,4},{6,7},{7,6},{8,9},{9,8},{10,11... | collective-permute-start | bytes 3145736 | tf_op jit(solution)/shard_map/ppermute | solution.py:92
  113.5 54.4 %all-gather.12.cloned.1.call-start = ((), (), s32[]{:S(2)}) async-start(), calls=%async_computation.8 | async-start | bytes 1310720 | tf_op jit(solution)/shard_map/all_gather | solution.py:195
  131.4 91.1 %reduce-scatter.11.cloned.1.call-start = ((), (), s32[]{:S(2)}) async-start(), calls=%async_computation.12 | async-start | bytes 2621440 | tf_op jit(solution)/shard_map/reduce_scatter | solution.py:301
  145.7 12.9 %collective-permute-start.19 = (bf16[128,1024]{1,0:T(8,128)(2,1)}, bf16[128,1024]{1,0:T(8,128)(2,1)}, u32[]{:S(2)}, u32[]{:S(2)}) collective-permute-start(bf16[128,1024]{1,0:T(8,128)(2,1)} %add_convert_fusion.3), channel_id=1, source_target_pairs={{0,24},{8,16},{16,8},{24,0},{1,25},{9,17},{17,9},{25,1},{2,26},{10... | collective-permute-start | bytes 786440 | tf_op jit(solution)/shard_map/ppermute | solution.py:92
  147.7 21.7 %collective-permute-start.24 = (bf16[4,128,1024]{2,1,0:T(8,128)(2,1)}, bf16[4,128,1024]{2,1,0:T(8,128)(2,1)}, u32[]{:S(2)}, u32[]{:S(2)}) collective-permute-start(bf16[4,128,1024]{2,1,0:T(8,128)(2,1)} %bitcast.481), channel_id=1, source_target_pairs={{0,1},{1,0},{2,3},{3,2},{4,5},{5,4},{6,7},{7,6},{8,9},{9,8},{10,11... | collective-permute-start | bytes 3145736 | tf_op jit(solution)/shard_map/ppermute | solution.py:92
  161.5 9.7 %collective-permute-start.22 = (bf16[4,128,1024]{2,1,0:T(8,128)(2,1)}, bf16[4,128,1024]{2,1,0:T(8,128)(2,1)}, u32[]{:S(2)}, u32[]{:S(2)}) collective-permute-start(bf16[4,128,1024]{2,1,0:T(8,128)(2,1)} %get-tuple-element.70), channel_id=1, source_target_pairs={{0,1},{1,0},{2,3},{3,2},{4,5},{5,4},{6,7},{7,6},{8,9},{9,8},{10,11... | collective-permute-start | bytes 3145736 | tf_op jit(solution)/shard_map/ppermute | solution.py:92
  179.0 74.3 %all-gather.14.cloned.1.call-start = ((), (), s32[]{:S(2)}) async-start(), calls=%async_computation.9 | async-start | bytes 1310720 | tf_op jit(solution)/shard_map/all_gather | solution.py:191
  225.8 86.8 %reduce-scatter.9.cloned.1.call-start = ((), (), s32[]{:S(2)}) async-start(), calls=%async_computation.11 | async-start | bytes 2621440 | tf_op jit(solution)/shard_map/reduce_scatter | solution.py:304
  261.8 83.9 %reduce-scatter.13.cloned.1.call-start = ((), (), s32[]{:S(2)}) async-start(), calls=%async_computation.14 | async-start | bytes 2621440
  295.8 13.7 %collective-permute-start.28 = (bf16[128,1024]{1,0:T(8,128)(2,1)S(1)}, bf16[128,1024]{1,0:T(8,128)(2,1)S(1)}, u32[]{:S(2)}, u32[]{:S(2)}) collective-permute-start(bf16[128,1024]{1,0:T(8,128)(2,1)S(1)} %get-tuple-element.64), channel_id=1, source_target_pairs={{0,24},{8,16},{16,8},{24,0},{1,25},{9,17},{17,9},{25,1},{2,26},{10... | collective-permute-start | bytes 786440 | tf_op jit(solution)/shard_map/ppermute | solution.py:92
  297.3 13.6 %collective-permute-start.27 = (bf16[128,1024]{1,0:T(8,128)(2,1)S(1)}, bf16[128,1024]{1,0:T(8,128)(2,1)S(1)}, u32[]{:S(2)}, u32[]{:S(2)}) collective-permute-start(bf16[128,1024]{1,0:T(8,128)(2,1)S(1)} %get-tuple-element.65), channel_id=1, source_target_pairs={{0,16},{8,24},{16,0},{24,8},{1,17},{9,25},{17,1},{25,9},{2,18},{10... | collective-permute-start | bytes 786440 | tf_op jit(solution)/shard_map/ppermute | solution.py:92
  314.4 13.4 %all-to-all-start.1 = ((bf16[8,32,512]{2,1,0:T(8,128)(2,1)}), bf16[8,32,512]{2,1,0:T(8,128)(2,1)S(1)}, u32[]{:S(2)}, u32[]{:S(2)}) async-start(bf16[8,32,512]{2,1,0:T(8,128)(2,1)} %bitcast.188), calls=%async_computation.3 | async-start | bytes 524288 | tf_op jit(solution)/shard_map/all_to_all | solution.py:307
  317.8 199.9 %reduce-scatter.7.cloned.1.call-start = ((), (), s32[]{:S(2)}) async-start(), calls=%async_computation.10 | async-start | bytes 2228224 | tf_op jit(solution)/shard_map/reduce_scatter | solution.py:325
  383.3 12.3 %collective-permute-start.33 = (bf16[4,128,1024]{2,1,0:T(8,128)(2,1)}, bf16[4,128,1024]{2,1,0:T(8,128)(2,1)}, u32[]{:S(2)}, u32[]{:S(2)}) collective-permute-start(bf16[4,128,1024]{2,1,0:T(8,128)(2,1)} %fusion.24), channel_id=1, source_target_pairs={{0,1},{1,0},{2,3},{3,2},{4,5},{5,4},{6,7},{7,6},{8,9},{9,8},{10,11... | collective-permute-start | bytes 3145736 | tf_op jit(solution)/shard_map/ppermute | solution.py:92
  384.6 45.8 %collective-permute-start.55 = (bf16[16,32,1024]{2,1,0:T(8,128)(2,1)}, bf16[16,32,1024]{2,1,0:T(8,128)(2,1)}, u32[]{:S(2)}, u32[]{:S(2)}) collective-permute-start(bf16[16,32,1024]{2,1,0:T(8,128)(2,1)} %fusion.21), channel_id=1, source_target_pairs={{0,1},{1,0},{2,3},{3,2},{4,5},{5,4},{6,7},{7,6},{8,9},{9,8},{10,11... | collective-permute-start | bytes 3145736 | tf_op jit(solution)/shard_map/ppermute | solution.py:92
  393.4 10.7 %collective-permute-start.50 = (bf16[8,32,384]{2,1,0:T(8,128)(2,1)S(1)}, bf16[8,32,384]{2,1,0:T(8,128)(2,1)S(1)}, u32[]{:S(2)}, u32[]{:S(2)}) collective-permute-start(bf16[8,32,384]{2,1,0:T(8,128)(2,1)S(1)} %get-tuple-element.78), channel_id=1, source_target_pairs={{0,24},{8,16},{16,8},{24,0},{1,25},{9,17},{17,9},{25,1},{2,26},{10... | collective-permute-start | bytes 589832 | tf_op jit(solution)/shard_map/ppermute | solution.py:92
  394.9 10.6 %collective-permute-start.49 = (bf16[8,32,384]{2,1,0:T(8,128)(2,1)S(1)}, bf16[8,32,384]{2,1,0:T(8,128)(2,1)S(1)}, u32[]{:S(2)}, u32[]{:S(2)}) collective-permute-start(bf16[8,32,384]{2,1,0:T(8,128)(2,1)S(1)} %get-tuple-element.79), channel_id=1, source_target_pairs={{0,16},{8,24},{16,0},{24,8},{1,17},{9,25},{17,1},{25,9},{2,18},{10... | collective-permute-start | bytes 589832 | tf_op jit(solution)/shard_map/ppermute | solution.py:92
  399.7 13.5 %collective-permute-start.36 = (bf16[128,1024]{1,0:T(8,128)(2,1)S(1)}, bf16[128,1024]{1,0:T(8,128)(2,1)S(1)}, u32[]{:S(2)}, u32[]{:S(2)}) collective-permute-start(bf16[128,1024]{1,0:T(8,128)(2,1)S(1)} %get-tuple-element.67), channel_id=1, source_target_pairs={{0,6},{2,4},{4,2},{6,0},{1,7},{3,5},{5,3},{7,1},{8,14},{10,12},{12... | collective-permute-start | bytes 786440 | tf_op jit(solution)/shard_map/ppermute | solution.py:92
  404.1 19.1 %collective-permute-start.35 = (bf16[128,1024]{1,0:T(8,128)(2,1)S(1)}, bf16[128,1024]{1,0:T(8,128)(2,1)S(1)}, u32[]{:S(2)}, u32[]{:S(2)}) collective-permute-start(bf16[128,1024]{1,0:T(8,128)(2,1)S(1)} %get-tuple-element.68), channel_id=1, source_target_pairs={{0,4},{2,6},{4,0},{6,2},{1,5},{3,7},{5,1},{7,3},{8,12},{10,14},{12... | collective-permute-start | bytes 786440 | tf_op jit(solution)/shard_map/ppermute | solution.py:92
  405.6 19.5 %collective-permute-start.51 = (f32[4,32,384]{2,1,0:T(8,128)S(1)}, f32[4,32,384]{2,1,0:T(8,128)S(1)}, u32[]{:S(2)}, u32[]{:S(2)}) collective-permute-start(f32[4,32,384]{2,1,0:T(8,128)S(1)} %get-tuple-element.96), channel_id=1, source_target_pairs={{0,1},{1,0},{2,3},{3,2},{4,5},{5,4},{6,7},{7,6},{8,9},{9,8},{10,11... | collective-permute-start | bytes 589832 | tf_op jit(solution)/shard_map/ppermute | solution.py:92
  425.1 18.0 %collective-permute-start.52 = (f32[2,32,384]{2,1,0:T(8,128)S(1)}, f32[2,32,384]{2,1,0:T(8,128)S(1)}, u32[]{:S(2)}, u32[]{:S(2)}) collective-permute-start(f32[2,32,384]{2,1,0:T(8,128)S(1)} %get-tuple-element.92), channel_id=1, source_target_pairs={{0,2},{2,0},{4,6},{6,4},{1,3},{3,1},{5,7},{7,5},{8,10},{10,8},{12,... | collective-permute-start | bytes 294920 | tf_op jit(solution)/shard_map/ppermute | solution.py:92
  425.2 20.3 %collective-permute-start.54 = (f32[2,32,384]{2,1,0:T(8,128)S(1)}, f32[2,32,384]{2,1,0:T(8,128)S(1)}, u32[]{:S(2)}, u32[]{:S(2)}) collective-permute-start(f32[2,32,384]{2,1,0:T(8,128)S(1)} %get-tuple-element.93), channel_id=1, source_target_pairs={{0,6},{2,4},{4,2},{6,0},{1,7},{3,5},{5,3},{7,1},{8,14},{10,12},{12... | collective-permute-start | bytes 294920 | tf_op jit(solution)/shard_map/ppermute | solution.py:92
  429.1 10.5 %collective-permute-start.39 = (f32[14336]{0:T(1024)S(1)}, f32[14336]{0:T(1024)S(1)}, u32[]{:S(2)}, u32[]{:S(2)}) collective-permute-start(f32[14336]{0:T(1024)S(1)} %add.422), channel_id=1, source_target_pairs={{0,4},{2,6},{4,0},{6,2},{1,5},{3,7},{5,1},{7,3},{8,12},{10,14},{12... | collective-permute-start | bytes 172040 | tf_op jit(solution)/shard_map/ppermute | solution.py:92
  435.5 9.9 %collective-permute-start.53 = (f32[2,32,384]{2,1,0:T(8,128)S(1)}, f32[2,32,384]{2,1,0:T(8,128)S(1)}, u32[]{:S(2)}, u32[]{:S(2)}) collective-permute-start(f32[2,32,384]{2,1,0:T(8,128)S(1)} %get-tuple-element.94), channel_id=1, source_target_pairs={{0,4},{2,6},{4,0},{6,2},{1,5},{3,7},{5,1},{7,3},{8,12},{10,14},{12... | collective-permute-start | bytes 294920 | tf_op jit(solution)/shard_map/ppermute | solution.py:92
  (120 other events, 942.9 us)
Sparse Core Ops, SparseCore 0:
  10.4 36.6 all-gather.7
  50.7 57.5 all-gather.9
  113.6 24.8 all-gather.15
  140.0 27.9 all-gather.11
  179.1 43.3 reduce-scatter.10
  226.0 27.2 all-gather.13
  261.9 43.3 reduce-scatter.8
  308.3 37.3 reduce-scatter.12
  435.6 82.0 reduce-scatter.6

commit v2 on v1

--- a/solution.py
+++ b/solution.py
@@ -106,13 +106,51 @@
     def all_f(values):
         return [swap_f(values, k) for k in range(n_f)]
 
-    def swap_rows_seq(values):
-        both = jnp.stack([values[:, 0], swap_c(values[:, 1])], axis=1)
-        return jnp.stack([swap_z(both[k], k) for k in range(n_z)])
+    def double(values, swap_with, size):
+        values = values[None]
+        step = 1
+        while step < size:
+            values = jnp.concatenate([values, swap_with(values, step)])
+            step *= 2
+        return values
+
+    def shift(entries, swap_with):
+        entries = list(entries)
+        step = 1
+        while step < len(entries):
+            moved = [k for k in range(len(entries)) if k & step]
+            came = swap_with(jnp.stack([entries[k] for k in moved]), step)
+            for i, k in enumerate(moved):
+                entries[k] = came[i]
+            step *= 2
+        return entries
+
+    def halve(parts, swap_with):
+        parts = list(parts)
+        step = len(parts) // 2
+        while step > 0:
+            low = jnp.stack([parts[k + step] for k in range(step)]).astype(bf16)
+            came = swap_with(low, step)
+            parts = [parts[k] + came[k].astype(f32) for k in range(step)]
+            step //= 2
+        return parts[0]
 
     def reduce_seq(values):
         values = values + swap_c(values)
-        return tree_sum(all_z(values))
+        step = 1
+        while step < n_z:
+            values = values + swap_z(values, step)
+            step *= 2
+        return values
+
+    def after(value, *others):
+        return lax.optimization_barrier((value,) + others)[0]
+
+    def join_cores(values):
+        return values[:, 0] + swap_c(values[:, 1].astype(bf16)).astype(f32)
+
+    def add_parts(own, parts):
+        return tree_sum([own] + [part.astype(f32) for part in parts])
 
     def shards(
         tokens,
@@ -149,59 +187,86 @@
         first_core = at_c == 0
         local_ids = block_image - at_f * images_group
 
-        def own_other(values, axis):
-            zero = lax.index_in_dim(values, 0, axis, keepdims=False)
-            one = lax.index_in_dim(values, 1, axis, keepdims=False)
+        pick_f = (jnp.arange(n_f) == at_f).astype(f32)
+        pick_c = (jnp.arange(CORES) == at_c).astype(f32)
+        pick_s = (jnp.arange(n_s) == at_s).astype(f32)
+
+        def by_core(zero, one):
             return jnp.where(first_core, zero, one), jnp.where(first_core, one, zero)
 
+        def trade_cores(zeros, ones):
+            pairs = [by_core(zero, one) for zero, one in zip(zeros, ones)]
+            came = swap_c(jnp.stack([other for _, other in pairs]))
+            return [by_core(own, came[i]) for i, (own, _) in enumerate(pairs)]
+
+        def trade_seq(entries):
+            pairs = trade_cores(entries[0::2], entries[1::2])
+            pairs = xor_parts([jnp.stack(pair) for pair in pairs], at_z)
+            pairs = xor_parts(shift(pairs, swap_z), at_z)
+            return [pairs[i // 2][i % 2] for i in range(n_s)]
+
+        def trade_mlp(entries):
+            pairs = trade_cores(entries[0::2], entries[1::2])
+            pairs = xor_parts([jnp.stack(pair) for pair in pairs], at_f)
+            pairs = xor_parts(shift(pairs, swap_f), at_f)
+            return [pairs[i // 2][i % 2] for i in range(n_f * CORES)]
+
         width = bias_vector.shape[0]
-        pad = -(-width // 1024) * 1024
-        small = jnp.concatenate(
-            [
-                jnp.pad(bias_vector.astype(bf16), (0, pad - width)).reshape(-1, 128),
-                condition.reshape(-1, 128),
-            ]
-        )
-        small = lax.all_gather(small, ("fsdp", "z", "core"), axis=0, tiled=False)
-        bias_all = small[:, : pad // 128].reshape(n_g, pad)[:, :width].reshape(-1).astype(f32)
-        cond_all = small.reshape(n_f, n_s, -1, 128)[:, 0, pad // 128 :]
+        modul_low = modul_weight.astype(bf16)
+        modul_rows = double(modul_low, swap_f, n_f).reshape(n_f * rows, 6 * D)
+        small = double(jnp.concatenate([condition.reshape(-1), bias_vector.astype(bf16)]), swap_f, n_f)
+        cond_all = small[:, : images_group * D]
         cond_all = cond_all.reshape(n_f * images_group, D).astype(f32)
-        bias_mod = bias_all[: 6 * D]
-        bias_query = bias_all[6 * D : 7 * D].reshape(n_s, hd)
-        bias_value = bias_all[7 * D : 8 * D].reshape(n_s, hd)
-        bias_proj = bias_all[8 * D : 9 * D]
-        bias_widen = bias_all[9 * D : 9 * D + FF].reshape(n_f, n_z, CORES, ub)
-        bias_narrow = bias_all[9 * D + FF :]
-
-        modul_low = modul_weight.astype(bf16)
-        modul_rows = lax.all_gather(modul_low, "fsdp", axis=0, tiled=True)
+        bias_rows = jnp.stack(
+            xor_parts([small[k, images_group * D :] for k in range(n_f)], at_f)
+        )
+        bias_placed = (bias_rows.astype(f32)[:, None, :] * pick_s[None, :, None]).reshape(-1)
 
         tokens_z = jnp.stack(all_z(tokens))
         tokens_group = jnp.stack([tokens_z, swap_c(tokens_z)], axis=1).reshape(n_s, BLOCK, D)
 
         qkv_low = qkv_weight.astype(bf16).reshape(rows, 3, n_s, hd)
-        qkv_out = xor_take(qkv_low.transpose(2, 0, 1, 3), at_s).reshape(n_z, CORES, rows, 3 * hd)
-        qkv_mine = swap_rows_seq(qkv_out).reshape(n_s, rows, 3 * hd)
-        qkv_in = jnp.stack(all_f(qkv_mine)).reshape(n_g, rows, 3 * hd)
-        qkv_full = xor_take(qkv_in, at_g).reshape(D, 3 * hd)
+        qkv_mine = trade_seq([qkv_low[:, :, i].reshape(rows, 3 * hd) for i in range(n_s)])
+        qkv_mine = jnp.stack(qkv_mine)
+        qkv_full = jnp.stack(xor_parts(all_f(qkv_mine), at_f)).reshape(D, 3 * hd)
 
         proj_full = lax.all_gather(
             proj_weight.astype(bf16), ("fsdp", "z", "core"), axis=0, tiled=True
-        )
-        narrow_full = lax.all_gather(narrow_weight.astype(bf16), "z", axis=0, tiled=True)
-        widen_low = widen_weight.astype(bf16).reshape(rows, n_f, n_z, CORES, ub)
-        widen_out = widen_low.transpose(1, 3, 0, 2, 4).reshape(n_f * CORES, rows, units)
-        widen_mine = lax.all_to_all(widen_out, ("fsdp", "core"), 0, 0)
-        widen_in = lax.all_gather(widen_mine.reshape(-1, units), "z", axis=0, tiled=False)
-        widen_full = (
-            widen_in.reshape(n_z, n_f, CORES, rows, units).transpose(1, 0, 2, 3, 4).reshape(D, units)
         )
 
         cond_float = condition.astype(f32)
         cond_act = jax.nn.silu(cond_float).astype(bf16).reshape(images_group, n_f, n_s, rows)
         cond_rows = lax.dynamic_index_in_dim(cond_act, at_s, 2, keepdims=False)
+        cond_rows = jnp.stack(xor_parts([cond_rows[:, k] for k in range(n_f)], at_f), axis=1)
         modul_part = matmul(cond_rows.reshape(images_group, n_f * rows), modul_rows)
-        modulation = reduce_seq(modul_part) + bias_mod
+        modul_part = (modul_part + bias_placed[: 6 * D]).reshape(-1)
+        whole = reduce_seq(jnp.concatenate([modul_part, bias_placed[6 * D :]]))
+        modulation = whole[: images_group * 6 * D].reshape(images_group, 6 * D)
+        bias_all = whole[images_group * 6 * D :]
+        bias_query = bias_all[:D].reshape(n_s, hd)
+        bias_value = bias_all[D : 2 * D].reshape(n_s, hd)
+        bias_proj = bias_all[2 * D : 3 * D]
+        bias_widen = bias_all[3 * D : 3 * D + FF].reshape(n_f, n_z, CORES, ub)
+        bias_narrow = bias_all[3 * D + FF :]
+
+        widen_late = after(widen_weight, qkv_mine)
+        widen_low = widen_late.astype(bf16).reshape(rows, n_f, n_z, CORES, ub)
+        widen_mine = trade_mlp(
+            [
+                widen_low[:, i // CORES, :, i % CORES].reshape(rows, units)
+                for i in range(n_f * CORES)
+            ]
+        )
+        narrow_low = narrow_weight.astype(bf16)
+        hidden = jnp.concatenate(
+            widen_mine + [narrow_low[:, i : i + units] for i in range(0, D, units)]
+        )
+        split = n_f * CORES * rows
+        hidden = lax.all_gather(hidden, "z", axis=0, tiled=False)
+        widen_full = hidden[:, :split].reshape(n_z, n_f, CORES * rows, units)
+        widen_full = widen_full.transpose(1, 0, 2, 3).reshape(D, units)
+        narrow_full = hidden[:, split:].reshape(n_z, D // units, ub, units)
+        narrow_full = narrow_full.transpose(0, 2, 1, 3).reshape(units, D)
 
         own_id = lax.dynamic_index_in_dim(local_ids, at_s, keepdims=False)
         image_pick = (own_id == jnp.arange(images_group, dtype=jnp.int32)).astype(f32)
@@ -233,6 +298,21 @@
                 values = values.reshape(n_s, BLOCK, hd)[restore].reshape(tok_group, hd)
             return values
 
+        def send_blocks(values):
+            came = swap_c(values[:, 1])
+            parts = shift([jnp.stack([values[k, 0], came[k]]) for k in range(n_z)], swap_z)
+            pairs = [by_core(part[0], part[1]) for part in xor_parts(parts, at_z)]
+            return jnp.concatenate([part for pair in pairs for part in pair], axis=1)
+
+        def send_heads(values):
+            parts = [values[:, i * hd : (i + 1) * hd] for i in range(n_s)]
+            pairs = [by_core(parts[2 * i], parts[2 * i + 1]) for i in range(n_z)]
+            own = xor_parts([pair[0] for pair in pairs], at_z)
+            other = xor_parts([pair[1] for pair in pairs], at_z)
+            came = swap_c(jnp.stack(other))
+            parts = shift([jnp.stack([own[k], came[k]]) for k in range(n_z)], swap_z)
+            return jnp.stack(parts).reshape(tok_group, hd)
+
         normed_group, _ = normalize(tokens_group.astype(f32))
         h_a = (
             normed_group * (1.0 + group_rows[:, None, D : 2 * D]) + group_rows[:, None, :D]
@@ -256,8 +336,7 @@
                 bf16
             )
         )
-        att_in = swap_rows_seq(attended.reshape(n_z, CORES, BLOCK, hd)).reshape(n_s, BLOCK, hd)
-        att_own = xor_take(att_in, at_s).transpose(1, 0, 2).reshape(BLOCK, D)
+        att_own = send_blocks(attended.reshape(n_z, CORES, BLOCK, hd))
 
         branch_a = matmul(att_own, proj_full) + bias_proj
         inputs = tokens.astype(f32)
@@ -267,9 +346,10 @@
         grad_out = cotangent.astype(f32)
         d_b_own = (gate_b * grad_out).astype(bf16)
 
-        d_b_f = lax.all_gather(d_b_own, "fsdp", axis=0, tiled=False)
+        d_b_f = double(d_b_own, swap_f, n_f)
         d_b = jnp.stack([d_b_f, swap_c(d_b_f)], axis=1).reshape(-1, D)
-        h_b_f = jnp.stack(xor_parts(all_f(h_b_own), at_f))
+        d_b = after(d_b, h_b_own)
+        h_b_f = jnp.stack(all_f(h_b_own))
         h_b = jnp.stack([h_b_f, swap_c(h_b_f)], axis=1).reshape(-1, D)
         bias_units = lax.dynamic_index_in_dim(bias_widen, at_f, 0, keepdims=False)
         bias_units = lax.dynamic_index_in_dim(bias_units, at_c, 1, keepdims=False).reshape(units)
@@ -279,36 +359,21 @@
         d_act = jnp.einsum("td,fd->tf", d_b, narrow_full, preferred_element_type=f32)
         d_wide = gelu_pull(d_act)[0].astype(bf16)
         d_hb_part = jnp.einsum("tf,df->td", d_wide, widen_full, preferred_element_type=f32)
-
-        def join_cores(values):
-            return values[:, 0] + swap_c(values[:, 1].astype(bf16)).astype(f32)
-
         d_hb_f = join_cores(d_hb_part.reshape(n_f, CORES, BLOCK, D))
-        d_hb_rel = [
-            lax.dynamic_index_in_dim(d_hb_f, at_f ^ k, keepdims=False) for k in range(n_f)
-        ]
-        d_hb = tree_sum(
-            [d_hb_rel[0]]
-            + [swap_f(d_hb_rel[k].astype(bf16), k).astype(f32) for k in range(1, n_f)]
-        )
+        d_hb = add_parts(d_hb_f[0], [swap_f(d_hb_f[k].astype(bf16), k) for k in range(1, n_f)])
         branch_part = join_cores(matmul(activated, narrow_full).reshape(n_f, CORES, BLOCK, D))
-        branch_b = (
-            lax.psum_scatter(branch_part, "fsdp", scatter_dimension=0, tiled=False) + bias_narrow
-        )
-        block_output = (middle + gate_b * branch_b).astype(bf16)
-        d_gate_b = jnp.sum(grad_out * branch_b, axis=0)
         grad_narrow = jnp.einsum("tf,td->fd", activated, d_b, preferred_element_type=f32)
-        narrow_sum = lax.psum_scatter(grad_narrow, "z", scatter_dimension=0, tiled=True)
         grad_widen = jnp.einsum("td,tf->df", h_b, d_wide, preferred_element_type=f32)
-        grad_widen = grad_widen.reshape(n_f, n_z, CORES * rows, units).transpose(1, 0, 2, 3)
-        widen_mid = lax.psum_scatter(
-            grad_widen.reshape(n_z, -1, units), "z", scatter_dimension=0, tiled=False
-        )
-        widen_back = lax.all_to_all(
-            widen_mid.astype(bf16).reshape(n_f * CORES, rows, units), ("fsdp", "core"), 0, 0
-        )
-        widen_sum = widen_back.reshape(n_f, CORES, rows, n_z, ub).transpose(2, 0, 3, 1, 4)
-        widen_sum = widen_sum.reshape(rows, FF).astype(f32)
+        grad_narrow = grad_narrow.reshape(n_z, ub, D)
+        grad_widen = grad_widen.reshape(n_f, n_z, CORES, rows, units)
+
+        grad_hidden = jnp.concatenate(
+            [grad_widen.transpose(1, 0, 2, 3, 4).reshape(n_z, split, units)]
+            + [grad_narrow[:, :, i : i + units] for i in range(0, D, units)],
+            axis=1,
+        )
+        grad_hidden = after(grad_hidden.astype(bf16), d_hb_f)
+        hidden_low = lax.psum_scatter(grad_hidden, "z", scatter_dimension=0, tiled=False)
 
         d_shift_b = jnp.sum(d_hb, axis=0)
         d_scale_b = jnp.sum(d_hb * normed_b, axis=0)
@@ -316,15 +381,17 @@
         d_gate_a = jnp.sum(d_middle * branch_a, axis=0)
         d_a = (gate_a * d_middle).astype(bf16)
         d_att_own = jnp.einsum("te,de->td", d_a, proj_full, preferred_element_type=f32)
-        d_att_own = d_att_own.astype(bf16).reshape(BLOCK, n_s, hd).transpose(1, 0, 2)
-        d_att_out = xor_take(d_att_own, at_s).reshape(n_z, CORES, BLOCK, hd)
-        d_att = by_image(swap_rows_seq(d_att_out).reshape(tok_group, hd))
+        d_att = by_image(send_heads(d_att_own.astype(bf16)))
         grad_proj = jnp.einsum("td,te->de", att_own, d_a, preferred_element_type=f32)
-        proj_own, proj_other = own_other(grad_proj.reshape(n_f * n_z, CORES, rows, D), 1)
+        grad_proj = grad_proj.reshape(n_f, n_z, CORES, rows, D)
+        proj_own, proj_other = by_core(grad_proj[:, :, 0], grad_proj[:, :, 1])
         proj_both = proj_own + swap_c(proj_other.astype(bf16)).astype(f32)
-        proj_sum = lax.psum_scatter(
-            proj_both.reshape(-1, D), ("fsdp", "z"), scatter_dimension=0, tiled=True
-        )
+
+        def mixed(k):
+            part = lax.dynamic_index_in_dim(proj_both, at_f ^ k, 0, keepdims=False)
+            return jnp.concatenate([branch_part[k], part.reshape(n_z * rows, D)])
+
+        mixed_sum = halve([mixed(k) for k in range(n_f)], swap_f)
 
         d_values = jnp.einsum("ihqk,ihqd->ihkd", probs_low, d_att, preferred_element_type=f32)
         d_probs = jnp.einsum("ihqd,ihkd->ihqk", d_att, values, preferred_element_type=f32)
@@ -341,19 +408,25 @@
             [by_block(part.astype(bf16)) for part in (d_queries, d_keys, d_values)], axis=1
         )
         d_ha_part = jnp.einsum("te,de->td", d_qkv, qkv_full, preferred_element_type=f32)
+        mixed_sum = after(mixed_sum, d_ha_part)
+        branch_b = mixed_sum[:BLOCK] + bias_narrow
+        block_output = (middle + gate_b * branch_b).astype(bf16)
+        d_gate_b = jnp.sum(grad_out * branch_b, axis=0)
+        proj_mid = xor_parts(
+            [mixed_sum[i : i + rows] for i in range(BLOCK, BLOCK + n_z * rows, rows)], at_z
+        )
+        proj_sum = halve(proj_mid, swap_z)
+
         d_ha_z = join_cores(d_ha_part.reshape(n_z, CORES, BLOCK, D))
-        d_ha = tree_sum(
-            [d_ha_z[0]] + [swap_z(d_ha_z[k].astype(bf16), k).astype(f32) for k in range(1, n_z)]
-        )
+        d_ha = add_parts(d_ha_z[0], [swap_z(d_ha_z[k].astype(bf16), k) for k in range(1, n_z)])
         grad_qkv = jnp.einsum("td,te->de", h_a, d_qkv, preferred_element_type=f32)
-        grad_qkv = xor_take(grad_qkv.reshape(n_g, rows, 3 * hd), at_g)
-        grad_qkv = grad_qkv.reshape(n_f, n_s, rows, 3 * hd)
-        qkv_mid = tree_sum(
-            [grad_qkv[0]]
-            + [swap_f(grad_qkv[k].astype(bf16), k).astype(f32) for k in range(1, n_f)]
-        )
-        qkv_back = swap_rows_seq(qkv_mid.reshape(n_z, CORES, rows, 3 * hd))
-        qkv_sum = xor_take(qkv_back.reshape(n_s, rows, 3, hd), at_s)
+        grad_qkv = grad_qkv.reshape(n_f, n_s * rows, 3 * hd)
+        grad_qkv = [
+            lax.dynamic_index_in_dim(grad_qkv, at_f ^ k, 0, keepdims=False) for k in range(n_f)
+        ]
+        qkv_mid = halve(grad_qkv, swap_f)
+        qkv_sum = trade_seq([qkv_mid[i : i + rows] for i in range(0, n_s * rows, rows)])
+        qkv_sum = jnp.stack(qkv_sum).reshape(n_s, rows, 3, hd)
         qkv_sum = qkv_sum.transpose(1, 2, 0, 3).reshape(rows, 3 * D)
         normed_a, spread_a = normalize(inputs)
         d_shift_a = jnp.sum(d_ha, axis=0)
@@ -362,9 +435,16 @@
             d_middle + norm_back(d_ha * (1.0 + scale_a), normed_a, spread_a)
         ).astype(bf16)
 
-        pick_f = (jnp.arange(n_f) == at_f).astype(f32)
-        pick_c = (jnp.arange(CORES) == at_c).astype(f32)
-        pick_s = (jnp.arange(n_s) == at_s).astype(f32)
+        hidden_sum = after(hidden_low, d_ha).astype(f32)
+        narrow_sum = jnp.concatenate(
+            [hidden_sum[i : i + ub] for i in range(split, hidden_sum.shape[0], ub)], axis=1
+        )
+        widen_back = trade_mlp(
+            [hidden_sum[i : i + rows].astype(bf16) for i in range(0, split, rows)]
+        )
+        widen_sum = jnp.stack(widen_back).reshape(n_f, CORES, rows, n_z, ub)
+        widen_sum = widen_sum.transpose(2, 0, 3, 1, 4).reshape(rows, FF).astype(f32)
+
         units_sum = column_sums(d_wide).reshape(n_z, ub)
         bias_g_widen = (
             pick_f[:, None, None, None] * pick_c[None, None, :, None] * units_sum[None, :, None, :]
@@ -374,31 +454,28 @@
         bias_g_value = (pick_s[:, None] * heads_sum[None, 2 * hd :]).reshape(D)
         d_block = jnp.concatenate([d_shift_a, d_scale_a, d_gate_a, d_shift_b, d_scale_b, d_gate_b])
         per_image = (image_pick[:, None] * d_block[None, :]).reshape(-1)
-        sums = reduce_seq(
-            jnp.concatenate(
-                [
-                    per_image,
-                    bias_g_query,
-                    bias_g_value,
-                    column_sums(d_a),
-                    bias_g_widen,
-                    column_sums(d_b_own),
-                ]
-            )
-        )
-        split = images_group * 6 * D
-        whole = jnp.stack(xor_parts(all_f(sums), at_f))
-        d_modulation = whole[:, :split].reshape(n_f * images_group, 6 * D)
+        pieces = [
+            per_image,
+            bias_g_query,
+            bias_g_value,
+            column_sums(d_a),
+            bias_g_widen,
+            column_sums(d_b_own),
+        ]
+        sums = reduce_seq(jnp.concatenate(pieces))
+        cut = images_group * 6 * D
+        whole = double(sums, swap_f, n_f)
+        d_modulation = whole[:, :cut].reshape(n_f * images_group, 6 * D)
         all_act = jax.nn.silu(cond_all).astype(bf16).astype(f32)
         act_cols = lax.dynamic_slice_in_dim(all_act, at_g * rows, rows, axis=1)
         modul_sum = sum(
             act_cols[i][:, None] * d_modulation[i][None, :] for i in range(n_f * images_group)
         )
         bias_grad = jnp.concatenate(
-            [jnp.sum(d_modulation, axis=0), jnp.sum(whole[:, split:], axis=0)]
+            [jnp.sum(d_modulation, axis=0), jnp.sum(whole[:, cut:], axis=0)]
         )
         bias_sum = lax.dynamic_slice_in_dim(bias_grad, at_g * width, width)
-        d_own = sums[:split].reshape(images_group, 6 * D)
+        d_own = sums[:cut].reshape(images_group, 6 * D)
         d_cond_rows = jnp.einsum(
             "im,dm->id",
             d_own,
@@ -406,10 +483,12 @@
             precision=lax.Precision.HIGHEST,
             preferred_element_type=f32,
         )
-        d_cond_z = jnp.stack(all_z(d_cond_rows))
-        d_cond = jnp.stack([d_cond_z, swap_c(d_cond_z)], axis=1)
-        d_cond = xor_take(d_cond.reshape(n_s, images_group, n_f, rows), at_s)
-        d_cond_act = d_cond.transpose(1, 2, 0, 3).reshape(images_group, D)
+        d_cond_z = double(d_cond_rows, swap_z, n_z)
+        d_cond_z = jnp.stack(xor_parts([d_cond_z[k] for k in range(n_z)], at_z))
+        d_cond = jnp.stack(by_core(d_cond_z, swap_c(d_cond_z)), axis=1)
+        d_cond = d_cond.reshape(n_s, images_group, n_f, rows).transpose(2, 1, 0, 3)
+        d_cond = jnp.stack(xor_parts([d_cond[k] for k in range(n_f)], at_f))
+        d_cond_act = d_cond.transpose(1, 0, 2, 3).reshape(images_group, D)
         silu_pull = jax.vjp(jax.nn.silu, cond_float)[1]
         condition_grad = silu_pull(d_cond_act)[0]
 

time: 534 us -> 444 us (0.83)
  waiting for transfers between devices: 224 us -> 166 us
  blocking collectives: 43 us -> 0 us
  local copies, waits for them, and re-layouts: 47.7 us -> 61.9 us
  matrix products: 52.3 us -> 39.6 us
  other arithmetic: 73.8 us -> 83.9 us
    reduce_scatter x3 -> x1, waiting for transfers between devices: 99.6 us -> 0.01 us  [shards(): lax.psum_scatter(grad_hidden, 'z', scatter_dimension=0, tiled=False)]
    ppermute x56 -> x63, waiting for transfers between devices: 76.5 us -> 166 us  [swap(): return lax.ppermute(values, axis, [(i, i ^ k) for i in range(size)])]
    all_gather x1 -> x0, blocking collectives: 43 us -> none  [shards(): small = lax.all_gather(small, ('fsdp', 'z', 'core'), axis=0, tiled=False)]
    all_gather x4 -> x1, waiting for transfers between devices: 25.6 us -> 0.01 us  [shards(): hidden = lax.all_gather(hidden, 'z', axis=0, tiled=False)]
    unnamed x10 -> x3, waiting for transfers between devices: 14.3 us -> 0.05 us
    another operation x11 -> x51, other arithmetic: 5.15 us -> 18.7 us
    unnamed x182 -> x216, local copies, waits for them, and re-layouts: 8.83 us -> 20.4 us
    ppermute x56 -> x63, starting transfers between devices: 59.7 us -> 68.7 us  [swap(): return lax.ppermute(values, axis, [(i, i ^ k) for i in range(size)])]
  transfers between devices with their start and end apart: 67 -> 66, of which waited for: 32 -> 38; matrix products, arithmetic and copies ran while one was open for 23% -> 37% of each run, Pallas kernels for 0% -> 0%
where the time goes in v2:
time: 444 us; the launch traced here: 438 us
  waiting for transfers between devices  166 us (37%)
  other arithmetic  83.9 us (19%)
  starting transfers between devices  69.3 us (16%)
  local copies, waits for them, and re-layouts  61.9 us (14%)
  matrix products  39.6 us (9%)
  between operations  17.4 us (4%)
    ppermute x63, waiting for transfers between devices, swap(): return lax.ppermute(values, axis, [(i, i ^ k) for i in range(size)])  166 us
    ppermute x63, starting transfers between devices, swap(): return lax.ppermute(values, axis, [(i, i ^ k) for i in range(size)])  68.7 us
    unnamed x216, local copies, waits for them, and re-layouts  20.4 us
    sub x6, other arithmetic, adam_step(): weight - rate * (first / fix_first / (jnp.sqrt(second / fix_second) + ada...  9.01 us
  transfers between devices with their start and end apart: 66, of which 38 were waited for; matrix products, arithmetic and copies ran while one was open for 37% of the time, Pallas kernels for 0%

profile of v2, /device:TPU:0, one launch (start us, length us, event | category | flops | bytes accessed | tf_op | source)
XLA Modules:
  0.0 437.8 jit_solution(13361622657446250093)
XLA Ops:
  7.3 3.1 collective-permute-start.7
  29.6 5.0 %collective-permute-done.12 = bf16[2,2,32,384]{3,2,1,0:T(8,128)(2,1)S(1)} collective-permute-done((bf16[2,2,32,384]{3,2,1,0:T(8,128)(2,1)S(1)}, bf16[2,2,32,384]{3,2,1,0:T(8,128)(2,1)S(1)}, u32[]{:S(2)}, u32[]{:S(2)}) %collective-permute-start.12) | collective-permute-done | bytes 98336 | tf_op jit(solution)/shard_map/ppermute | solution.py:92
  34.6 4.4 %collective-permute-start.13 = (bf16[2,2,32,384]{3,2,1,0:T(8,128)(2,1)S(1)}, bf16[2,2,32,384]{3,2,1,0:T(8,128)(2,1)S(1)}, u32[]{:S(2)}, u32[]{:S(2)}) collective-permute-start(bf16[2,2,32,384]{3,2,1,0:T(8,128)(2,1)S(1)} %pad_maximum_fusion.37), channel_id=1, source_target_pairs={{0,4},{2,6},{4,0},{6,2},{1,5},{3,7},{5,1},{7,3},{8,12},{10,14},{12... | collective-permute-start | bytes 294920 | tf_op jit(solution)/shard_map/ppermute | solution.py:92
  62.9 18.1 %collective-permute-done.26 = bf16[2,2,32,512]{3,2,1,0:T(8,128)(2,1)S(1)} collective-permute-done((bf16[2,2,32,512]{3,2,1,0:T(8,128)(2,1)S(1)}, bf16[2,2,32,512]{3,2,1,0:T(8,128)(2,1)S(1)}, u32[]{:S(2)}, u32[]{:S(2)}) %collective-permute-start.26) | collective-permute-done | bytes 131104 | tf_op jit(solution)/shard_map/ppermute | solution.py:92
  95.0 3.1 collective-permute-start.6
  124.1 11.1 %collective-permute-done.18 = bf16[2,2,128,128]{3,2,1,0:T(8,128)(2,1)S(1)} collective-permute-done((bf16[2,2,128,128]{3,2,1,0:T(8,128)(2,1)}, bf16[2,2,128,128]{3,2,1,0:T(8,128)(2,1)S(1)}, u32[]{:S(2)}, u32[]{:S(2)}) %collective-permute-start.18) | collective-permute-done | bytes 131104 | tf_op jit(solution)/shard_map/ppermute | solution.py:92
  137.7 2.9 fusion.4
  143.1 3.1 collective-permute-done.19
  148.2 7.2 %collective-permute-done.29 = bf16[2,128,1024]{2,1,0:T(8,128)(2,1)S(1)} collective-permute-done((bf16[2,128,1024]{2,1,0:T(8,128)(2,1)S(1)}, bf16[2,128,1024]{2,1,0:T(8,128)(2,1)S(1)}, u32[]{:S(2)}, u32[]{:S(2)}) %collective-permute-start.29) | collective-permute-done | bytes 524320 | tf_op jit(solution)/shard_map/ppermute | solution.py:92
  157.9 3.1 fusion.133
  168.5 3.9 collective-permute-done.22
  172.5 5.2 %collective-permute-done.21 = bf16[128,1024]{1,0:T(8,128)(2,1)} collective-permute-done((bf16[128,1024]{1,0:T(8,128)(2,1)}, bf16[128,1024]{1,0:T(8,128)(2,1)}, u32[]{:S(2)}, u32[]{:S(2)}) %collective-permute-start.21) | collective-permute-done | bytes 262176 | tf_op jit(solution)/shard_map/ppermute | solution.py:92
  210.2 3.2 fusion.15
  215.8 4.0 fusion.131
  230.1 5.4 %collective-permute-done.34 = bf16[128,1024]{1,0:T(8,128)(2,1)} collective-permute-done((bf16[128,1024]{1,0:T(8,128)(2,1)}, bf16[128,1024]{1,0:T(8,128)(2,1)}, u32[]{:S(2)}, u32[]{:S(2)}) %collective-permute-start.34) | collective-permute-done | bytes 262176 | tf_op jit(solution)/shard_map/ppermute | solution.py:92
  246.5 9.1 %collective-permute-done.39 = bf16[2,2,128,128]{3,2,1,0:T(8,128)(2,1)S(1)} collective-permute-done((bf16[2,2,128,128]{3,2,1,0:T(8,128)(2,1)S(1)}, bf16[2,2,128,128]{3,2,1,0:T(8,128)(2,1)S(1)}, u32[]{:S(2)}, u32[]{:S(2)}) %collective-permute-start.39) | collective-permute-done | bytes 131104 | tf_op jit(solution)/shard_map/ppermute | solution.py:92
  257.0 15.8 %collective-permute-done.40 = bf16[2,2,128,128]{3,2,1,0:T(8,128)(2,1)S(1)} collective-permute-done((bf16[2,2,128,128]{3,2,1,0:T(8,128)(2,1)S(1)}, bf16[2,2,128,128]{3,2,1,0:T(8,128)(2,1)S(1)}, u32[]{:S(2)}, u32[]{:S(2)}) %collective-permute-start.40) | collective-permute-done | bytes 131104 | tf_op jit(solution)/shard_map/ppermute | solution.py:92
  273.1 5.1 %convolution_convert_fusion.3 = bf16[2,1024,64]{1,2,0:T(8,128)(2,1)S(1)} fusion(f32[2,1024,1024]{1,2,0:T(8,128)} %copy-done, f32[2,1024]{1,0:T(2,128)S(1)} %log_add_fusion, bf16[1,1024,2,64]{1,3,2,0:T(8,128)(2,1)S(1)} %reshape_reshape.7), kind=kOutput, calls=%fused_computation.51 | convolution fusion | flops 274857984 | bytes 8921088 | tf_op jit(solution)/shard_map/ihqk,ihqd->ihkd/dot_general | solution.py:396
  278.3 5.3 %multiply_reduce_fusion = (f32[2,1024]{1,0:T(2,128)S(1)}, f32[2,1024,1024]{1,2,0:T(8,128)S(1)}) fusion(f32[2,1024,1024]{1,2,0:T(8,128)} %copy-done, f32[2,1024]{1,0:T(2,128)S(1)} %log_add_fusion, bf16[2,1024,64]{1,2,0:T(8,128)(2,1)S(1)} %bitcast.735, bf16[1,1024,2,64]{1,3,2,0:T(8,128)(2,1)S(1)} %reshape_reshape.7), kind=kOutput, calls=%fused_computation.1 | convolution fusion | flops 276822016 | bytes 17317888 | tf_op jit(solution)/shard_map/ihqd,ihkd->ihqk/dot_general | solution.py:397
  289.2 2.8 fusion.31
  295.3 7.7 %collective-permute-done.53 = bf16[2,256,384]{2,1,0:T(8,128)(2,1)S(1)} collective-permute-done((bf16[2,256,384]{2,1,0:T(8,128)(2,1)S(1)}, bf16[2,256,384]{2,1,0:T(8,128)(2,1)S(1)}, u32[]{:S(2)}, u32[]{:S(2)}) %collective-permute-start.53) | collective-permute-done | bytes 393248 | tf_op jit(solution)/shard_map/ppermute | solution.py:92
  304.8 4.0 collective-permute-done.54
  321.0 3.0 collective-permute-start.57
  330.8 3.2 collective-permute-done.57
  339.7 4.3 collective-permute-done.42
  344.0 11.8 %collective-permute-done.43 = bf16[128,1024]{1,0:T(8,128)(2,1)} collective-permute-done((bf16[128,1024]{1,0:T(8,128)(2,1)}, bf16[128,1024]{1,0:T(8,128)(2,1)}, u32[]{:S(2)}, u32[]{:S(2)}) %collective-permute-start.43) | collective-permute-done | bytes 262176 | tf_op jit(solution)/shard_map/ppermute | solution.py:92
  362.2 11.6 %collective-permute-done.37 = bf16[1,256,1024]{2,1,0:T(8,128)(2,1)S(1)} collective-permute-done((bf16[1,256,1024]{2,1,0:T(8,128)(2,1)S(1)}, bf16[1,256,1024]{2,1,0:T(8,128)(2,1)S(1)}, u32[]{:S(2)}, u32[]{:S(2)}) %collective-permute-start.37) | collective-permute-done | bytes 524320 | tf_op jit(solution)/shard_map/ppermute | solution.py:92
  378.1 3.8 collective-permute-done.46
  384.2 2.9 collective-permute-done.47
  388.6 3.5 collective-permute-done.48
  410.7 3.1 multiply_subtract_fusion
  419.0 4.0 collective-permute-done.61
  (621 shorter events, 236.6 us)
Async XLA Ops:
  7.2 150.6 %all-gather.4.cloned.1.call-start = ((), (), s32[]{:S(2)}) async-start(), calls=%async_computation.1 | async-start | bytes 2162688 | tf_op jit(solution)/shard_map/all_gather | solution.py:233
  7.3 31.8 %collective-permute-start.7 = (bf16[128,1024]{1,0:T(8,128)(2,1)}, bf16[128,1024]{1,0:T(8,128)(2,1)S(1)}, u32[]{:S(2)}, u32[]{:S(2)}) collective-permute-start(bf16[128,1024]{1,0:T(8,128)(2,1)} %param.22), channel_id=1, source_target_pairs={{0,2},{2,0},{4,6},{6,4},{1,3},{3,1},{5,7},{7,5},{8,10},{10,8},{12,... | collective-permute-start | bytes 786440 | tf_op jit(solution)/shard_map/ppermute | solution.py:92
  10.4 28.7 %collective-permute-start.9 = (bf16[128,1024]{1,0:T(8,128)(2,1)}, bf16[128,1024]{1,0:T(8,128)(2,1)S(1)}, u32[]{:S(2)}, u32[]{:S(2)}) collective-permute-start(bf16[128,1024]{1,0:T(8,128)(2,1)} %param.22), channel_id=1, source_target_pairs={{0,6},{2,4},{4,2},{6,0},{1,7},{3,5},{5,3},{7,1},{8,14},{10,12},{12... | collective-permute-start | bytes 786440 | tf_op jit(solution)/shard_map/ppermute | solution.py:92
  12.8 26.2 %collective-permute-start.8 = (bf16[128,1024]{1,0:T(8,128)(2,1)}, bf16[128,1024]{1,0:T(8,128)(2,1)S(1)}, u32[]{:S(2)}, u32[]{:S(2)}) collective-permute-start(bf16[128,1024]{1,0:T(8,128)(2,1)} %param.22), channel_id=1, source_target_pairs={{0,4},{2,6},{4,0},{6,2},{1,5},{3,7},{5,1},{7,3},{8,12},{10,14},{12... | collective-permute-start | bytes 786440 | tf_op jit(solution)/shard_map/ppermute | solution.py:92
  18.2 164.8 %all-gather.6.cloned.1.call-start = ((), (), s32[]{:S(2)}) async-start(), calls=%async_computation.3 | async-start | bytes 2621440 | tf_op jit(solution)/shard_map/all_gather | solution.py:265
  25.5 26.1 %collective-permute-start = (bf16[1,32,6144]{2,1,0:T(8,128)(2,1)S(1)}, bf16[1,32,6144]{2,1,0:T(8,128)(2,1)}, u32[]{:S(2)}, u32[]{:S(2)}) collective-permute-start(bf16[1,32,6144]{2,1,0:T(8,128)(2,1)S(1)} %convert_bitcast_fusion), channel_id=1, source_target_pairs={{0,8},{8,0},{16,24},{24,16},{1,9},{9,1},{17,25},{25,17},{2,10},{10... | collective-permute-start | bytes 1179656 | tf_op jit(solution)/shard_map/ppermute | solution.py:92
  40.2 58.0 %collective-permute-start.10 = (bf16[4,128,1024]{2,1,0:T(8,128)(2,1)}, bf16[4,128,1024]{2,1,0:T(8,128)(2,1)S(1)}, u32[]{:S(2)}, u32[]{:S(2)}) collective-permute-start(bf16[4,128,1024]{2,1,0:T(8,128)(2,1)} %get-tuple-element.134), channel_id=1, source_target_pairs={{0,1},{1,0},{2,3},{3,2},{4,5},{5,4},{6,7},{7,6},{8,9},{9,8},{10,11... | collective-permute-start | bytes 3145736 | tf_op jit(solution)/shard_map/ppermute | solution.py:92
  45.5 11.5 %collective-permute-start.15 = (bf16[8,32,384]{2,1,0:T(8,128)(2,1)}, bf16[8,32,384]{2,1,0:T(8,128)(2,1)}, u32[]{:S(2)}, u32[]{:S(2)}) collective-permute-start(bf16[8,32,384]{2,1,0:T(8,128)(2,1)} %pad_maximum_fusion.16), channel_id=1, source_target_pairs={{0,16},{8,24},{16,0},{24,8},{1,17},{9,25},{17,1},{25,9},{2,18},{10... | collective-permute-start | bytes 589832 | tf_op jit(solution)/shard_map/ppermute | solution.py:92
  52.9 33.1 %collective-permute-start.1 = (bf16[2,32,6144]{2,1,0:T(8,128)(2,1)S(1)}, bf16[2,32,6144]{2,1,0:T(8,128)(2,1)S(1)}, u32[]{:S(2)}, u32[]{:S(2)}) collective-permute-start(bf16[2,32,6144]{2,1,0:T(8,128)(2,1)S(1)} %pad_maximum_fusion.9), channel_id=1, source_target_pairs={{0,16},{8,24},{16,0},{24,8},{1,17},{9,25},{17,1},{25,9},{2,18},{10... | collective-permute-start | bytes 2359304 | tf_op jit(solution)/shard_map/ppermute | solution.py:92
  60.3 20.7 %collective-permute-start.26 = (bf16[2,2,32,512]{3,2,1,0:T(8,128)(2,1)S(1)}, bf16[2,2,32,512]{3,2,1,0:T(8,128)(2,1)S(1)}, u32[]{:S(2)}, u32[]{:S(2)}) collective-permute-start(bf16[2,2,32,512]{3,2,1,0:T(8,128)(2,1)S(1)} %pad_maximum_fusion.26), channel_id=1, source_target_pairs={{0,16},{8,24},{16,0},{24,8},{1,17},{9,25},{17,1},{25,9},{2,18},{10... | collective-permute-start | bytes 393224 | tf_op jit(solution)/shard_map/ppermute | solution.py:92
  93.2 320.7 %reduce-scatter.2.cloned.1.call-start = ((), (), s32[]{:S(2)}) async-start(), calls=%async_computation.2 | async-start | bytes 2621440 | tf_op jit(solution)/shard_map/reduce_scatter | solution.py:376
  118.3 16.8 %collective-permute-start.18 = (bf16[2,2,128,128]{3,2,1,0:T(8,128)(2,1)}, bf16[2,2,128,128]{3,2,1,0:T(8,128)(2,1)S(1)}, u32[]{:S(2)}, u32[]{:S(2)}) collective-permute-start(bf16[2,2,128,128]{3,2,1,0:T(8,128)(2,1)} %pad_maximum_fusion.22), channel_id=1, source_target_pairs={{0,2},{2,0},{4,6},{6,4},{1,3},{3,1},{5,7},{7,5},{8,10},{10,8},{12,... | collective-permute-start | bytes 393224 | tf_op jit(solution)/shard_map/ppermute | solution.py:92
  120.7 20.9 %collective-permute-start.28 = (bf16[1,128,1024]{2,1,0:T(8,128)(2,1)S(1)}, bf16[1,128,1024]{2,1,0:T(8,128)(2,1)S(1)}, u32[]{:S(2)}, u32[]{:S(2)}) collective-permute-start(bf16[1,128,1024]{2,1,0:T(8,128)(2,1)S(1)} %fusion.60), channel_id=1, source_target_pairs={{0,8},{8,0},{16,24},{24,16},{1,9},{9,1},{17,25},{25,17},{2,10},{10... | collective-permute-start | bytes 786440 | tf_op jit(solution)/shard_map/ppermute | solution.py:92
  141.7 13.7 %collective-permute-start.29 = (bf16[2,128,1024]{2,1,0:T(8,128)(2,1)S(1)}, bf16[2,128,1024]{2,1,0:T(8,128)(2,1)S(1)}, u32[]{:S(2)}, u32[]{:S(2)}) collective-permute-start(bf16[2,128,1024]{2,1,0:T(8,128)(2,1)S(1)} %pad_maximum_fusion.12), channel_id=1, source_target_pairs={{0,16},{8,24},{16,0},{24,8},{1,17},{9,25},{17,1},{25,9},{2,18},{10... | collective-permute-start | bytes 1572872 | tf_op jit(solution)/shard_map/ppermute | solution.py:92
  157.8 22.1 %collective-permute-start.30 = (bf16[4,128,1024]{2,1,0:T(8,128)(2,1)}, bf16[4,128,1024]{2,1,0:T(8,128)(2,1)}, u32[]{:S(2)}, u32[]{:S(2)}) collective-permute-start(bf16[4,128,1024]{2,1,0:T(8,128)(2,1)} %get-tuple-element.132), channel_id=1, source_target_pairs={{0,1},{1,0},{2,3},{3,2},{4,5},{5,4},{6,7},{7,6},{8,9},{9,8},{10,11... | collective-permute-start | bytes 3145736 | tf_op jit(solution)/shard_map/ppermute | solution.py:92
  164.1 13.5 %collective-permute-start.21 = (bf16[128,1024]{1,0:T(8,128)(2,1)}, bf16[128,1024]{1,0:T(8,128)(2,1)}, u32[]{:S(2)}, u32[]{:S(2)}) collective-permute-start(bf16[128,1024]{1,0:T(8,128)(2,1)} %add_convert_fusion.3), channel_id=1, source_target_pairs={{0,16},{8,24},{16,0},{24,8},{1,17},{9,25},{17,1},{25,9},{2,18},{10... | collective-permute-start | bytes 786440 | tf_op jit(solution)/shard_map/ppermute | solution.py:92
  165.0 12.7 %collective-permute-start.20 = (bf16[128,1024]{1,0:T(8,128)(2,1)}, bf16[128,1024]{1,0:T(8,128)(2,1)}, u32[]{:S(2)}, u32[]{:S(2)}) collective-permute-start(bf16[128,1024]{1,0:T(8,128)(2,1)} %add_convert_fusion.3), channel_id=1, source_target_pairs={{0,8},{8,0},{16,24},{24,16},{1,9},{9,1},{17,25},{25,17},{2,10},{10... | collective-permute-start | bytes 786440 | tf_op jit(solution)/shard_map/ppermute | solution.py:92
  179.9 11.4 %collective-permute-start.23 = (bf16[4,128,1024]{2,1,0:T(8,128)(2,1)}, bf16[4,128,1024]{2,1,0:T(8,128)(2,1)}, u32[]{:S(2)}, u32[]{:S(2)}) collective-permute-start(bf16[4,128,1024]{2,1,0:T(8,128)(2,1)} %get-tuple-element.130), channel_id=1, source_target_pairs={{0,1},{1,0},{2,3},{3,2},{4,5},{5,4},{6,7},{7,6},{8,9},{9,8},{10,11... | collective-permute-start | bytes 3145736 | tf_op jit(solution)/shard_map/ppermute | solution.py:92
  201.3 14.4 %collective-permute-start.31 = (bf16[4,128,1024]{2,1,0:T(8,128)(2,1)}, bf16[4,128,1024]{2,1,0:T(8,128)(2,1)}, u32[]{:S(2)}, u32[]{:S(2)}) collective-permute-start(bf16[4,128,1024]{2,1,0:T(8,128)(2,1)} %fusion.21), channel_id=1, source_target_pairs={{0,1},{1,0},{2,3},{3,2},{4,5},{5,4},{6,7},{7,6},{8,9},{9,8},{10,11... | collective-permute-start | bytes 3145736 | tf_op jit(solution)/shard_map/ppermute | solution.py:92
  206.9 17.2 %collective-permute-start.27 = (bf16[4,128,1024]{2,1,0:T(8,128)(2,1)}, bf16[4,128,1024]{2,1,0:T(8,128)(2,1)}, u32[]{:S(2)}, u32[]{:S(2)}) collective-permute-start(bf16[4,128,1024]{2,1,0:T(8,128)(2,1)} %fusion.20), channel_id=1, source_target_pairs={{0,1},{1,0},{2,3},{3,2},{4,5},{5,4},{6,7},{7,6},{8,9},{9,8},{10,11... | collective-permute-start | bytes 3145736 | tf_op jit(solution)/shard_map/ppermute | solution.py:92
  222.0 13.5 %collective-permute-start.34 = (bf16[128,1024]{1,0:T(8,128)(2,1)}, bf16[128,1024]{1,0:T(8,128)(2,1)}, u32[]{:S(2)}, u32[]{:S(2)}) collective-permute-start(bf16[128,1024]{1,0:T(8,128)(2,1)} %get-tuple-element.127), channel_id=1, source_target_pairs={{0,24},{8,16},{16,8},{24,0},{1,25},{9,17},{17,9},{25,1},{2,26},{10... | collective-permute-start | bytes 786440 | tf_op jit(solution)/shard_map/ppermute | solution.py:92
  223.3 13.6 %collective-permute-start.33 = (bf16[128,1024]{1,0:T(8,128)(2,1)}, bf16[128,1024]{1,0:T(8,128)(2,1)}, u32[]{:S(2)}, u32[]{:S(2)}) collective-permute-start(bf16[128,1024]{1,0:T(8,128)(2,1)} %get-tuple-element.128), channel_id=1, source_target_pairs={{0,16},{8,24},{16,0},{24,8},{1,17},{9,25},{17,1},{25,9},{2,18},{10... | collective-permute-start | bytes 786440 | tf_op jit(solution)/shard_map/ppermute | solution.py:92
  243.2 12.4 %collective-permute-start.39 = (bf16[2,2,128,128]{3,2,1,0:T(8,128)(2,1)S(1)}, bf16[2,2,128,128]{3,2,1,0:T(8,128)(2,1)S(1)}, u32[]{:S(2)}, u32[]{:S(2)}) collective-permute-start(bf16[2,2,128,128]{3,2,1,0:T(8,128)(2,1)S(1)} %pad_maximum_fusion.28), channel_id=1, source_target_pairs={{0,2},{2,0},{4,6},{6,4},{1,3},{3,1},{5,7},{7,5},{8,10},{10,8},{12,... | collective-permute-start | bytes 393224 | tf_op jit(solution)/shard_map/ppermute | solution.py:92
  255.7 17.1 %collective-permute-start.40 = (bf16[2,2,128,128]{3,2,1,0:T(8,128)(2,1)S(1)}, bf16[2,2,128,128]{3,2,1,0:T(8,128)(2,1)S(1)}, u32[]{:S(2)}, u32[]{:S(2)}) collective-permute-start(bf16[2,2,128,128]{3,2,1,0:T(8,128)(2,1)S(1)} %pad_maximum_fusion.29), channel_id=1, source_target_pairs={{0,4},{2,6},{4,0},{6,2},{1,5},{3,7},{5,1},{7,3},{8,12},{10,14},{12... | collective-permute-start | bytes 393224 | tf_op jit(solution)/shard_map/ppermute | solution.py:92
  257.0 52.1 %collective-permute-start.35 = (bf16[4,4,32,1024]{3,2,1,0:T(8,128)(2,1)}, bf16[4,4,32,1024]{3,2,1,0:T(8,128)(2,1)}, u32[]{:S(2)}, u32[]{:S(2)}) collective-permute-start(bf16[4,4,32,1024]{3,2,1,0:T(8,128)(2,1)} %fusion.19), channel_id=1, source_target_pairs={{0,1},{1,0},{2,3},{3,2},{4,5},{5,4},{6,7},{7,6},{8,9},{9,8},{10,11... | collective-permute-start | bytes 3145736 | tf_op jit(solution)/shard_map/ppermute | solution.py:92
  295.0 29.0 %collective-permute-start.41 = (bf16[4,128,1024]{2,1,0:T(8,128)(2,1)S(1)}, bf16[4,128,1024]{2,1,0:T(8,128)(2,1)}, u32[]{:S(2)}, u32[]{:S(2)}) collective-permute-start(bf16[4,128,1024]{2,1,0:T(8,128)(2,1)S(1)} %fusion.22), channel_id=1, source_target_pairs={{0,1},{1,0},{2,3},{3,2},{4,5},{5,4},{6,7},{7,6},{8,9},{9,8},{10,11... | collective-permute-start | bytes 3145736 | tf_op jit(solution)/shard_map/ppermute | solution.py:92
  313.4 45.8 %collective-permute-start.36 = (bf16[2,256,1024]{2,1,0:T(8,128)(2,1)}, bf16[2,256,1024]{2,1,0:T(8,128)(2,1)}, u32[]{:S(2)}, u32[]{:S(2)}) collective-permute-start(bf16[2,256,1024]{2,1,0:T(8,128)(2,1)} %pad_maximum_fusion.8), channel_id=1, source_target_pairs={{0,16},{8,24},{16,0},{24,8},{1,17},{9,25},{17,1},{25,9},{2,18},{10... | collective-permute-start | bytes 3145736 | tf_op jit(solution)/shard_map/ppermute | solution.py:92
  321.0 13.0 %collective-permute-start.57 = (f32[2,2,32,384]{3,2,1,0:T(8,128)S(1)}, f32[2,2,32,384]{3,2,1,0:T(8,128)S(1)}, u32[]{:S(2)}, u32[]{:S(2)}) collective-permute-start(f32[2,2,32,384]{3,2,1,0:T(8,128)S(1)} %pad_maximum_fusion.19), channel_id=1, source_target_pairs={{0,4},{2,6},{4,0},{6,2},{1,5},{3,7},{5,1},{7,3},{8,12},{10,14},{12... | collective-permute-start | bytes 589832 | tf_op jit(solution)/shard_map/ppermute | solution.py:92
  327.3 16.7 %collective-permute-start.42 = (bf16[128,1024]{1,0:T(8,128)(2,1)}, bf16[128,1024]{1,0:T(8,128)(2,1)}, u32[]{:S(2)}, u32[]{:S(2)}) collective-permute-start(bf16[128,1024]{1,0:T(8,128)(2,1)} %get-tuple-element.121), channel_id=1, source_target_pairs={{0,2},{2,0},{4,6},{6,4},{1,3},{3,1},{5,7},{7,5},{8,10},{10,8},{12,... | collective-permute-start | bytes 786440 | tf_op jit(solution)/shard_map/ppermute | solution.py:92
  327.3 16.7 %collective-permute-start.44 = (bf16[128,1024]{1,0:T(8,128)(2,1)}, bf16[128,1024]{1,0:T(8,128)(2,1)}, u32[]{:S(2)}, u32[]{:S(2)}) collective-permute-start(bf16[128,1024]{1,0:T(8,128)(2,1)} %get-tuple-element.122), channel_id=1, source_target_pairs={{0,6},{2,4},{4,2},{6,0},{1,7},{3,5},{5,3},{7,1},{8,14},{10,12},{12... | collective-permute-start | bytes 786440 | tf_op jit(solution)/shard_map/ppermute | solution.py:92
  328.8 27.1 %collective-permute-start.43 = (bf16[128,1024]{1,0:T(8,128)(2,1)}, bf16[128,1024]{1,0:T(8,128)(2,1)}, u32[]{:S(2)}, u32[]{:S(2)}) collective-permute-start(bf16[128,1024]{1,0:T(8,128)(2,1)} %get-tuple-element.123), channel_id=1, source_target_pairs={{0,4},{2,6},{4,0},{6,2},{1,5},{3,7},{5,1},{7,3},{8,12},{10,14},{12... | collective-permute-start | bytes 786440 | tf_op jit(solution)/shard_map/ppermute | solution.py:92
  360.5 13.3 %collective-permute-start.37 = (bf16[1,256,1024]{2,1,0:T(8,128)(2,1)S(1)}, bf16[1,256,1024]{2,1,0:T(8,128)(2,1)S(1)}, u32[]{:S(2)}, u32[]{:S(2)}) collective-permute-start(bf16[1,256,1024]{2,1,0:T(8,128)(2,1)S(1)} %fusion.24), channel_id=1, source_target_pairs={{0,8},{8,0},{16,24},{24,16},{1,9},{9,1},{17,25},{25,17},{2,10},{10... | collective-permute-start | bytes 1572872 | tf_op jit(solution)/shard_map/ppermute | solution.py:92
  (131 other events, 1033.7 us)
Sparse Core Ops, SparseCore 0:
  18.3 61.5 all-gather.3
  93.3 47.0 all-gather.5
  226.8 48.8 reduce-scatter.1

commit v3 on v2

--- a/solution.py
+++ b/solution.py
@@ -106,11 +106,37 @@
     def all_f(values):
         return [swap_f(values, k) for k in range(n_f)]
 
+
+    def run(*chains):
+        results = [None] * len(chains)
+        pending = {}
+        for i, chain in enumerate(chains):
+            try:
+                pending[i] = next(chain)
+            except StopIteration as stop:
+                results[i] = stop.value
+        while pending:
+            leaves, tree = jax.tree.flatten(pending)
+            if len(leaves) > 1:
+                leaves = lax.optimization_barrier(leaves)
+            came = jax.tree.unflatten(tree, leaves)
+            pending = {}
+            for i, value in came.items():
+                try:
+                    pending[i] = chains[i].send(value)
+                except StopIteration as stop:
+                    results[i] = stop.value
+        return results
+
+    def alone(chain):
+        return run(chain)[0]
+
     def double(values, swap_with, size):
         values = values[None]
         step = 1
         while step < size:
-            values = jnp.concatenate([values, swap_with(values, step)])
+            came = yield swap_with(values, step)
+            values = jnp.concatenate([values, came])
             step *= 2
         return values
 
@@ -119,35 +145,70 @@
         step = 1
         while step < len(entries):
             moved = [k for k in range(len(entries)) if k & step]
-            came = swap_with(jnp.stack([entries[k] for k in moved]), step)
+            came = yield swap_with(jnp.stack([entries[k] for k in moved]), step)
             for i, k in enumerate(moved):
                 entries[k] = came[i]
             step *= 2
         return entries
 
-    def halve(parts, swap_with):
+    def halve(parts, swap_with, kind=bf16):
         parts = list(parts)
         step = len(parts) // 2
         while step > 0:
-            low = jnp.stack([parts[k + step] for k in range(step)]).astype(bf16)
-            came = swap_with(low, step)
+            low = jnp.stack([parts[k + step] for k in range(step)]).astype(kind)
+            came = yield swap_with(low, step)
             parts = [parts[k] + came[k].astype(f32) for k in range(step)]
             step //= 2
         return parts[0]
 
-    def reduce_seq(values):
-        values = values + swap_c(values)
+    def halve_near(parts, swap_with):
+        parts = list(parts)
+        step = 1
+        while len(parts) > 1:
+            low = jnp.stack(parts[1::2]).astype(bf16)
+            came = yield swap_with(low, step)
+            parts = [part + came[i].astype(f32) for i, part in enumerate(parts[0::2])]
+            step *= 2
+        return parts[0]
+
+    def resume(chain, came, done=None):
+        if came is None:
+            return done
+        try:
+            came = chain.send(came)
+        except StopIteration as stop:
+            return stop.value
+        while True:
+            came = yield came
+            try:
+                came = chain.send(came)
+            except StopIteration as stop:
+                return stop.value
+
+    def add_z(values):
         step = 1
         while step < n_z:
-            values = values + swap_z(values, step)
+            came = yield swap_z(values, step)
+            values = values + came
             step *= 2
         return values
 
+    def add_seq(values):
+        came = yield swap_c(values)
+        values = yield from add_z(values + came)
+        return values
+
     def after(value, *others):
         return lax.optimization_barrier((value,) + others)[0]
 
     def join_cores(values):
-        return values[:, 0] + swap_c(values[:, 1].astype(bf16)).astype(f32)
+        low = values[:, 1].astype(bf16)
+        return [
+            values[k, 0] + swap_c(low[k]).astype(f32) for k in range(values.shape[0])
+        ]
+
+    def with_cores(pieces):
+        return jnp.concatenate([part for own in pieces for part in (own, swap_c(own))])
 
     def add_parts(own, parts):
         return tree_sum([own] + [part.astype(f32) for part in parts])
@@ -196,51 +257,77 @@
 
         def trade_cores(zeros, ones):
             pairs = [by_core(zero, one) for zero, one in zip(zeros, ones)]
-            came = swap_c(jnp.stack([other for _, other in pairs]))
+            came = yield swap_c(jnp.stack([other for _, other in pairs]))
             return [by_core(own, came[i]) for i, (own, _) in enumerate(pairs)]
 
         def trade_seq(entries):
-            pairs = trade_cores(entries[0::2], entries[1::2])
+            pairs = yield from trade_cores(entries[0::2], entries[1::2])
             pairs = xor_parts([jnp.stack(pair) for pair in pairs], at_z)
-            pairs = xor_parts(shift(pairs, swap_z), at_z)
+            pairs = xor_parts((yield from shift(pairs, swap_z)), at_z)
             return [pairs[i // 2][i % 2] for i in range(n_s)]
 
         def trade_mlp(entries):
-            pairs = trade_cores(entries[0::2], entries[1::2])
+            pairs = yield from trade_cores(entries[0::2], entries[1::2])
             pairs = xor_parts([jnp.stack(pair) for pair in pairs], at_f)
-            pairs = xor_parts(shift(pairs, swap_f), at_f)
+            pairs = xor_parts((yield from shift(pairs, swap_f)), at_f)
             return [pairs[i // 2][i % 2] for i in range(n_f * CORES)]
 
         width = bias_vector.shape[0]
         modul_low = modul_weight.astype(bf16)
-        modul_rows = double(modul_low, swap_f, n_f).reshape(n_f * rows, 6 * D)
-        small = double(jnp.concatenate([condition.reshape(-1), bias_vector.astype(bf16)]), swap_f, n_f)
-        cond_all = small[:, : images_group * D]
-        cond_all = cond_all.reshape(n_f * images_group, D).astype(f32)
-        bias_rows = jnp.stack(
-            xor_parts([small[k, images_group * D :] for k in range(n_f)], at_f)
-        )
-        bias_placed = (bias_rows.astype(f32)[:, None, :] * pick_s[None, :, None]).reshape(-1)
-
-        tokens_z = jnp.stack(all_z(tokens))
-        tokens_group = jnp.stack([tokens_z, swap_c(tokens_z)], axis=1).reshape(n_s, BLOCK, D)
+        tokens_z = all_z(tokens)
+        tokens_group = with_cores(tokens_z).reshape(n_s, BLOCK, D)
 
         qkv_low = qkv_weight.astype(bf16).reshape(rows, 3, n_s, hd)
-        qkv_mine = trade_seq([qkv_low[:, :, i].reshape(rows, 3 * hd) for i in range(n_s)])
-        qkv_mine = jnp.stack(qkv_mine)
-        qkv_full = jnp.stack(xor_parts(all_f(qkv_mine), at_f)).reshape(D, 3 * hd)
 
         proj_full = lax.all_gather(
             proj_weight.astype(bf16), ("fsdp", "z", "core"), axis=0, tiled=True
         )
 
         cond_float = condition.astype(f32)
-        cond_act = jax.nn.silu(cond_float).astype(bf16).reshape(images_group, n_f, n_s, rows)
-        cond_rows = lax.dynamic_index_in_dim(cond_act, at_s, 2, keepdims=False)
-        cond_rows = jnp.stack(xor_parts([cond_rows[:, k] for k in range(n_f)], at_f), axis=1)
-        modul_part = matmul(cond_rows.reshape(images_group, n_f * rows), modul_rows)
-        modul_part = (modul_part + bias_placed[: 6 * D]).reshape(-1)
-        whole = reduce_seq(jnp.concatenate([modul_part, bias_placed[6 * D :]]))
+
+        def modul_chain():
+            small = yield from double(
+                jnp.concatenate([condition.reshape(-1), bias_vector.astype(bf16)]), swap_f, n_f
+            )
+            cond_all = small[:, : images_group * D].reshape(n_f * images_group, D).astype(f32)
+            all_act = jax.nn.silu(cond_all).astype(bf16)
+            act_cols = lax.dynamic_slice_in_dim(all_act, at_g * rows, rows, axis=1)
+            part = matmul(act_cols, modul_low).reshape(n_f, images_group, 6 * D)
+            due = [part[k] for k in range(n_f)]
+            while len(due) > 1:
+                half = len(due) // 2
+                low = jnp.stack(due[half:])
+                if half == 1:
+                    low = after(low, *tokens_z[1:])
+                came = yield swap_f(low, half)
+                due = [due[k] + came[k] for k in range(half)]
+            part = due[0]
+            bias_rows = xor_parts([small[k, images_group * D :] for k in range(n_f)], at_f)
+            bias_rows = jnp.stack(bias_rows).astype(f32)
+            placed = (bias_rows[:, None, :] * pick_s[None, :, None]).reshape(-1)
+            part = (part + placed[: 6 * D]).reshape(-1)
+            return act_cols, jnp.concatenate([part, placed[6 * D :]])
+
+        widen_low = widen_weight.astype(bf16).reshape(rows, n_f, n_z, CORES, ub)
+        (act_cols, whole), qkv_mine, widen_mine = run(
+            modul_chain(),
+            trade_seq([qkv_low[:, :, i].reshape(rows, 3 * hd) for i in range(n_s)]),
+            trade_mlp(
+                [
+                    widen_low[:, i // CORES, :, i % CORES].reshape(rows, units)
+                    for i in range(n_f * CORES)
+                ]
+            ),
+        )
+        qkv_parts = all_f(jnp.stack(qkv_mine))
+        qkv_full = jnp.stack(xor_parts(qkv_parts, at_f)).reshape(D, 3 * hd)
+        whole = whole + swap_c(whole)
+        near = 1
+        while near < n_z:
+            if 2 * near == n_z:
+                whole = after(whole, *qkv_parts[1:])
+            whole = whole + swap_z(whole, near)
+            near *= 2
         modulation = whole[: images_group * 6 * D].reshape(images_group, 6 * D)
         bias_all = whole[images_group * 6 * D :]
         bias_query = bias_all[:D].reshape(n_s, hd)
@@ -249,24 +336,11 @@
         bias_widen = bias_all[3 * D : 3 * D + FF].reshape(n_f, n_z, CORES, ub)
         bias_narrow = bias_all[3 * D + FF :]
 
-        widen_late = after(widen_weight, qkv_mine)
-        widen_low = widen_late.astype(bf16).reshape(rows, n_f, n_z, CORES, ub)
-        widen_mine = trade_mlp(
-            [
-                widen_low[:, i // CORES, :, i % CORES].reshape(rows, units)
-                for i in range(n_f * CORES)
-            ]
-        )
-        narrow_low = narrow_weight.astype(bf16)
-        hidden = jnp.concatenate(
-            widen_mine + [narrow_low[:, i : i + units] for i in range(0, D, units)]
-        )
-        split = n_f * CORES * rows
-        hidden = lax.all_gather(hidden, "z", axis=0, tiled=False)
-        widen_full = hidden[:, :split].reshape(n_z, n_f, CORES * rows, units)
+        widen_full = lax.all_gather(jnp.concatenate(widen_mine), "z", axis=0, tiled=False)
+        widen_full = widen_full.reshape(n_z, n_f, CORES * rows, units)
         widen_full = widen_full.transpose(1, 0, 2, 3).reshape(D, units)
-        narrow_full = hidden[:, split:].reshape(n_z, D // units, ub, units)
-        narrow_full = narrow_full.transpose(0, 2, 1, 3).reshape(units, D)
+        narrow_late = after(narrow_weight, *widen_mine).astype(bf16)
+        narrow_full = lax.all_gather(narrow_late, "z", axis=0, tiled=True)
 
         own_id = lax.dynamic_index_in_dim(local_ids, at_s, keepdims=False)
         image_pick = (own_id == jnp.arange(images_group, dtype=jnp.int32)).astype(f32)
@@ -300,7 +374,7 @@
 
         def send_blocks(values):
             came = swap_c(values[:, 1])
-            parts = shift([jnp.stack([values[k, 0], came[k]]) for k in range(n_z)], swap_z)
+            parts = [swap_z(jnp.stack([values[k, 0], came[k]]), k) for k in range(n_z)]
             pairs = [by_core(part[0], part[1]) for part in xor_parts(parts, at_z)]
             return jnp.concatenate([part for pair in pairs for part in pair], axis=1)
 
@@ -310,8 +384,11 @@
             own = xor_parts([pair[0] for pair in pairs], at_z)
             other = xor_parts([pair[1] for pair in pairs], at_z)
             came = swap_c(jnp.stack(other))
-            parts = shift([jnp.stack([own[k], came[k]]) for k in range(n_z)], swap_z)
+            parts = [swap_z(jnp.stack([own[k], came[k]]), k) for k in range(n_z)]
             return jnp.stack(parts).reshape(tok_group, hd)
+
+        grad_out = cotangent.astype(f32)
+        d_b_own = (gate_b * grad_out).astype(bf16)
 
         normed_group, _ = normalize(tokens_group.astype(f32))
         h_a = (
@@ -336,6 +413,7 @@
                 bf16
             )
         )
+        attended = after(attended, proj_full)
         att_own = send_blocks(attended.reshape(n_z, CORES, BLOCK, hd))
 
         branch_a = matmul(att_own, proj_full) + bias_proj
@@ -343,14 +421,11 @@
         middle = inputs + gate_a * branch_a
         normed_b, spread_b = normalize(middle)
         h_b_own = (normed_b * (1.0 + scale_b) + shift_b).astype(bf16)
-        grad_out = cotangent.astype(f32)
-        d_b_own = (gate_b * grad_out).astype(bf16)
-
-        d_b_f = double(d_b_own, swap_f, n_f)
-        d_b = jnp.stack([d_b_f, swap_c(d_b_f)], axis=1).reshape(-1, D)
-        d_b = after(d_b, h_b_own)
-        h_b_f = jnp.stack(all_f(h_b_own))
-        h_b = jnp.stack([h_b_f, swap_c(h_b_f)], axis=1).reshape(-1, D)
+
+        d_b_f = after(alone(double(d_b_own, swap_f, n_f)), h_b_own)
+        modul_rows = lax.all_gather(after(modul_low, h_b_own), "fsdp", axis=0, tiled=True)
+        d_b = with_cores([d_b_f[k] for k in range(n_f)])
+        h_b = with_cores(all_f(h_b_own))
         bias_units = lax.dynamic_index_in_dim(bias_widen, at_f, 0, keepdims=False)
         bias_units = lax.dynamic_index_in_dim(bias_units, at_c, 1, keepdims=False).reshape(units)
         widened = matmul(h_b, widen_full) + bias_units
@@ -360,20 +435,22 @@
         d_wide = gelu_pull(d_act)[0].astype(bf16)
         d_hb_part = jnp.einsum("tf,df->td", d_wide, widen_full, preferred_element_type=f32)
         d_hb_f = join_cores(d_hb_part.reshape(n_f, CORES, BLOCK, D))
-        d_hb = add_parts(d_hb_f[0], [swap_f(d_hb_f[k].astype(bf16), k) for k in range(1, n_f)])
-        branch_part = join_cores(matmul(activated, narrow_full).reshape(n_f, CORES, BLOCK, D))
+        d_hb_came = [swap_f(d_hb_f[k].astype(bf16), k) for k in range(1, n_f)]
         grad_narrow = jnp.einsum("tf,td->fd", activated, d_b, preferred_element_type=f32)
+        grad_narrow = after(grad_narrow, *d_hb_f).reshape(n_z, ub, D)
+        narrow_chain = halve_near(
+            [
+                lax.dynamic_index_in_dim(grad_narrow, at_z ^ k, 0, keepdims=False)
+                for k in range(n_z)
+            ],
+            swap_z,
+        )
+        narrow_came = next(narrow_chain)
+        d_hb = add_parts(d_hb_f[0], [after(part, narrow_came) for part in d_hb_came])
+        branch_part = matmul(activated, narrow_full).reshape(n_f, CORES, BLOCK, D)
         grad_widen = jnp.einsum("td,tf->df", h_b, d_wide, preferred_element_type=f32)
-        grad_narrow = grad_narrow.reshape(n_z, ub, D)
-        grad_widen = grad_widen.reshape(n_f, n_z, CORES, rows, units)
-
-        grad_hidden = jnp.concatenate(
-            [grad_widen.transpose(1, 0, 2, 3, 4).reshape(n_z, split, units)]
-            + [grad_narrow[:, :, i : i + units] for i in range(0, D, units)],
-            axis=1,
-        )
-        grad_hidden = after(grad_hidden.astype(bf16), d_hb_f)
-        hidden_low = lax.psum_scatter(grad_hidden, "z", scatter_dimension=0, tiled=False)
+        grad_widen = grad_widen.astype(bf16).reshape(n_f, n_z, CORES, rows, units)
+        grad_widen = grad_widen.transpose(1, 0, 2, 3, 4).reshape(n_z, -1, units)
 
         d_shift_b = jnp.sum(d_hb, axis=0)
         d_scale_b = jnp.sum(d_hb * normed_b, axis=0)
@@ -381,17 +458,35 @@
         d_gate_a = jnp.sum(d_middle * branch_a, axis=0)
         d_a = (gate_a * d_middle).astype(bf16)
         d_att_own = jnp.einsum("te,de->td", d_a, proj_full, preferred_element_type=f32)
-        d_att = by_image(send_heads(d_att_own.astype(bf16)))
-        grad_proj = jnp.einsum("td,te->de", att_own, d_a, preferred_element_type=f32)
+        d_att_own = d_att_own.astype(bf16)
+        d_att = send_heads(d_att_own)
+        grad_proj = jnp.einsum(
+            "td,te->de", att_own, after(d_a, d_att_own), preferred_element_type=f32
+        )
         grad_proj = grad_proj.reshape(n_f, n_z, CORES, rows, D)
         proj_own, proj_other = by_core(grad_proj[:, :, 0], grad_proj[:, :, 1])
+
+        branch_chain = halve(join_cores(after(branch_part, d_hb)), swap_f)
+        branch_came = next(branch_chain)
+
+        def further(chain, came):
+            try:
+                return chain.send(came), None
+            except StopIteration as stop:
+                return None, stop.value
+
+        narrow_came, narrow_sum = further(narrow_chain, narrow_came)
+        if narrow_came is not None:
+            d_att, narrow_came, branch_came = lax.optimization_barrier(
+                (d_att, narrow_came, branch_came)
+            )
+        else:
+            d_att, branch_came = lax.optimization_barrier((d_att, branch_came))
+        branch_came, branch_b = further(branch_chain, branch_came)
+        grad_widen = after(grad_widen, d_att)
+        widen_part = lax.psum_scatter(grad_widen, "z", scatter_dimension=0, tiled=False)
+        d_att = by_image(d_att)
         proj_both = proj_own + swap_c(proj_other.astype(bf16)).astype(f32)
-
-        def mixed(k):
-            part = lax.dynamic_index_in_dim(proj_both, at_f ^ k, 0, keepdims=False)
-            return jnp.concatenate([branch_part[k], part.reshape(n_z * rows, D)])
-
-        mixed_sum = halve([mixed(k) for k in range(n_f)], swap_f)
 
         d_values = jnp.einsum("ihqk,ihqd->ihkd", probs_low, d_att, preferred_element_type=f32)
         d_probs = jnp.einsum("ihqd,ihkd->ihqk", d_att, values, preferred_element_type=f32)
@@ -407,43 +502,50 @@
         d_qkv = jnp.concatenate(
             [by_block(part.astype(bf16)) for part in (d_queries, d_keys, d_values)], axis=1
         )
+        if branch_came is not None:
+            d_qkv, branch_came, proj_both = lax.optimization_barrier(
+                (d_qkv, branch_came, proj_both)
+            )
+        else:
+            d_qkv, proj_both = lax.optimization_barrier((d_qkv, proj_both))
+        proj_chain = halve(
+            [
+                lax.dynamic_index_in_dim(proj_both, at_f ^ k, 0, keepdims=False)
+                for k in range(n_f)
+            ],
+            swap_f,
+        )
         d_ha_part = jnp.einsum("te,de->td", d_qkv, qkv_full, preferred_element_type=f32)
-        mixed_sum = after(mixed_sum, d_ha_part)
-        branch_b = mixed_sum[:BLOCK] + bias_narrow
-        block_output = (middle + gate_b * branch_b).astype(bf16)
-        d_gate_b = jnp.sum(grad_out * branch_b, axis=0)
-        proj_mid = xor_parts(
-            [mixed_sum[i : i + rows] for i in range(BLOCK, BLOCK + n_z * rows, rows)], at_z
-        )
-        proj_sum = halve(proj_mid, swap_z)
-
         d_ha_z = join_cores(d_ha_part.reshape(n_z, CORES, BLOCK, D))
-        d_ha = add_parts(d_ha_z[0], [swap_z(d_ha_z[k].astype(bf16), k) for k in range(1, n_z)])
+        d_ha_low = [d_ha_z[k].astype(bf16) for k in range(1, n_z)]
+        d_ha_came = [swap_z(d_ha_low[k - 1], k) for k in range(1, n_z)]
         grad_qkv = jnp.einsum("td,te->de", h_a, d_qkv, preferred_element_type=f32)
-        grad_qkv = grad_qkv.reshape(n_f, n_s * rows, 3 * hd)
+        grad_qkv = after(grad_qkv.reshape(n_f, n_s * rows, 3 * hd), *d_ha_low)
         grad_qkv = [
             lax.dynamic_index_in_dim(grad_qkv, at_f ^ k, 0, keepdims=False) for k in range(n_f)
         ]
-        qkv_mid = halve(grad_qkv, swap_f)
-        qkv_sum = trade_seq([qkv_mid[i : i + rows] for i in range(0, n_s * rows, rows)])
-        qkv_sum = jnp.stack(qkv_sum).reshape(n_s, rows, 3, hd)
-        qkv_sum = qkv_sum.transpose(1, 2, 0, 3).reshape(rows, 3 * D)
+        widen_part = after(widen_part, *d_ha_low).reshape(n_f * CORES, rows, units)
+
+        branch_b, narrow_sum, proj_mid, qkv_mid, widen_back = run(
+            resume(branch_chain, branch_came, branch_b),
+            resume(narrow_chain, narrow_came, narrow_sum),
+            proj_chain,
+            halve(grad_qkv, swap_f),
+            trade_mlp([widen_part[i] for i in range(n_f * CORES)]),
+        )
+        d_ha_came = [after(part, branch_b, proj_mid, qkv_mid, *widen_back) for part in d_ha_came]
+        d_ha = add_parts(d_ha_z[0], d_ha_came)
+        widen_sum = jnp.stack(widen_back).reshape(n_f, CORES, rows, n_z, ub)
+        widen_sum = widen_sum.transpose(2, 0, 3, 1, 4).reshape(rows, FF).astype(f32)
+        branch_b = branch_b + bias_narrow
+        block_output = (middle + gate_b * branch_b).astype(bf16)
+        d_gate_b = jnp.sum(grad_out * branch_b, axis=0)
         normed_a, spread_a = normalize(inputs)
         d_shift_a = jnp.sum(d_ha, axis=0)
         d_scale_a = jnp.sum(d_ha * normed_a, axis=0)
         tokens_grad = (
             d_middle + norm_back(d_ha * (1.0 + scale_a), normed_a, spread_a)
         ).astype(bf16)
-
-        hidden_sum = after(hidden_low, d_ha).astype(f32)
-        narrow_sum = jnp.concatenate(
-            [hidden_sum[i : i + ub] for i in range(split, hidden_sum.shape[0], ub)], axis=1
-        )
-        widen_back = trade_mlp(
-            [hidden_sum[i : i + rows].astype(bf16) for i in range(0, split, rows)]
-        )
-        widen_sum = jnp.stack(widen_back).reshape(n_f, CORES, rows, n_z, ub)
-        widen_sum = widen_sum.transpose(2, 0, 3, 1, 4).reshape(rows, FF).astype(f32)
 
         units_sum = column_sums(d_wide).reshape(n_z, ub)
         bias_g_widen = (
@@ -462,19 +564,8 @@
             bias_g_widen,
             column_sums(d_b_own),
         ]
-        sums = reduce_seq(jnp.concatenate(pieces))
+        sums = alone(add_seq(jnp.concatenate(pieces)))
         cut = images_group * 6 * D
-        whole = double(sums, swap_f, n_f)
-        d_modulation = whole[:, :cut].reshape(n_f * images_group, 6 * D)
-        all_act = jax.nn.silu(cond_all).astype(bf16).astype(f32)
-        act_cols = lax.dynamic_slice_in_dim(all_act, at_g * rows, rows, axis=1)
-        modul_sum = sum(
-            act_cols[i][:, None] * d_modulation[i][None, :] for i in range(n_f * images_group)
-        )
-        bias_grad = jnp.concatenate(
-            [jnp.sum(d_modulation, axis=0), jnp.sum(whole[:, cut:], axis=0)]
-        )
-        bias_sum = lax.dynamic_slice_in_dim(bias_grad, at_g * width, width)
         d_own = sums[:cut].reshape(images_group, 6 * D)
         d_cond_rows = jnp.einsum(
             "im,dm->id",
@@ -483,14 +574,37 @@
             precision=lax.Precision.HIGHEST,
             preferred_element_type=f32,
         )
-        d_cond_z = double(d_cond_rows, swap_z, n_z)
-        d_cond_z = jnp.stack(xor_parts([d_cond_z[k] for k in range(n_z)], at_z))
-        d_cond = jnp.stack(by_core(d_cond_z, swap_c(d_cond_z)), axis=1)
-        d_cond = d_cond.reshape(n_s, images_group, n_f, rows).transpose(2, 1, 0, 3)
-        d_cond = jnp.stack(xor_parts([d_cond[k] for k in range(n_f)], at_f))
-        d_cond_act = d_cond.transpose(1, 0, 2, 3).reshape(images_group, D)
+
+        def cond_chain():
+            part = yield from double(d_cond_rows, swap_z, n_z)
+            part = jnp.stack(xor_parts([part[k] for k in range(n_z)], at_z))
+            came = yield swap_c(part)
+            return jnp.stack(by_core(part, came), axis=1)
+
+        qkv_mid = after(qkv_mid, sums)
+        proj_mid = after(proj_mid, sums)
+        whole, d_cond, proj_sum, qkv_sum = run(
+            double(sums, swap_f, n_f),
+            cond_chain(),
+            halve(xor_parts([proj_mid[k] for k in range(n_z)], at_z), swap_z),
+            trade_seq([qkv_mid[i : i + rows] for i in range(0, n_s * rows, rows)]),
+        )
+        qkv_sum = jnp.stack(qkv_sum).reshape(n_s, rows, 3, hd)
+        qkv_sum = qkv_sum.transpose(1, 2, 0, 3).reshape(rows, 3 * D)
+        d_cond = d_cond.reshape(n_s, images_group, n_f, rows)
+        d_cond_act = d_cond.transpose(1, 2, 0, 3).reshape(images_group, D)
         silu_pull = jax.vjp(jax.nn.silu, cond_float)[1]
         condition_grad = silu_pull(d_cond_act)[0]
+
+        d_modulation = whole[:, :cut].reshape(n_f * images_group, 6 * D)
+        act_wide = act_cols.astype(f32)
+        modul_sum = sum(
+            act_wide[i][:, None] * d_modulation[i][None, :] for i in range(n_f * images_group)
+        )
+        bias_grad = jnp.concatenate(
+            [jnp.sum(d_modulation, axis=0), jnp.sum(whole[:, cut:], axis=0)]
+        )
+        bias_sum = lax.dynamic_slice_in_dim(bias_grad, at_g * width, width)
 
         rate_wide = 2.0 / math.sqrt(D)
         modul_new = adam_step(modul_weight, modul_sum, modul_mean, modul_square, rate_wide)

time: 444 us -> 383 us (0.86)
  waiting for transfers between devices: 166 us -> 139 us
  local copies, waits for them, and re-layouts: 61.9 us -> 37.9 us
  other arithmetic: 83.9 us -> 66.1 us
  starting transfers between devices: 69.3 us -> 75.3 us
    ppermute x63 -> x87, waiting for transfers between devices: 166 us -> 130 us  [swap(): return lax.ppermute(values, axis, [(i, i ^ k) for i in range(size)])]
    another operation x50 -> x39, other arithmetic: 26.3 us -> 6.8 us  [the longest x6 1.81 us: trade_cores(): came = (yield swap_c(jnp.stack([other for _, other in pairs])))]
    all_gather x1 -> x3, waiting for transfers between devices: 0.01 us -> 8.49 us  [the longest x1 6.51 us: shards(): narrow_full = lax.all_gather(narrow_late, 'z', axis=0, tiled=True)]
    ppermute x63 -> x87, starting transfers between devices: 68.7 us -> 74.9 us  [swap(): return lax.ppermute(values, axis, [(i, i ^ k) for i in range(size)])]
    slice x9 -> x5, local copies, waits for them, and re-layouts: 6.8 us -> 0.81 us  [the longest x1 0.74 us: modul_chain(): due = [due[k] + came[k] for k in range(half)]]
    convert_element_type x1, other arithmetic: 2.75 us -> 7.33 us  [shards(): d_scores = (probs * (d_probs - row_term)).astype(bf16)]
    unnamed x216 -> x259, local copies, waits for them, and re-layouts: 20.4 us -> 17.1 us
    convert_element_type x12 -> x14, other arithmetic: 9.61 us -> 9.61 us  [the longest x4 4.46 us: halve(): low = jnp.stack([parts[k + step] for k in range(step)]).astype(kind)]
  transfers between devices with their start and end apart: 66 -> 92, of which waited for: 38 -> 41; matrix products, arithmetic and copies ran while one was open for 37% -> 32% of each run, Pallas kernels for 0% -> 0%
where the time goes in v3:
time: 383 us; the launch traced here: 378 us
  waiting for transfers between devices  139 us (36%)
  starting transfers between devices  75.3 us (20%)
  other arithmetic  66.1 us (17%)
  matrix products  42.1 us (11%)
  local copies, waits for them, and re-layouts  37.9 us (10%)
  between operations  17.5 us (5%)
    ppermute x87, waiting for transfers between devices, swap(): return lax.ppermute(values, axis, [(i, i ^ k) for i in range(size)])  130 us
    ppermute x87, starting transfers between devices, swap(): return lax.ppermute(values, axis, [(i, i ^ k) for i in range(size)])  74.9 us
    unnamed x259, local copies, waits for them, and re-layouts  17.1 us
    sub x6, other arithmetic, adam_step(): weight - rate * (first / fix_first / (jnp.sqrt(second / fix_second) + ada...  10.9 us
  transfers between devices with their start and end apart: 92, of which 41 were waited for; matrix products, arithmetic and copies ran while one was open for 32% of the time, Pallas kernels for 0%

profile of v3, /device:TPU:0, one launch (start us, length us, event | category | flops | bytes accessed | tf_op | source)
XLA Modules:
  0.0 377.6 jit_solution(2171514353129423274)
XLA Ops:
  10.7 3.0 collective-permute-start
  23.2 2.7 collective-permute-start.7
  28.3 3.9 %collective-permute-done.6 = f32[2,1,6144]{2,1,0:T(1,128)S(1)} collective-permute-done((f32[2,1,6144]{2,1,0:T(1,128)S(1)}, f32[2,1,6144]{2,1,0:T(1,128)S(1)}, u32[]{:S(2)}, u32[]{:S(2)}) %collective-permute-start.6) | collective-permute-done | bytes 49184 | tf_op jit(solution)/shard_map/ppermute | solution.py:92
  35.5 2.8 collective-permute-start.9
  40.2 5.2 %collective-permute-done.11 = bf16[128,1024]{1,0:T(8,128)(2,1)S(1)} collective-permute-done((bf16[128,1024]{1,0:T(8,128)(2,1)S(1)}, bf16[128,1024]{1,0:T(8,128)(2,1)S(1)}, u32[]{:S(2)}, u32[]{:S(2)}) %collective-permute-start.11) | collective-permute-done | bytes 262176 | tf_op jit(solution)/shard_map/ppermute | solution.py:92
  45.4 11.0 %collective-permute-done.10 = bf16[128,1024]{1,0:T(8,128)(2,1)} collective-permute-done((bf16[128,1024]{1,0:T(8,128)(2,1)S(1)}, bf16[128,1024]{1,0:T(8,128)(2,1)}, u32[]{:S(2)}, u32[]{:S(2)}) %collective-permute-start.10) | collective-permute-done | bytes 262176 | tf_op jit(solution)/shard_map/ppermute | solution.py:92
  70.8 3.3 collective-permute-done.14
  75.9 4.8 %collective-permute-done.16 = bf16[8,32,384]{2,1,0:T(8,128)(2,1)S(1)} collective-permute-done((bf16[8,32,384]{2,1,0:T(8,128)(2,1)S(1)}, bf16[8,32,384]{2,1,0:T(8,128)(2,1)S(1)}, u32[]{:S(2)}, u32[]{:S(2)}) %collective-permute-start.16) | collective-permute-done | bytes 196640 | tf_op jit(solution)/shard_map/ppermute | solution.py:92
  81.0 6.3 %collective-permute-done.18 = f32[14336]{0:T(1024)S(1)} collective-permute-done((f32[14336]{0:T(1024)S(1)}, f32[14336]{0:T(1024)S(1)}, u32[]{:S(2)}, u32[]{:S(2)}) %collective-permute-start.18) | collective-permute-done | bytes 57376 | tf_op jit(solution)/shard_map/ppermute | solution.py:92
  107.6 5.0 %collective-permute-done.35 = bf16[2,128,1024]{2,1,0:T(8,128)(2,1)} collective-permute-done((bf16[2,128,1024]{2,1,0:T(8,128)(2,1)}, bf16[2,128,1024]{2,1,0:T(8,128)(2,1)}, u32[]{:S(2)}, u32[]{:S(2)}) %collective-permute-start.35) | collective-permute-done | bytes 524320 | tf_op jit(solution)/shard_map/ppermute | solution.py:92
  113.8 4.0 %collective-permute-done.25 = bf16[2,128,128]{2,1,0:T(8,128)(2,1)S(1)} collective-permute-done((bf16[2,128,128]{2,1,0:T(8,128)(2,1)S(1)}, bf16[2,128,128]{2,1,0:T(8,128)(2,1)S(1)}, u32[]{:S(2)}, u32[]{:S(2)}) %collective-permute-start.25) | collective-permute-done | bytes 65568 | tf_op jit(solution)/shard_map/ppermute | solution.py:92
  132.4 2.9 collective-permute-done.32
  135.3 4.4 %collective-permute-done.30 = bf16[128,1024]{1,0:T(8,128)(2,1)S(1)} collective-permute-done((bf16[128,1024]{1,0:T(8,128)(2,1)S(1)}, bf16[128,1024]{1,0:T(8,128)(2,1)S(1)}, u32[]{:S(2)}, u32[]{:S(2)}) %collective-permute-start.30) | collective-permute-done | bytes 262176 | tf_op jit(solution)/shard_map/ppermute | solution.py:92
  143.1 3.0 fusion.138
  146.1 6.5 %all-gather.8.cloned.1.call-done = bf16[512,1024]{1,0:T(8,128)(2,1)} async-done(((bf16[128,1024]{1,0:T(8,128)(2,1)}), bf16[512,1024]{1,0:T(8,128)(2,1)}) %all-gather.8.cloned.1.call-update) | async-done | bytes 1048592 | tf_op jit(solution)/shard_map/all_gather | solution.py:343
  152.6 5.2 %convert_reduce_fusion.1 = (f32[512]{0:T(512)S(1)}, bf16[1024,512]{1,0:T(8,128)(2,1)S(1)}) fusion(f32[1024,512]{1,0:T(8,128)} %fusion.138, f32[512]{0:T(512)S(1)} %bitcast.821, bf16[1024,1024]{1,0:T(8,128)(2,1)} %copy-done.77, bf16[512,1024]{1,0:T(8,128)(2,1)} %all-gather.8.cloned.1.call-done), kind=kOutput, calls=%fused_computation.26 | convolution fusion | flops 1085799936 | bytes 6295552 | tf_op jit(solution)/shard_map/td,fd->tf/dot_general | solution.py:434
  171.9 6.7 %collective-permute-done.47 = bf16[128,1024]{1,0:T(8,128)(2,1)S(1)} collective-permute-done((bf16[128,1024]{1,0:T(8,128)(2,1)S(1)}, bf16[128,1024]{1,0:T(8,128)(2,1)S(1)}, u32[]{:S(2)}, u32[]{:S(2)}) %collective-permute-start.47) | collective-permute-done | bytes 262176 | tf_op jit(solution)/shard_map/ppermute | solution.py:92
  198.1 3.5 collective-permute-done.51
  202.3 2.9 collective-permute-done.56
  211.1 4.0 %copy.188 = bf16[1024,1024]{1,0:T(8,128)(2,1)} copy(bf16[1024,1024]{0,1:T(8,128)(2,1)} %fusion.109) | data formatting | bytes 4194304 | tf_op jit(solution)/shard_map/td,te->de/dot_general | solution.py:522
  220.0 6.4 %multiply_reduce_fusion = (f32[2,1024]{1,0:T(2,128)S(1)}, f32[2,1024,1024]{1,2,0:T(8,128)}) fusion(f32[2,1024,1024]{1,2,0:T(8,128)} %copy-done, f32[2,1024]{1,0:T(2,128)S(1)} %log_add_fusion, bf16[2,1024,64]{1,2,0:T(8,128)(2,1)S(1)} %bitcast.717, bf16[2,1024,64]{1,2,0:T(8,128)(2,1)S(1)} %bitcast.720), kind=kOutput, calls=%fused_computation.1 | convolution fusion | flops 276822016 | bytes 17317888 | tf_op jit(solution)/shard_map/ihqd,ihkd->ihqk/dot_general | solution.py:492
  226.5 5.0 %convolution_convert_fusion.2 = bf16[2,1024,64]{1,2,0:T(8,128)(2,1)S(1)} fusion(bf16[2,1024,64]{1,2,0:T(8,128)(2,1)S(1)} %bitcast.718, f32[2,1024,1024]{1,2,0:T(8,128)} %copy-done, f32[2,1024]{1,0:T(2,128)S(1)} %log_add_fusion), kind=kOutput, calls=%fused_computation.35 | convolution fusion | flops 274857984 | bytes 8921088 | tf_op jit(solution)/shard_map/ihqk,ihqd->ihkd/dot_general | solution.py:491
  235.1 7.3 %multiply_convert_fusion = bf16[2,1024,1024]{1,2,0:T(8,128)(2,1)S(1)} fusion(f32[2,1024,1024]{1,2,0:T(8,128)} %get-tuple-element.429, f32[2,1024,1024]{1,2,0:T(8,128)} %copy-done, f32[2,1024]{1,0:T(2,128)S(1)} %get-tuple-element.428, f32[2,1024]{1,0:T(2,128)S(1)} %log_add_fusion), kind=kLoop, calls=%fused_computation | loop fusion | flops 10485760 | bytes 20987904 | tf_op jit(solution)/shard_map/convert_element_type | solution.py:494
  244.6 3.6 fusion.14
  248.5 3.1 bitcast_add_fusion
  265.6 10.0 %collective-permute-done.63 = bf16[2,4,32,1024]{3,2,1,0:T(8,128)(2,1)S(1)} collective-permute-done((bf16[2,4,32,1024]{3,2,1,0:T(8,128)(2,1)}, bf16[2,4,32,1024]{3,2,1,0:T(8,128)(2,1)S(1)}, u32[]{:S(2)}, u32[]{:S(2)}) %collective-permute-start.63) | collective-permute-done | bytes 524320 | tf_op jit(solution)/shard_map/ppermute | solution.py:92
  275.6 8.2 %collective-permute-done.66 = bf16[2,256,384]{2,1,0:T(8,128)(2,1)} collective-permute-done((bf16[2,256,384]{2,1,0:T(8,128)(2,1)S(1)}, bf16[2,256,384]{2,1,0:T(8,128)(2,1)}, u32[]{:S(2)}, u32[]{:S(2)}) %collective-permute-start.66) | collective-permute-done | bytes 393248 | tf_op jit(solution)/shard_map/ppermute | solution.py:92
  289.4 11.4 %collective-permute-done.70 = bf16[2,2,32,512]{3,2,1,0:T(8,128)(2,1)S(1)} collective-permute-done((bf16[2,2,32,512]{3,2,1,0:T(8,128)(2,1)S(1)}, bf16[2,2,32,512]{3,2,1,0:T(8,128)(2,1)S(1)}, u32[]{:S(2)}, u32[]{:S(2)}) %collective-permute-start.70) | collective-permute-done | bytes 131104 | tf_op jit(solution)/shard_map/ppermute | solution.py:92
  307.1 4.8 %collective-permute-done.73 = bf16[128,1024]{1,0:T(8,128)(2,1)S(1)} collective-permute-done((bf16[128,1024]{1,0:T(8,128)(2,1)S(1)}, bf16[128,1024]{1,0:T(8,128)(2,1)S(1)}, u32[]{:S(2)}, u32[]{:S(2)}) %collective-permute-start.73) | collective-permute-done | bytes 262176 | tf_op jit(solution)/shard_map/ppermute | solution.py:92
  331.3 2.7 fusion.140
  358.2 3.2 multiply_subtract_fusion
  362.2 5.3 %collective-permute-done.86 = f32[2,2,32,384]{3,2,1,0:T(8,128)S(1)} collective-permute-done((f32[2,2,32,384]{3,2,1,0:T(8,128)}, f32[2,2,32,384]{3,2,1,0:T(8,128)S(1)}, u32[]{:S(2)}, u32[]{:S(2)}) %collective-permute-start.86) | collective-permute-done | bytes 196640 | tf_op jit(solution)/shard_map/ppermute | solution.py:92
  (695 shorter events, 198.0 us)
Async XLA Ops:
  7.2 92.6 %all-gather.6.cloned.1.call-start = ((), (), s32[]{:S(2)}) async-start(), calls=%async_computation.1 | async-start | bytes 2162688 | tf_op jit(solution)/shard_map/all_gather | solution.py:282
  21.6 102.0 %all-gather.12.cloned.1.call-start = ((), (), s32[]{:S(2)}) async-start(), calls=%async_computation.5 | async-start | bytes 1310720 | tf_op jit(solution)/shard_map/all_gather | solution.py:339
  33.7 118.9 %all-gather.8.cloned.1.call-start = ((), (), s32[]{:S(2)}) async-start(), calls=%async_computation.2 | async-start | bytes 1310720 | tf_op jit(solution)/shard_map/all_gather | solution.py:343
  33.9 22.5 %collective-permute-start.10 = (bf16[128,1024]{1,0:T(8,128)(2,1)S(1)}, bf16[128,1024]{1,0:T(8,128)(2,1)}, u32[]{:S(2)}, u32[]{:S(2)}) collective-permute-start(bf16[128,1024]{1,0:T(8,128)(2,1)S(1)} %copy-done.9), channel_id=1, source_target_pairs={{0,4},{2,6},{4,0},{6,2},{1,5},{3,7},{5,1},{7,3},{8,12},{10,14},{12... | collective-permute-start | bytes 786440 | tf_op jit(solution)/shard_map/ppermute | solution.py:92
  35.5 21.0 %collective-permute-start.9 = (bf16[128,1024]{1,0:T(8,128)(2,1)S(1)}, bf16[128,1024]{1,0:T(8,128)(2,1)}, u32[]{:S(2)}, u32[]{:S(2)}) collective-permute-start(bf16[128,1024]{1,0:T(8,128)(2,1)S(1)} %copy-done.9), channel_id=1, source_target_pairs={{0,2},{2,0},{4,6},{6,4},{1,3},{3,1},{5,7},{7,5},{8,10},{10,8},{12,... | collective-permute-start | bytes 786440 | tf_op jit(solution)/shard_map/ppermute | solution.py:92
  38.2 18.7 %collective-permute-start.19 = (bf16[128,1024]{1,0:T(8,128)(2,1)S(1)}, bf16[128,1024]{1,0:T(8,128)(2,1)}, u32[]{:S(2)}, u32[]{:S(2)}) collective-permute-start(bf16[128,1024]{1,0:T(8,128)(2,1)S(1)} %copy-done.9), channel_id=1, source_target_pairs={{0,1},{1,0},{2,3},{3,2},{4,5},{5,4},{6,7},{7,6},{8,9},{9,8},{10,11... | collective-permute-start | bytes 786440 | tf_op jit(solution)/shard_map/ppermute | solution.py:92
  39.0 225.2 %reduce-scatter.2.cloned.1.call-start = ((), (), s32[]{:S(2)}) async-start(), calls=%async_computation.3 | async-start | bytes 1310720 | tf_op jit(solution)/shard_map/reduce_scatter | solution.py:487
  45.4 24.3 %collective-permute-start.22 = (bf16[128,1024]{1,0:T(8,128)(2,1)S(1)}, bf16[128,1024]{1,0:T(8,128)(2,1)S(1)}, u32[]{:S(2)}, u32[]{:S(2)}) collective-permute-start(bf16[128,1024]{1,0:T(8,128)(2,1)S(1)} %collective-permute-done.11), channel_id=1, source_target_pairs={{0,1},{1,0},{2,3},{3,2},{4,5},{5,4},{6,7},{7,6},{8,9},{9,8},{10,11... | collective-permute-start | bytes 786440 | tf_op jit(solution)/shard_map/ppermute | solution.py:92
  56.4 13.2 %collective-permute-start.21 = (bf16[128,1024]{1,0:T(8,128)(2,1)}, bf16[128,1024]{1,0:T(8,128)(2,1)S(1)}, u32[]{:S(2)}, u32[]{:S(2)}) collective-permute-start(bf16[128,1024]{1,0:T(8,128)(2,1)} %collective-permute-done.10), channel_id=1, source_target_pairs={{0,1},{1,0},{2,3},{3,2},{4,5},{5,4},{6,7},{7,6},{8,9},{9,8},{10,11... | collective-permute-start | bytes 786440 | tf_op jit(solution)/shard_map/ppermute | solution.py:92
  66.8 13.9 %collective-permute-start.16 = (bf16[8,32,384]{2,1,0:T(8,128)(2,1)S(1)}, bf16[8,32,384]{2,1,0:T(8,128)(2,1)S(1)}, u32[]{:S(2)}, u32[]{:S(2)}) collective-permute-start(bf16[8,32,384]{2,1,0:T(8,128)(2,1)S(1)} %pad_maximum_fusion.9), channel_id=1, source_target_pairs={{0,16},{8,24},{16,0},{24,8},{1,17},{9,25},{17,1},{25,9},{2,18},{10... | collective-permute-start | bytes 589832 | tf_op jit(solution)/shard_map/ppermute | solution.py:92
  67.9 12.8 %collective-permute-start.15 = (bf16[8,32,384]{2,1,0:T(8,128)(2,1)S(1)}, bf16[8,32,384]{2,1,0:T(8,128)(2,1)S(1)}, u32[]{:S(2)}, u32[]{:S(2)}) collective-permute-start(bf16[8,32,384]{2,1,0:T(8,128)(2,1)S(1)} %pad_maximum_fusion.9), channel_id=1, source_target_pairs={{0,8},{8,0},{16,24},{24,16},{1,9},{9,1},{17,25},{25,17},{2,10},{10... | collective-permute-start | bytes 589832 | tf_op jit(solution)/shard_map/ppermute | solution.py:92
  98.7 13.8 %collective-permute-start.35 = (bf16[2,128,1024]{2,1,0:T(8,128)(2,1)}, bf16[2,128,1024]{2,1,0:T(8,128)(2,1)}, u32[]{:S(2)}, u32[]{:S(2)}) collective-permute-start(bf16[2,128,1024]{2,1,0:T(8,128)(2,1)} %pad_maximum_fusion.3), channel_id=1, source_target_pairs={{0,16},{8,24},{16,0},{24,8},{1,17},{9,25},{17,1},{25,9},{2,18},{10... | collective-permute-start | bytes 1572872 | tf_op jit(solution)/shard_map/ppermute | solution.py:92
  105.2 12.6 %collective-permute-start.25 = (bf16[2,128,128]{2,1,0:T(8,128)(2,1)S(1)}, bf16[2,128,128]{2,1,0:T(8,128)(2,1)S(1)}, u32[]{:S(2)}, u32[]{:S(2)}) collective-permute-start(bf16[2,128,128]{2,1,0:T(8,128)(2,1)S(1)} %pad_maximum_fusion.36), channel_id=1, source_target_pairs={{0,4},{2,6},{4,0},{6,2},{1,5},{3,7},{5,1},{7,3},{8,12},{10,14},{12... | collective-permute-start | bytes 196616 | tf_op jit(solution)/shard_map/ppermute | solution.py:92
  105.3 12.6 %collective-permute-start.26 = (bf16[2,128,128]{2,1,0:T(8,128)(2,1)S(1)}, bf16[2,128,128]{2,1,0:T(8,128)(2,1)S(1)}, u32[]{:S(2)}, u32[]{:S(2)}) collective-permute-start(bf16[2,128,128]{2,1,0:T(8,128)(2,1)S(1)} %pad_maximum_fusion.37), channel_id=1, source_target_pairs={{0,2},{2,0},{4,6},{6,4},{1,3},{3,1},{5,7},{7,5},{8,10},{10,8},{12,... | collective-permute-start | bytes 196616 | tf_op jit(solution)/shard_map/ppermute | solution.py:92
  162.7 15.9 %collective-permute-start.45 = (bf16[2,128,1024]{2,1,0:T(8,128)(2,1)S(1)}, bf16[2,128,1024]{2,1,0:T(8,128)(2,1)S(1)}, u32[]{:S(2)}, u32[]{:S(2)}) collective-permute-start(bf16[2,128,1024]{2,1,0:T(8,128)(2,1)S(1)} %pad_maximum_fusion.4), channel_id=1, source_target_pairs={{0,2},{2,0},{4,6},{6,4},{1,3},{3,1},{5,7},{7,5},{8,10},{10,8},{12,... | collective-permute-start | bytes 1572872 | tf_op jit(solution)/shard_map/ppermute | solution.py:92
  166.9 13.5 %collective-permute-start.46 = (bf16[128,1024]{1,0:T(8,128)(2,1)S(1)}, bf16[128,1024]{1,0:T(8,128)(2,1)S(1)}, u32[]{:S(2)}, u32[]{:S(2)}) collective-permute-start(bf16[128,1024]{1,0:T(8,128)(2,1)S(1)} %get-tuple-element.194), channel_id=1, source_target_pairs={{0,16},{8,24},{16,0},{24,8},{1,17},{9,25},{17,1},{25,9},{2,18},{10... | collective-permute-start | bytes 786440 | tf_op jit(solution)/shard_map/ppermute | solution.py:92
  182.6 19.6 %collective-permute-start.53 = (bf16[1,128,1024]{2,1,0:T(8,128)(2,1)S(1)}, bf16[1,128,1024]{2,1,0:T(8,128)(2,1)S(1)}, u32[]{:S(2)}, u32[]{:S(2)}) collective-permute-start(bf16[1,128,1024]{2,1,0:T(8,128)(2,1)S(1)} %add_convert_fusion.3), channel_id=1, source_target_pairs={{0,4},{2,6},{4,0},{6,2},{1,5},{3,7},{5,1},{7,3},{8,12},{10,14},{12... | collective-permute-start | bytes 786440 | tf_op jit(solution)/shard_map/ppermute | solution.py:92
  190.9 14.3 %collective-permute-start.56 = (bf16[2,128,1024]{2,1,0:T(8,128)(2,1)S(1)}, bf16[2,128,1024]{2,1,0:T(8,128)(2,1)S(1)}, u32[]{:S(2)}, u32[]{:S(2)}) collective-permute-start(bf16[2,128,1024]{2,1,0:T(8,128)(2,1)S(1)} %pad_maximum_fusion.5), channel_id=1, source_target_pairs={{0,16},{8,24},{16,0},{24,8},{1,17},{9,25},{17,1},{25,9},{2,18},{10... | collective-permute-start | bytes 1572872 | tf_op jit(solution)/shard_map/ppermute | solution.py:92
  206.0 125.3 %all-gather.10.cloned.1.call-start = ((), (), s32[]{:S(2)}) async-start(), calls=%async_computation.4 | async-start | bytes 1966080 | tf_op jit(solution)/shard_map/all_gather | solution.py:426
  216.3 43.4 %collective-permute-start.48 = (bf16[128,1024]{1,0:T(8,128)(2,1)}, bf16[128,1024]{1,0:T(8,128)(2,1)}, u32[]{:S(2)}, u32[]{:S(2)}) collective-permute-start(bf16[128,1024]{1,0:T(8,128)(2,1)} %get-tuple-element.203), channel_id=1, source_target_pairs={{0,1},{1,0},{2,3},{3,2},{4,5},{5,4},{6,7},{7,6},{8,9},{9,8},{10,11... | collective-permute-start | bytes 786440 | tf_op jit(solution)/shard_map/ppermute | solution.py:92
  216.3 15.3 %collective-permute-start.57 = (bf16[128,1024]{1,0:T(8,128)(2,1)}, bf16[128,1024]{1,0:T(8,128)(2,1)S(1)}, u32[]{:S(2)}, u32[]{:S(2)}) collective-permute-start(bf16[128,1024]{1,0:T(8,128)(2,1)} %get-tuple-element.204), channel_id=1, source_target_pairs={{0,1},{1,0},{2,3},{3,2},{4,5},{5,4},{6,7},{7,6},{8,9},{9,8},{10,11... | collective-permute-start | bytes 786440 | tf_op jit(solution)/shard_map/ppermute | solution.py:92
  219.8 28.7 %collective-permute-start.59 = (bf16[4,4,32,1024]{3,2,1,0:T(8,128)(2,1)S(1)}, bf16[4,4,32,1024]{3,2,1,0:T(8,128)(2,1)}, u32[]{:S(2)}, u32[]{:S(2)}) collective-permute-start(bf16[4,4,32,1024]{3,2,1,0:T(8,128)(2,1)S(1)} %fusion.16), channel_id=1, source_target_pairs={{0,1},{1,0},{2,3},{3,2},{4,5},{5,4},{6,7},{7,6},{8,9},{9,8},{10,11... | collective-permute-start | bytes 3145736 | tf_op jit(solution)/shard_map/ppermute | solution.py:92
  233.5 18.1 %collective-permute-start.58 = (bf16[1,128,1024]{2,1,0:T(8,128)(2,1)}, bf16[1,128,1024]{2,1,0:T(8,128)(2,1)}, u32[]{:S(2)}, u32[]{:S(2)}) collective-permute-start(bf16[1,128,1024]{2,1,0:T(8,128)(2,1)} %fusion.59), channel_id=1, source_target_pairs={{0,8},{8,0},{16,24},{24,16},{1,9},{9,1},{17,25},{25,17},{2,10},{10... | collective-permute-start | bytes 786440 | tf_op jit(solution)/shard_map/ppermute | solution.py:92
  252.6 23.0 %collective-permute-start.63 = (bf16[2,4,32,1024]{3,2,1,0:T(8,128)(2,1)}, bf16[2,4,32,1024]{3,2,1,0:T(8,128)(2,1)S(1)}, u32[]{:S(2)}, u32[]{:S(2)}) collective-permute-start(bf16[2,4,32,1024]{3,2,1,0:T(8,128)(2,1)} %pad_maximum_fusion.6), channel_id=1, source_target_pairs={{0,16},{8,24},{16,0},{24,8},{1,17},{9,25},{17,1},{25,9},{2,18},{10... | collective-permute-start | bytes 1572872 | tf_op jit(solution)/shard_map/ppermute | solution.py:92
  256.1 57.8 %collective-permute-start.60 = (bf16[128,1024]{1,0:T(8,128)(2,1)}, bf16[128,1024]{1,0:T(8,128)(2,1)}, u32[]{:S(2)}, u32[]{:S(2)}) collective-permute-start(bf16[128,1024]{1,0:T(8,128)(2,1)} %get-tuple-element.197), channel_id=1, source_target_pairs={{0,1},{1,0},{2,3},{3,2},{4,5},{5,4},{6,7},{7,6},{8,9},{9,8},{10,11... | collective-permute-start | bytes 786440 | tf_op jit(solution)/shard_map/ppermute | solution.py:92
  263.4 20.3 %collective-permute-start.66 = (bf16[2,256,384]{2,1,0:T(8,128)(2,1)S(1)}, bf16[2,256,384]{2,1,0:T(8,128)(2,1)}, u32[]{:S(2)}, u32[]{:S(2)}) collective-permute-start(bf16[2,256,384]{2,1,0:T(8,128)(2,1)S(1)} %pad_maximum_fusion.7), channel_id=1, source_target_pairs={{0,16},{8,24},{16,0},{24,8},{1,17},{9,25},{17,1},{25,9},{2,18},{10... | collective-permute-start | bytes 1179656 | tf_op jit(solution)/shard_map/ppermute | solution.py:92
  265.3 18.5 %collective-permute-start.67 = (bf16[4,32,512]{2,1,0:T(8,128)(2,1)S(1)}, bf16[4,32,512]{2,1,0:T(8,128)(2,1)S(1)}, u32[]{:S(2)}, u32[]{:S(2)}) collective-permute-start(bf16[4,32,512]{2,1,0:T(8,128)(2,1)S(1)} %pad_maximum_fusion.19), channel_id=1, source_target_pairs={{0,1},{1,0},{2,3},{3,2},{4,5},{5,4},{6,7},{7,6},{8,9},{9,8},{10,11... | collective-permute-start | bytes 393224 | tf_op jit(solution)/shard_map/ppermute | solution.py:92
  285.8 16.1 %collective-permute-start.69 = (bf16[1,256,384]{2,1,0:T(8,128)(2,1)S(1)}, bf16[1,256,384]{2,1,0:T(8,128)(2,1)S(1)}, u32[]{:S(2)}, u32[]{:S(2)}) collective-permute-start(bf16[1,256,384]{2,1,0:T(8,128)(2,1)S(1)} %add_convert_fusion.5), channel_id=1, source_target_pairs={{0,8},{8,0},{16,24},{24,16},{1,9},{9,1},{17,25},{25,17},{2,10},{10... | collective-permute-start | bytes 589832 | tf_op jit(solution)/shard_map/ppermute | solution.py:92
  286.3 15.6 %collective-permute-start.68 = (bf16[1,4,32,1024]{3,2,1,0:T(8,128)(2,1)S(1)}, bf16[1,4,32,1024]{3,2,1,0:T(8,128)(2,1)S(1)}, u32[]{:S(2)}, u32[]{:S(2)}) collective-permute-start(bf16[1,4,32,1024]{3,2,1,0:T(8,128)(2,1)S(1)} %add_convert_fusion.1), channel_id=1, source_target_pairs={{0,8},{8,0},{16,24},{24,16},{1,9},{9,1},{17,25},{25,17},{2,10},{10... | collective-permute-start | bytes 786440 | tf_op jit(solution)/shard_map/ppermute | solution.py:92
  288.0 12.8 %collective-permute-start.70 = (bf16[2,2,32,512]{3,2,1,0:T(8,128)(2,1)S(1)}, bf16[2,2,32,512]{3,2,1,0:T(8,128)(2,1)S(1)}, u32[]{:S(2)}, u32[]{:S(2)}) collective-permute-start(bf16[2,2,32,512]{3,2,1,0:T(8,128)(2,1)S(1)} %pad_maximum_fusion.20), channel_id=1, source_target_pairs={{0,8},{8,0},{16,24},{24,16},{1,9},{9,1},{17,25},{25,17},{2,10},{10... | collective-permute-start | bytes 393224 | tf_op jit(solution)/shard_map/ppermute | solution.py:92
  288.5 23.4 %collective-permute-start.72 = (bf16[128,1024]{1,0:T(8,128)(2,1)S(1)}, bf16[128,1024]{1,0:T(8,128)(2,1)S(1)}, u32[]{:S(2)}, u32[]{:S(2)}) collective-permute-start(bf16[128,1024]{1,0:T(8,128)(2,1)S(1)} %copy-done.60), channel_id=1, source_target_pairs={{0,4},{2,6},{4,0},{6,2},{1,5},{3,7},{5,1},{7,3},{8,12},{10,14},{12... | collective-permute-start | bytes 786440 | tf_op jit(solution)/shard_map/ppermute | solution.py:92
  355.2 12.3 %collective-permute-start.86 = (f32[2,2,32,384]{3,2,1,0:T(8,128)}, f32[2,2,32,384]{3,2,1,0:T(8,128)S(1)}, u32[]{:S(2)}, u32[]{:S(2)}) collective-permute-start(f32[2,2,32,384]{3,2,1,0:T(8,128)} %pad_maximum_fusion.12), channel_id=1, source_target_pairs={{0,4},{2,6},{4,0},{6,2},{1,5},{3,7},{5,1},{7,3},{8,12},{10,14},{12... | collective-permute-start | bytes 589832 | tf_op jit(solution)/shard_map/ppermute | solution.py:92
  (174 other events, 1285.9 us)
Sparse Core Ops, SparseCore 0:
  21.7 66.2 all-gather.5
  90.1 33.4 all-gather.11
  125.7 26.8 all-gather.7
  206.1 26.3 reduce-scatter.1
  235.0 38.0 all-gather.9

commit v4 on v3

--- a/solution.py
+++ b/solution.py
@@ -3,6 +3,8 @@
 import jax
 import jax.numpy as jnp
 from jax import lax
+from jax.experimental import pallas as pl
+from jax.experimental.pallas import tpu as pltpu
 from jax.sharding import PartitionSpec as P
 
 D = 1024
@@ -14,6 +16,7 @@
 STEP = 10
 
 CORES = 2
+QUERIES = 256
 
 norm_eps = 1e-06
 beta_first = 0.9
@@ -75,6 +78,66 @@
         parts = [jnp.where(turned, parts[i ^ step], parts[i]) for i in range(len(parts))]
         step *= 2
     return parts
+
+
+def attention_back(qkv_ref, d_att_ref, out_ref, d_keys, d_values):
+    at = pl.program_id(1)
+    hd = d_att_ref.shape[2]
+    first = pl.multiple_of(at * QUERIES, QUERIES)
+
+    @pl.when(at == 0)
+    def _():
+        d_keys[...] = jnp.zeros_like(d_keys)
+        d_values[...] = jnp.zeros_like(d_values)
+
+    def dot(left, right, dims):
+        return lax.dot_general(left, right, (dims, ((), ())), preferred_element_type=f32)
+
+    d_queries, k_parts, v_parts = [], [], []
+    for head in range(hd // HEAD):
+        low = head * HEAD
+        query = qkv_ref[0, pl.ds(first, QUERIES), low : low + HEAD]
+        key = qkv_ref[0, :, hd + low : hd + low + HEAD]
+        value = qkv_ref[0, :, 2 * hd + low : 2 * hd + low + HEAD]
+        d_att = d_att_ref[0, :, low : low + HEAD]
+        scores = dot(query, key, ((1,), (1,))) * HEAD ** (-0.5)
+        probs = jnp.exp(scores - jnp.max(scores, axis=1, keepdims=True))
+        probs = probs / jnp.sum(probs, axis=1, keepdims=True)
+        v_parts.append(dot(probs.astype(bf16), d_att, ((0,), (0,))))
+        d_probs = dot(d_att, value, ((1,), (1,)))
+        row_term = jnp.sum(probs * d_probs, axis=1, keepdims=True)
+        d_scores = (probs * (d_probs - row_term)).astype(bf16)
+        d_queries.append(dot(d_scores, key, ((1,), (0,))) * HEAD ** (-0.5))
+        k_parts.append(dot(d_scores, query, ((0,), (0,))) * HEAD ** (-0.5))
+    d_keys[...] += jnp.concatenate(k_parts, axis=1)
+    d_values[...] += jnp.concatenate(v_parts, axis=1)
+    out_ref[0, pl.ds(first, QUERIES), :hd] = jnp.concatenate(d_queries, axis=1).astype(bf16)
+
+    @pl.when(at == pl.num_programs(1) - 1)
+    def _():
+        out_ref[0, :, hd : 2 * hd] = d_keys[...].astype(bf16)
+        out_ref[0, :, 2 * hd :] = d_values[...].astype(bf16)
+
+
+def attention_grads(qkv, d_att):
+    images, _, hd = d_att.shape
+    return pl.pallas_call(
+        attention_back,
+        grid=(images, SEQ_LEN // QUERIES),
+        in_specs=[
+            pl.BlockSpec((1, SEQ_LEN, 3 * hd), lambda i, j: (i, 0, 0)),
+            pl.BlockSpec((1, QUERIES, hd), lambda i, j: (i, j, 0)),
+        ],
+        out_specs=pl.BlockSpec((1, SEQ_LEN, 3 * hd), lambda i, j: (i, 0, 0)),
+        out_shape=jax.ShapeDtypeStruct((images, SEQ_LEN, 3 * hd), bf16),
+        scratch_shapes=[pltpu.VMEM((SEQ_LEN, hd), f32), pltpu.VMEM((SEQ_LEN, hd), f32)],
+        compiler_params=pltpu.CompilerParams(vmem_limit_bytes=40 * 1024 * 1024),
+        cost_estimate=pl.CostEstimate(
+            flops=10 * images * SEQ_LEN * SEQ_LEN * hd,
+            bytes_accessed=14 * images * SEQ_LEN * hd,
+            transcendentals=images * SEQ_LEN * SEQ_LEN * hd // HEAD,
+        ),
+    )(qkv, d_att)
 
 
 def make_shards(n_f, n_z):
@@ -485,23 +548,18 @@
         branch_came, branch_b = further(branch_chain, branch_came)
         grad_widen = after(grad_widen, d_att)
         widen_part = lax.psum_scatter(grad_widen, "z", scatter_dimension=0, tiled=False)
-        d_att = by_image(d_att)
+        def in_images(values, order):
+            if images_group > 1:
+                values = values.reshape(n_s, BLOCK, -1)[order]
+            return values.reshape(images_group, SEQ_LEN, -1)
+
         proj_both = proj_own + swap_c(proj_other.astype(bf16)).astype(f32)
 
-        d_values = jnp.einsum("ihqk,ihqd->ihkd", probs_low, d_att, preferred_element_type=f32)
-        d_probs = jnp.einsum("ihqd,ihkd->ihqk", d_att, values, preferred_element_type=f32)
-        row_term = jnp.sum(probs * d_probs, axis=-1, keepdims=True)
-        d_scores = (probs * (d_probs - row_term)).astype(bf16)
-        d_queries = (
-            jnp.einsum("ihqk,ihkd->ihqd", d_scores, keys, preferred_element_type=f32) * head_scale
-        )
-        d_keys = (
-            jnp.einsum("ihqk,ihqd->ihkd", d_scores, queries, preferred_element_type=f32)
-            * head_scale
-        )
-        d_qkv = jnp.concatenate(
-            [by_block(part.astype(bf16)) for part in (d_queries, d_keys, d_values)], axis=1
-        )
+        order = None if images_group == 1 else arrange
+        d_qkv = attention_grads(in_images(qkv, order), in_images(d_att, order))
+        if images_group > 1:
+            d_qkv = d_qkv.reshape(n_s, BLOCK, 3 * hd)[restore]
+        d_qkv = d_qkv.reshape(tok_group, 3 * hd)
         if branch_came is not None:
             d_qkv, branch_came, proj_both = lax.optimization_barrier(
                 (d_qkv, branch_came, proj_both)
@@ -526,17 +584,16 @@
         ]
         widen_part = after(widen_part, *d_ha_low).reshape(n_f * CORES, rows, units)
 
-        branch_b, narrow_sum, proj_mid, qkv_mid, widen_back = run(
-            resume(branch_chain, branch_came, branch_b),
-            resume(narrow_chain, narrow_came, narrow_sum),
-            proj_chain,
-            halve(grad_qkv, swap_f),
-            trade_mlp([widen_part[i] for i in range(n_f * CORES)]),
-        )
-        d_ha_came = [after(part, branch_b, proj_mid, qkv_mid, *widen_back) for part in d_ha_came]
+        if branch_came is not None:
+            branch_b = alone(resume(branch_chain, branch_came))
+        if narrow_came is not None:
+            narrow_sum = alone(resume(narrow_chain, narrow_came))
+        proj_came = next(proj_chain)
+        qkv_chain = halve(grad_qkv, swap_f)
+        qkv_came = next(qkv_chain)
+        widen_chain = trade_mlp([widen_part[i] for i in range(n_f * CORES)])
+        widen_came = next(widen_chain)
         d_ha = add_parts(d_ha_z[0], d_ha_came)
-        widen_sum = jnp.stack(widen_back).reshape(n_f, CORES, rows, n_z, ub)
-        widen_sum = widen_sum.transpose(2, 0, 3, 1, 4).reshape(rows, FF).astype(f32)
         branch_b = branch_b + bias_narrow
         block_output = (middle + gate_b * branch_b).astype(bf16)
         d_gate_b = jnp.sum(grad_out * branch_b, axis=0)
@@ -564,7 +621,14 @@
             bias_g_widen,
             column_sums(d_b_own),
         ]
-        sums = alone(add_seq(jnp.concatenate(pieces)))
+        sums, proj_mid, qkv_mid, widen_back = run(
+            add_seq(jnp.concatenate(pieces)),
+            resume(proj_chain, proj_came),
+            resume(qkv_chain, qkv_came),
+            resume(widen_chain, widen_came),
+        )
+        widen_sum = jnp.stack(widen_back).reshape(n_f, CORES, rows, n_z, ub)
+        widen_sum = widen_sum.transpose(2, 0, 3, 1, 4).reshape(rows, FF).astype(f32)
         cut = images_group * 6 * D
         d_own = sums[:cut].reshape(images_group, 6 * D)
         d_cond_rows = jnp.einsum(
@@ -581,8 +645,6 @@
             came = yield swap_c(part)
             return jnp.stack(by_core(part, came), axis=1)
 
-        qkv_mid = after(qkv_mid, sums)
-        proj_mid = after(proj_mid, sums)
         whole, d_cond, proj_sum, qkv_sum = run(
             double(sums, swap_f, n_f),
             cond_chain(),

time: 383 us -> 351 us (0.916)
  waiting for transfers between devices: 139 us -> 104 us
  Pallas kernels: 0 us -> 12.5 us
  matrix products: 42.1 us -> 33.1 us
  other arithmetic: 66.1 us -> 58.3 us
  local copies, waits for them, and re-layouts: 37.9 us -> 44 us
    ppermute x87, waiting for transfers between devices: 130 us -> 104 us  [swap(): return lax.ppermute(values, axis, [(i, i ^ k) for i in range(size)])]
    dot_general x4 -> x0, matrix products: 15.8 us -> none  [the longest x1 6.42 us: shards(): jnp.einsum('ihqd,ihkd->ihqk', d_att, values, preferred_element_type=f32)]
    pallas_call x0 -> x1, Pallas kernels: none -> 12.5 us  [attention_grads(): pl.pallas_call(attention_back, grid=(images, SEQ_LEN // QUERIES), in_spec...]
    convert_element_type x2 -> x0, other arithmetic: 8.12 us -> none  [the longest x1 7.33 us: shards(): d_scores = (probs * (d_probs - row_term)).astype(bf16)]
    all_gather x1, waiting for transfers between devices: 6.51 us -> 0.01 us  [shards(): narrow_full = lax.all_gather(narrow_late, 'z', axis=0, tiled=True)]
    dot_general x1, matrix products: 1.53 us -> 5.64 us  [shards(): jnp.einsum('ihqk,ihkd->ihqd', probs_low, values, preferred_element_type=f32)]
    unnamed x259 -> x247, local copies, waits for them, and re-layouts: 17.1 us -> 15.4 us
  transfers between devices with their start and end apart: 92 -> 92, of which waited for: 41 -> 39; matrix products, arithmetic and copies ran while one was open for 32% -> 31% of each run, Pallas kernels for 0% -> 4%
where the time goes in v4:
time: 351 us; the launch traced here: 346 us
  waiting for transfers between devices  104 us (30%)
  starting transfers between devices  77 us (22%)
  other arithmetic  58.3 us (17%)
  local copies, waits for them, and re-layouts  44 us (13%)
  matrix products  33.1 us (9%)
  between operations  17.2 us (5%)
  Pallas kernels  12.5 us (4%)
    ppermute x87, waiting for transfers between devices, swap(): return lax.ppermute(values, axis, [(i, i ^ k) for i in range(size)])  104 us
    ppermute x87, starting transfers between devices, swap(): return lax.ppermute(values, axis, [(i, i ^ k) for i in range(size)])  76.6 us
    unnamed x247, local copies, waits for them, and re-layouts  15.4 us
    pallas_call x1, Pallas kernels, attention_grads(): pl.pallas_call(attention_back, grid=(images, SEQ_LEN // QUERIES), in_spec...  12.5 us
    sub x6, other arithmetic, adam_step(): weight - rate * (first / fix_first / (jnp.sqrt(second / fix_second) + ada...  10.9 us
    dot_general x5, matrix products, matmul(): return jnp.dot(left, right, preferred_element_type=f32)  7.58 us
  transfers between devices with their start and end apart: 92, of which 39 were waited for; matrix products, arithmetic and copies ran while one was open for 31% of the time, Pallas kernels for 4%

profile of v4, /device:TPU:0, one launch (start us, length us, event | category | flops | bytes accessed | tf_op | source)
XLA Modules:
  0.0 346.3 jit_solution(7779541336650530619)
XLA Ops:
  10.7 3.0 collective-permute-start
  24.7 2.7 collective-permute-start.7
  28.3 3.9 %collective-permute-done.6 = f32[2,1,6144]{2,1,0:T(1,128)S(1)} collective-permute-done((f32[2,1,6144]{2,1,0:T(1,128)S(1)}, f32[2,1,6144]{2,1,0:T(1,128)S(1)}, u32[]{:S(2)}, u32[]{:S(2)}) %collective-permute-start.6) | collective-permute-done | bytes 49184 | tf_op jit(solution)/shard_map/ppermute | solution.py:155
  34.1 2.7 collective-permute-start.11
  40.6 12.3 %collective-permute-done.9 = bf16[128,1024]{1,0:T(8,128)(2,1)} collective-permute-done((bf16[128,1024]{1,0:T(8,128)(2,1)S(1)}, bf16[128,1024]{1,0:T(8,128)(2,1)}, u32[]{:S(2)}, u32[]{:S(2)}) %collective-permute-start.9) | collective-permute-done | bytes 262176 | tf_op jit(solution)/shard_map/ppermute | solution.py:155
  65.6 2.3 collective-permute-start.14
  70.0 5.2 %collective-permute-done.16 = bf16[8,32,384]{2,1,0:T(8,128)(2,1)S(1)} collective-permute-done((bf16[8,32,384]{2,1,0:T(8,128)(2,1)S(1)}, bf16[8,32,384]{2,1,0:T(8,128)(2,1)S(1)}, u32[]{:S(2)}, u32[]{:S(2)}) %collective-permute-start.16) | collective-permute-done | bytes 196640 | tf_op jit(solution)/shard_map/ppermute | solution.py:155
  76.4 4.5 %collective-permute-done.18 = f32[14336]{0:T(1024)S(1)} collective-permute-done((f32[14336]{0:T(1024)S(1)}, f32[14336]{0:T(1024)S(1)}, u32[]{:S(2)}, u32[]{:S(2)}) %collective-permute-start.18) | collective-permute-done | bytes 57376 | tf_op jit(solution)/shard_map/ppermute | solution.py:155
  87.5 2.3 multiply_reduce_fusion
  96.8 5.6 %fusion.14 = bf16[2,1024,64]{1,2,0:T(8,128)(2,1)} fusion(bf16[2,1024,64]{1,2,0:T(8,128)(2,1)} %bitcast.701, f32[2,1024,1024]{1,2,0:T(8,128)} %copy-done, f32[2,1024]{1,0:T(2,128)} %log_add_fusion), kind=kOutput, calls=%fused_computation.30 | convolution fusion | flops 274857984 | bytes 8921088 | tf_op jit(solution)/shard_map/ihqk,ihkd->ihqd/dot_general | solution.py:475
  118.6 2.7 collective-permute-done.25
  136.5 2.3 collective-permute-done.28
  139.3 5.4 %collective-permute-done.30 = bf16[128,1024]{1,0:T(8,128)(2,1)S(1)} collective-permute-done((bf16[128,1024]{1,0:T(8,128)(2,1)S(1)}, bf16[128,1024]{1,0:T(8,128)(2,1)S(1)}, u32[]{:S(2)}, u32[]{:S(2)}) %collective-permute-start.30) | collective-permute-done | bytes 262176 | tf_op jit(solution)/shard_map/ppermute | solution.py:155
  148.1 2.7 fusion.139
  150.7 5.7 %convert_reduce_fusion.1 = (f32[512]{0:T(512)}, bf16[1024,512]{1,0:T(8,128)(2,1)S(1)}) fusion(f32[1024,512]{1,0:T(8,128)} %fusion.139, f32[512]{0:T(512)} %bitcast.785, bf16[1024,1024]{1,0:T(8,128)(2,1)} %copy-done.66, bf16[512,1024]{1,0:T(8,128)(2,1)} %all-gather.8.cloned.1.call-done), kind=kOutput, calls=%fused_computation.24 | convolution fusion | flops 1085799936 | bytes 6295552 | tf_op jit(solution)/shard_map/td,fd->tf/dot_general | solution.py:497
  170.5 4.2 %collective-permute-done.42 = bf16[128,1024]{1,0:T(8,128)(2,1)S(1)} collective-permute-done((bf16[128,1024]{1,0:T(8,128)(2,1)S(1)}, bf16[128,1024]{1,0:T(8,128)(2,1)S(1)}, u32[]{:S(2)}, u32[]{:S(2)}) %collective-permute-start.42) | collective-permute-done | bytes 262176 | tf_op jit(solution)/shard_map/ppermute | solution.py:155
  175.4 3.4 collective-permute-done.46
  194.1 2.7 collective-permute-done.50
  196.8 4.9 %collective-permute-done.51 = bf16[2,128,128]{2,1,0:T(8,128)(2,1)S(1)} collective-permute-done((bf16[2,128,128]{2,1,0:T(8,128)(2,1)S(1)}, bf16[2,128,128]{2,1,0:T(8,128)(2,1)S(1)}, u32[]{:S(2)}, u32[]{:S(2)}) %collective-permute-start.51) | collective-permute-done | bytes 65568 | tf_op jit(solution)/shard_map/ppermute | solution.py:155
  214.3 4.0 %copy.174 = bf16[1024,1024]{1,0:T(8,128)(2,1)} copy(bf16[1024,1024]{0,1:T(8,128)(2,1)} %fusion.110) | data formatting | bytes 4194304 | tf_op jit(solution)/shard_map/td,te->de/dot_general | solution.py:580
  222.2 12.5 %shard_map.373 = bf16[1,1024,384]{2,1,0:T(8,128)(2,1)S(1)} custom-call(bf16[1,1024,384]{2,1,0:T(8,128)(2,1)S(1)} %bitcast.675, bf16[1,1024,128]{2,1,0:T(8,128)(2,1)S(1)} %bitcast.676), custom_call_target="tpu_custom_call" | custom-call | flops 1342177280 | bytes 1835008 | tf_op jit(solution)/shard_map/pallas_call | solution.py:124
  241.7 2.4 convert_reduce_fusion.4
  249.9 5.9 %collective-permute-done.68 = bf16[2,4,32,1024]{3,2,1,0:T(8,128)(2,1)S(1)} collective-permute-done((bf16[2,4,32,1024]{3,2,1,0:T(8,128)(2,1)S(1)}, bf16[2,4,32,1024]{3,2,1,0:T(8,128)(2,1)S(1)}, u32[]{:S(2)}, u32[]{:S(2)}) %collective-permute-start.68) | collective-permute-done | bytes 524320 | tf_op jit(solution)/shard_map/ppermute | solution.py:155
  258.6 9.2 %collective-permute-done.64 = bf16[128,1024]{1,0:T(8,128)(2,1)S(1)} collective-permute-done((bf16[128,1024]{1,0:T(8,128)(2,1)S(1)}, bf16[128,1024]{1,0:T(8,128)(2,1)S(1)}, u32[]{:S(2)}, u32[]{:S(2)}) %collective-permute-start.64) | collective-permute-done | bytes 262176 | tf_op jit(solution)/shard_map/ppermute | solution.py:155
  279.1 2.6 multiply_subtract_fusion.1
  290.2 5.1 %collective-permute-start.74 = (f32[14336]{0:T(1024)S(1)}, f32[14336]{0:T(1024)S(1)}, u32[]{:S(2)}, u32[]{:S(2)}) collective-permute-start(f32[14336]{0:T(1024)S(1)} %add.528), channel_id=1, source_target_pairs={{0,2},{2,0},{4,6},{6,4},{1,3},{3,1},{5,7},{7,5},{8,10},{10,8},{12,... | collective-permute-start | bytes 172040 | tf_op jit(solution)/shard_map/ppermute | solution.py:155
  297.6 2.6 collective-permute-start.76
  300.3 6.5 %collective-permute-done.76 = f32[14336]{0:T(1024)S(1)} collective-permute-done((f32[14336]{0:T(1024)S(1)}, f32[14336]{0:T(1024)S(1)}, u32[]{:S(2)}, u32[]{:S(2)}) %collective-permute-start.76) | collective-permute-done | bytes 57376 | tf_op jit(solution)/shard_map/ppermute | solution.py:155
  308.0 2.7 fusion.141
  311.8 2.4 collective-permute-done.78
  327.5 2.5 collective-permute-start.86
  332.0 3.1 multiply_subtract_fusion
  (675 shorter events, 189.1 us)
Async XLA Ops:
  7.2 97.2 %all-gather.6.cloned.1.call-start = ((), (), s32[]{:S(2)}) async-start(), calls=%async_computation.1 | async-start | bytes 2162688 | tf_op jit(solution)/shard_map/all_gather | solution.py:345
  21.6 105.9 %all-gather.12.cloned.1.call-start = ((), (), s32[]{:S(2)}) async-start(), calls=%async_computation.5 | async-start | bytes 1310720 | tf_op jit(solution)/shard_map/all_gather | solution.py:402
  33.7 117.0 %all-gather.8.cloned.1.call-start = ((), (), s32[]{:S(2)}) async-start(), calls=%async_computation.2 | async-start | bytes 1310720 | tf_op jit(solution)/shard_map/all_gather | solution.py:406
  33.7 19.2 %collective-permute-start.10 = (bf16[128,1024]{1,0:T(8,128)(2,1)S(1)}, bf16[128,1024]{1,0:T(8,128)(2,1)S(1)}, u32[]{:S(2)}, u32[]{:S(2)}) collective-permute-start(bf16[128,1024]{1,0:T(8,128)(2,1)S(1)} %copy-done.11), channel_id=1, source_target_pairs={{0,4},{2,6},{4,0},{6,2},{1,5},{3,7},{5,1},{7,3},{8,12},{10,14},{12... | collective-permute-start | bytes 786440 | tf_op jit(solution)/shard_map/ppermute | solution.py:155
  34.1 21.2 %collective-permute-start.11 = (bf16[128,1024]{1,0:T(8,128)(2,1)S(1)}, bf16[128,1024]{1,0:T(8,128)(2,1)S(1)}, u32[]{:S(2)}, u32[]{:S(2)}) collective-permute-start(bf16[128,1024]{1,0:T(8,128)(2,1)S(1)} %copy-done.11), channel_id=1, source_target_pairs={{0,6},{2,4},{4,2},{6,0},{1,7},{3,5},{5,3},{7,1},{8,14},{10,12},{12... | collective-permute-start | bytes 786440 | tf_op jit(solution)/shard_map/ppermute | solution.py:155
  36.8 16.1 %collective-permute-start.9 = (bf16[128,1024]{1,0:T(8,128)(2,1)S(1)}, bf16[128,1024]{1,0:T(8,128)(2,1)}, u32[]{:S(2)}, u32[]{:S(2)}) collective-permute-start(bf16[128,1024]{1,0:T(8,128)(2,1)S(1)} %copy-done.11), channel_id=1, source_target_pairs={{0,2},{2,0},{4,6},{6,4},{1,3},{3,1},{5,7},{7,5},{8,10},{10,8},{12,... | collective-permute-start | bytes 786440 | tf_op jit(solution)/shard_map/ppermute | solution.py:155
  37.3 16.1 %collective-permute-start.19 = (bf16[128,1024]{1,0:T(8,128)(2,1)S(1)}, bf16[128,1024]{1,0:T(8,128)(2,1)}, u32[]{:S(2)}, u32[]{:S(2)}) collective-permute-start(bf16[128,1024]{1,0:T(8,128)(2,1)S(1)} %copy-done.11), channel_id=1, source_target_pairs={{0,1},{1,0},{2,3},{3,2},{4,5},{5,4},{6,7},{7,6},{8,9},{9,8},{10,11... | collective-permute-start | bytes 786440 | tf_op jit(solution)/shard_map/ppermute | solution.py:155
  38.1 235.1 %reduce-scatter.2.cloned.1.call-start = ((), (), s32[]{:S(2)}) async-start(), calls=%async_computation.3 | async-start | bytes 1310720 | tf_op jit(solution)/shard_map/reduce_scatter | solution.py:550
  52.9 12.6 %collective-permute-start.21 = (bf16[128,1024]{1,0:T(8,128)(2,1)S(1)}, bf16[128,1024]{1,0:T(8,128)(2,1)S(1)}, u32[]{:S(2)}, u32[]{:S(2)}) collective-permute-start(bf16[128,1024]{1,0:T(8,128)(2,1)S(1)} %collective-permute-done.10), channel_id=1, source_target_pairs={{0,1},{1,0},{2,3},{3,2},{4,5},{5,4},{6,7},{7,6},{8,9},{9,8},{10,11... | collective-permute-start | bytes 786440 | tf_op jit(solution)/shard_map/ppermute | solution.py:155
  55.4 12.5 %collective-permute-start.22 = (bf16[128,1024]{1,0:T(8,128)(2,1)S(1)}, bf16[128,1024]{1,0:T(8,128)(2,1)S(1)}, u32[]{:S(2)}, u32[]{:S(2)}) collective-permute-start(bf16[128,1024]{1,0:T(8,128)(2,1)S(1)} %collective-permute-done.11), channel_id=1, source_target_pairs={{0,1},{1,0},{2,3},{3,2},{4,5},{5,4},{6,7},{7,6},{8,9},{9,8},{10,11... | collective-permute-start | bytes 786440 | tf_op jit(solution)/shard_map/ppermute | solution.py:155
  63.0 12.1 %collective-permute-start.16 = (bf16[8,32,384]{2,1,0:T(8,128)(2,1)S(1)}, bf16[8,32,384]{2,1,0:T(8,128)(2,1)S(1)}, u32[]{:S(2)}, u32[]{:S(2)}) collective-permute-start(bf16[8,32,384]{2,1,0:T(8,128)(2,1)S(1)} %pad_maximum_fusion.8), channel_id=1, source_target_pairs={{0,16},{8,24},{16,0},{24,8},{1,17},{9,25},{17,1},{25,9},{2,18},{10... | collective-permute-start | bytes 589832 | tf_op jit(solution)/shard_map/ppermute | solution.py:155
  129.1 16.2 %collective-permute-start.27 = (bf16[128,1024]{1,0:T(8,128)(2,1)S(1)}, bf16[128,1024]{1,0:T(8,128)(2,1)S(1)}, u32[]{:S(2)}, u32[]{:S(2)}) collective-permute-start(bf16[128,1024]{1,0:T(8,128)(2,1)S(1)} %copy-done.51), channel_id=1, source_target_pairs={{0,1},{1,0},{2,3},{3,2},{4,5},{5,4},{6,7},{7,6},{8,9},{9,8},{10,11... | collective-permute-start | bytes 786440 | tf_op jit(solution)/shard_map/ppermute | solution.py:155
  131.1 13.6 %collective-permute-start.30 = (bf16[128,1024]{1,0:T(8,128)(2,1)S(1)}, bf16[128,1024]{1,0:T(8,128)(2,1)S(1)}, u32[]{:S(2)}, u32[]{:S(2)}) collective-permute-start(bf16[128,1024]{1,0:T(8,128)(2,1)S(1)} %copy-done.51), channel_id=1, source_target_pairs={{0,16},{8,24},{16,0},{24,8},{1,17},{9,25},{17,1},{25,9},{2,18},{10... | collective-permute-start | bytes 786440 | tf_op jit(solution)/shard_map/ppermute | solution.py:155
  132.6 12.2 %collective-permute-start.32 = (bf16[128,1024]{1,0:T(8,128)(2,1)S(1)}, bf16[128,1024]{1,0:T(8,128)(2,1)S(1)}, u32[]{:S(2)}, u32[]{:S(2)}) collective-permute-start(bf16[128,1024]{1,0:T(8,128)(2,1)S(1)} %copy-done.51), channel_id=1, source_target_pairs={{0,24},{8,16},{16,8},{24,0},{1,25},{9,17},{17,9},{25,1},{2,26},{10... | collective-permute-start | bytes 786440 | tf_op jit(solution)/shard_map/ppermute | solution.py:155
  161.4 14.0 %collective-permute-start.45 = (bf16[2,128,1024]{2,1,0:T(8,128)(2,1)S(1)}, bf16[2,128,1024]{2,1,0:T(8,128)(2,1)S(1)}, u32[]{:S(2)}, u32[]{:S(2)}) collective-permute-start(bf16[2,128,1024]{2,1,0:T(8,128)(2,1)S(1)} %pad_maximum_fusion.3), channel_id=1, source_target_pairs={{0,2},{2,0},{4,6},{6,4},{1,3},{3,1},{5,7},{7,5},{8,10},{10,8},{12,... | collective-permute-start | bytes 1572872 | tf_op jit(solution)/shard_map/ppermute | solution.py:155
  166.3 12.5 %collective-permute-start.46 = (bf16[128,1024]{1,0:T(8,128)(2,1)S(1)}, bf16[128,1024]{1,0:T(8,128)(2,1)S(1)}, u32[]{:S(2)}, u32[]{:S(2)}) collective-permute-start(bf16[128,1024]{1,0:T(8,128)(2,1)S(1)} %get-tuple-element.184), channel_id=1, source_target_pairs={{0,16},{8,24},{16,0},{24,8},{1,17},{9,25},{17,1},{25,9},{2,18},{10... | collective-permute-start | bytes 786440 | tf_op jit(solution)/shard_map/ppermute | solution.py:155
  167.6 12.8 %collective-permute-start.47 = (bf16[128,1024]{1,0:T(8,128)(2,1)S(1)}, bf16[128,1024]{1,0:T(8,128)(2,1)S(1)}, u32[]{:S(2)}, u32[]{:S(2)}) collective-permute-start(bf16[128,1024]{1,0:T(8,128)(2,1)S(1)} %get-tuple-element.185), channel_id=1, source_target_pairs={{0,24},{8,16},{16,8},{24,0},{1,25},{9,17},{17,9},{25,1},{2,26},{10... | collective-permute-start | bytes 786440 | tf_op jit(solution)/shard_map/ppermute | solution.py:155
  183.1 18.7 %collective-permute-start.53 = (bf16[1,128,1024]{2,1,0:T(8,128)(2,1)S(1)}, bf16[1,128,1024]{2,1,0:T(8,128)(2,1)S(1)}, u32[]{:S(2)}, u32[]{:S(2)}) collective-permute-start(bf16[1,128,1024]{2,1,0:T(8,128)(2,1)S(1)} %add_convert_fusion.3), channel_id=1, source_target_pairs={{0,4},{2,6},{4,0},{6,2},{1,5},{3,7},{5,1},{7,3},{8,12},{10,14},{12... | collective-permute-start | bytes 786440 | tf_op jit(solution)/shard_map/ppermute | solution.py:155
  188.0 14.1 %collective-permute-start.56 = (bf16[2,128,1024]{2,1,0:T(8,128)(2,1)S(1)}, bf16[2,128,1024]{2,1,0:T(8,128)(2,1)}, u32[]{:S(2)}, u32[]{:S(2)}) collective-permute-start(bf16[2,128,1024]{2,1,0:T(8,128)(2,1)S(1)} %pad_maximum_fusion.4), channel_id=1, source_target_pairs={{0,16},{8,24},{16,0},{24,8},{1,17},{9,25},{17,1},{25,9},{2,18},{10... | collective-permute-start | bytes 1572872 | tf_op jit(solution)/shard_map/ppermute | solution.py:155
  202.5 105.4 %all-gather.10.cloned.1.call-start = ((), (), s32[]{:S(2)}) async-start(), calls=%async_computation.4 | async-start | bytes 1966080 | tf_op jit(solution)/shard_map/all_gather | solution.py:489
  212.1 22.6 %collective-permute-start.59 = (bf16[4,4,32,1024]{3,2,1,0:T(8,128)(2,1)}, bf16[4,4,32,1024]{3,2,1,0:T(8,128)(2,1)}, u32[]{:S(2)}, u32[]{:S(2)}) collective-permute-start(bf16[4,4,32,1024]{3,2,1,0:T(8,128)(2,1)} %fusion.15), channel_id=1, source_target_pairs={{0,1},{1,0},{2,3},{3,2},{4,5},{5,4},{6,7},{7,6},{8,9},{9,8},{10,11... | collective-permute-start | bytes 3145736 | tf_op jit(solution)/shard_map/ppermute | solution.py:155
  219.4 22.0 %collective-permute-start.48 = (bf16[128,1024]{1,0:T(8,128)(2,1)}, bf16[128,1024]{1,0:T(8,128)(2,1)S(1)}, u32[]{:S(2)}, u32[]{:S(2)}) collective-permute-start(bf16[128,1024]{1,0:T(8,128)(2,1)} %get-tuple-element.193), channel_id=1, source_target_pairs={{0,1},{1,0},{2,3},{3,2},{4,5},{5,4},{6,7},{7,6},{8,9},{9,8},{10,11... | collective-permute-start | bytes 786440 | tf_op jit(solution)/shard_map/ppermute | solution.py:155
  221.1 15.4 %collective-permute-start.58 = (bf16[1,128,1024]{2,1,0:T(8,128)(2,1)S(1)}, bf16[1,128,1024]{2,1,0:T(8,128)(2,1)S(1)}, u32[]{:S(2)}, u32[]{:S(2)}) collective-permute-start(bf16[1,128,1024]{2,1,0:T(8,128)(2,1)S(1)} %fusion.57), channel_id=1, source_target_pairs={{0,8},{8,0},{16,24},{24,16},{1,9},{9,1},{17,25},{25,17},{2,10},{10... | collective-permute-start | bytes 786440 | tf_op jit(solution)/shard_map/ppermute | solution.py:155
  238.7 17.1 %collective-permute-start.68 = (bf16[2,4,32,1024]{3,2,1,0:T(8,128)(2,1)S(1)}, bf16[2,4,32,1024]{3,2,1,0:T(8,128)(2,1)S(1)}, u32[]{:S(2)}, u32[]{:S(2)}) collective-permute-start(bf16[2,4,32,1024]{3,2,1,0:T(8,128)(2,1)S(1)} %pad_maximum_fusion.5), channel_id=1, source_target_pairs={{0,16},{8,24},{16,0},{24,8},{1,17},{9,25},{17,1},{25,9},{2,18},{10... | collective-permute-start | bytes 1572872 | tf_op jit(solution)/shard_map/ppermute | solution.py:155
  241.4 15.5 %collective-permute-start.60 = (bf16[128,1024]{1,0:T(8,128)(2,1)S(1)}, bf16[128,1024]{1,0:T(8,128)(2,1)S(1)}, u32[]{:S(2)}, u32[]{:S(2)}) collective-permute-start(bf16[128,1024]{1,0:T(8,128)(2,1)S(1)} %get-tuple-element.189), channel_id=1, source_target_pairs={{0,1},{1,0},{2,3},{3,2},{4,5},{5,4},{6,7},{7,6},{8,9},{9,8},{10,11... | collective-permute-start | bytes 786440 | tf_op jit(solution)/shard_map/ppermute | solution.py:155
  244.6 14.0 %collective-permute-start.62 = (bf16[128,1024]{1,0:T(8,128)(2,1)S(1)}, bf16[128,1024]{1,0:T(8,128)(2,1)S(1)}, u32[]{:S(2)}, u32[]{:S(2)}) collective-permute-start(bf16[128,1024]{1,0:T(8,128)(2,1)S(1)} %get-tuple-element.179), channel_id=1, source_target_pairs={{0,2},{2,0},{4,6},{6,4},{1,3},{3,1},{5,7},{7,5},{8,10},{10,8},{12,... | collective-permute-start | bytes 786440 | tf_op jit(solution)/shard_map/ppermute | solution.py:155
  246.5 21.3 %collective-permute-start.64 = (bf16[128,1024]{1,0:T(8,128)(2,1)S(1)}, bf16[128,1024]{1,0:T(8,128)(2,1)S(1)}, u32[]{:S(2)}, u32[]{:S(2)}) collective-permute-start(bf16[128,1024]{1,0:T(8,128)(2,1)S(1)} %get-tuple-element.181), channel_id=1, source_target_pairs={{0,4},{2,6},{4,0},{6,2},{1,5},{3,7},{5,1},{7,3},{8,12},{10,14},{12... | collective-permute-start | bytes 786440 | tf_op jit(solution)/shard_map/ppermute | solution.py:155
  246.9 20.9 %collective-permute-start.66 = (bf16[128,1024]{1,0:T(8,128)(2,1)S(1)}, bf16[128,1024]{1,0:T(8,128)(2,1)S(1)}, u32[]{:S(2)}, u32[]{:S(2)}) collective-permute-start(bf16[128,1024]{1,0:T(8,128)(2,1)S(1)} %get-tuple-element.180), channel_id=1, source_target_pairs={{0,6},{2,4},{4,2},{6,0},{1,7},{3,5},{5,3},{7,1},{8,14},{10,12},{12... | collective-permute-start | bytes 786440 | tf_op jit(solution)/shard_map/ppermute | solution.py:155
  255.8 18.9 %collective-permute-start.70 = (bf16[2,256,384]{2,1,0:T(8,128)(2,1)}, bf16[2,256,384]{2,1,0:T(8,128)(2,1)}, u32[]{:S(2)}, u32[]{:S(2)}) collective-permute-start(bf16[2,256,384]{2,1,0:T(8,128)(2,1)} %pad_maximum_fusion.6), channel_id=1, source_target_pairs={{0,16},{8,24},{16,0},{24,8},{1,17},{9,25},{17,1},{25,9},{2,18},{10... | collective-permute-start | bytes 1179656 | tf_op jit(solution)/shard_map/ppermute | solution.py:155
  256.9 24.8 %collective-permute-start.69 = (bf16[1,4,32,1024]{3,2,1,0:T(8,128)(2,1)}, bf16[1,4,32,1024]{3,2,1,0:T(8,128)(2,1)}, u32[]{:S(2)}, u32[]{:S(2)}) collective-permute-start(bf16[1,4,32,1024]{3,2,1,0:T(8,128)(2,1)} %add_convert_fusion.1), channel_id=1, source_target_pairs={{0,8},{8,0},{16,24},{24,16},{1,9},{9,1},{17,25},{25,17},{2,10},{10... | collective-permute-start | bytes 786440 | tf_op jit(solution)/shard_map/ppermute | solution.py:155
  287.4 26.8 %collective-permute-start.80 = (f32[4,32,384]{2,1,0:T(8,128)}, f32[4,32,384]{2,1,0:T(8,128)S(1)}, u32[]{:S(2)}, u32[]{:S(2)}) collective-permute-start(f32[4,32,384]{2,1,0:T(8,128)} %pad_maximum_fusion.9), channel_id=1, source_target_pairs={{0,1},{1,0},{2,3},{3,2},{4,5},{5,4},{6,7},{7,6},{8,9},{9,8},{10,11... | collective-permute-start | bytes 589832 | tf_op jit(solution)/shard_map/ppermute | solution.py:155
  295.4 16.5 %collective-permute-start.79 = (bf16[2,32,1024]{2,1,0:T(8,128)(2,1)S(1)}, bf16[2,32,1024]{2,1,0:T(8,128)(2,1)S(1)}, u32[]{:S(2)}, u32[]{:S(2)}) collective-permute-start(bf16[2,32,1024]{2,1,0:T(8,128)(2,1)S(1)} %pad_maximum_fusion.21), channel_id=1, source_target_pairs={{0,4},{2,6},{4,0},{6,2},{1,5},{3,7},{5,1},{7,3},{8,12},{10,14},{12... | collective-permute-start | bytes 393224 | tf_op jit(solution)/shard_map/ppermute | solution.py:155
  (167 other events, 1098.0 us)
Sparse Core Ops, SparseCore 0:
  21.7 64.8 all-gather.5
  88.8 28.5 all-gather.11
  119.6 29.6 all-gather.7
  202.6 26.2 reduce-scatter.1
  231.3 40.0 all-gather.9

commit v5 on v4

--- a/solution.py
+++ b/solution.py
@@ -117,6 +117,42 @@
     def _():
         out_ref[0, :, hd : 2 * hd] = d_keys[...].astype(bf16)
         out_ref[0, :, 2 * hd :] = d_values[...].astype(bf16)
+
+
+def attention_forward(qkv_ref, out_ref):
+    hd = out_ref.shape[2]
+    first = pl.multiple_of(pl.program_id(1) * QUERIES, QUERIES)
+    parts = []
+    for head in range(hd // HEAD):
+        low = head * HEAD
+        query = qkv_ref[0, pl.ds(first, QUERIES), low : low + HEAD]
+        key = qkv_ref[0, :, hd + low : hd + low + HEAD]
+        value = qkv_ref[0, :, 2 * hd + low : 2 * hd + low + HEAD]
+        scores = lax.dot_general(
+            query, key, (((1,), (1,)), ((), ())), preferred_element_type=f32
+        ) * HEAD ** (-0.5)
+        probs = jnp.exp(scores - jnp.max(scores, axis=1, keepdims=True))
+        probs = (probs / jnp.sum(probs, axis=1, keepdims=True)).astype(bf16)
+        parts.append(jnp.dot(probs, value, preferred_element_type=f32))
+    out_ref[0] = jnp.concatenate(parts, axis=1).astype(bf16)
+
+
+def attention(qkv):
+    images, _, wide = qkv.shape
+    hd = wide // 3
+    return pl.pallas_call(
+        attention_forward,
+        grid=(images, SEQ_LEN // QUERIES),
+        in_specs=[pl.BlockSpec((1, SEQ_LEN, wide), lambda i, j: (i, 0, 0))],
+        out_specs=pl.BlockSpec((1, QUERIES, hd), lambda i, j: (i, j, 0)),
+        out_shape=jax.ShapeDtypeStruct((images, SEQ_LEN, hd), bf16),
+        compiler_params=pltpu.CompilerParams(vmem_limit_bytes=40 * 1024 * 1024),
+        cost_estimate=pl.CostEstimate(
+            flops=4 * images * SEQ_LEN * SEQ_LEN * hd,
+            bytes_accessed=8 * images * SEQ_LEN * hd,
+            transcendentals=images * SEQ_LEN * SEQ_LEN * hd // HEAD,
+        ),
+    )(qkv)
 
 
 def attention_grads(qkv, d_att):
@@ -360,7 +396,7 @@
             while len(due) > 1:
                 half = len(due) // 2
                 low = jnp.stack(due[half:])
-                if half == 1:
+                if len(due) == n_f:
                     low = after(low, *tokens_z[1:])
                 came = yield swap_f(low, half)
                 due = [due[k] + came[k] for k in range(half)]
@@ -423,17 +459,10 @@
             own_row[i * D : (i + 1) * D] for i in range(6)
         ]
 
-        def by_image(values):
+        def in_images(values, order):
             if images_group > 1:
-                values = values.reshape(n_s, BLOCK, hd)[arrange]
-            values = values.reshape(images_group, SEQ_LEN, heads_dev, HEAD)
-            return values.transpose(0, 2, 1, 3)
-
-        def by_block(values):
-            values = values.transpose(0, 2, 1, 3).reshape(tok_group, hd)
-            if images_group > 1:
-                values = values.reshape(n_s, BLOCK, hd)[restore].reshape(tok_group, hd)
-            return values
+                values = values.reshape(n_s, BLOCK, -1)[order]
+            return values.reshape(images_group, SEQ_LEN, -1)
 
         def send_blocks(values):
             came = swap_c(values[:, 1])
@@ -462,20 +491,11 @@
         value_bias = lax.dynamic_index_in_dim(bias_value, at_s, keepdims=False)
         qkv_bias = jnp.concatenate([query_bias, jnp.zeros((hd,), f32), value_bias])
         qkv = (matmul(h_a, qkv_full) + qkv_bias).astype(bf16)
-        queries = by_image(qkv[:, :hd])
-        keys = by_image(qkv[:, hd : 2 * hd])
-        values = by_image(qkv[:, 2 * hd :])
-        scores = (
-            jnp.einsum("ihqd,ihkd->ihqk", queries, keys, preferred_element_type=f32) * head_scale
-        )
-        log_total = jax.nn.logsumexp(scores, axis=-1, keepdims=True)
-        probs = jnp.exp(scores - log_total)
-        probs_low = probs.astype(bf16)
-        attended = by_block(
-            jnp.einsum("ihqk,ihkd->ihqd", probs_low, values, preferred_element_type=f32).astype(
-                bf16
-            )
-        )
+        order = None if images_group == 1 else arrange
+        attended = attention(in_images(qkv, order))
+        if images_group > 1:
+            attended = attended.reshape(n_s, BLOCK, hd)[restore]
+        attended = attended.reshape(tok_group, hd)
         attended = after(attended, proj_full)
         att_own = send_blocks(attended.reshape(n_z, CORES, BLOCK, hd))
 
@@ -523,12 +543,6 @@
         d_att_own = jnp.einsum("te,de->td", d_a, proj_full, preferred_element_type=f32)
         d_att_own = d_att_own.astype(bf16)
         d_att = send_heads(d_att_own)
-        grad_proj = jnp.einsum(
-            "td,te->de", att_own, after(d_a, d_att_own), preferred_element_type=f32
-        )
-        grad_proj = grad_proj.reshape(n_f, n_z, CORES, rows, D)
-        proj_own, proj_other = by_core(grad_proj[:, :, 0], grad_proj[:, :, 1])
-
         branch_chain = halve(join_cores(after(branch_part, d_hb)), swap_f)
         branch_came = next(branch_chain)
 
@@ -548,24 +562,19 @@
         branch_came, branch_b = further(branch_chain, branch_came)
         grad_widen = after(grad_widen, d_att)
         widen_part = lax.psum_scatter(grad_widen, "z", scatter_dimension=0, tiled=False)
-        def in_images(values, order):
-            if images_group > 1:
-                values = values.reshape(n_s, BLOCK, -1)[order]
-            return values.reshape(images_group, SEQ_LEN, -1)
-
-        proj_both = proj_own + swap_c(proj_other.astype(bf16)).astype(f32)
-
-        order = None if images_group == 1 else arrange
+
         d_qkv = attention_grads(in_images(qkv, order), in_images(d_att, order))
         if images_group > 1:
             d_qkv = d_qkv.reshape(n_s, BLOCK, 3 * hd)[restore]
         d_qkv = d_qkv.reshape(tok_group, 3 * hd)
         if branch_came is not None:
-            d_qkv, branch_came, proj_both = lax.optimization_barrier(
-                (d_qkv, branch_came, proj_both)
-            )
-        else:
-            d_qkv, proj_both = lax.optimization_barrier((d_qkv, proj_both))
+            d_qkv, branch_came = lax.optimization_barrier((d_qkv, branch_came))
+        grad_proj = jnp.einsum(
+            "td,te->de", att_own, after(d_a, d_qkv), preferred_element_type=f32
+        )
+        grad_proj = grad_proj.reshape(n_f, n_z, CORES, rows, D)
+        proj_own, proj_other = by_core(grad_proj[:, :, 0], grad_proj[:, :, 1])
+        proj_both = proj_own + swap_c(proj_other.astype(bf16)).astype(f32)
         proj_chain = halve(
             [
                 lax.dynamic_index_in_dim(proj_both, at_f ^ k, 0, keepdims=False)
@@ -577,7 +586,7 @@
         d_ha_z = join_cores(d_ha_part.reshape(n_z, CORES, BLOCK, D))
         d_ha_low = [d_ha_z[k].astype(bf16) for k in range(1, n_z)]
         d_ha_came = [swap_z(d_ha_low[k - 1], k) for k in range(1, n_z)]
-        grad_qkv = jnp.einsum("td,te->de", h_a, d_qkv, preferred_element_type=f32)
+        grad_qkv = jnp.einsum("td,te->de", after(h_a, d_ha_part), d_qkv, preferred_element_type=f32)
         grad_qkv = after(grad_qkv.reshape(n_f, n_s * rows, 3 * hd), *d_ha_low)
         grad_qkv = [
             lax.dynamic_index_in_dim(grad_qkv, at_f ^ k, 0, keepdims=False) for k in range(n_f)
@@ -621,14 +630,7 @@
             bias_g_widen,
             column_sums(d_b_own),
         ]
-        sums, proj_mid, qkv_mid, widen_back = run(
-            add_seq(jnp.concatenate(pieces)),
-            resume(proj_chain, proj_came),
-            resume(qkv_chain, qkv_came),
-            resume(widen_chain, widen_came),
-        )
-        widen_sum = jnp.stack(widen_back).reshape(n_f, CORES, rows, n_z, ub)
-        widen_sum = widen_sum.transpose(2, 0, 3, 1, 4).reshape(rows, FF).astype(f32)
+        sums = alone(add_seq(jnp.concatenate(pieces)))
         cut = images_group * 6 * D
         d_own = sums[:cut].reshape(images_group, 6 * D)
         d_cond_rows = jnp.einsum(
@@ -645,12 +647,24 @@
             came = yield swap_c(part)
             return jnp.stack(by_core(part, came), axis=1)
 
-        whole, d_cond, proj_sum, qkv_sum = run(
+        def proj_rest():
+            mid = yield from resume(proj_chain, proj_came)
+            mid = xor_parts([mid[k] for k in range(n_z)], at_z)
+            return (yield from halve(mid, swap_z))
+
+        def qkv_rest():
+            mid = yield from resume(qkv_chain, qkv_came)
+            return (yield from trade_seq([mid[i : i + rows] for i in range(0, n_s * rows, rows)]))
+
+        whole, d_cond, proj_sum, qkv_sum, widen_back = run(
             double(sums, swap_f, n_f),
             cond_chain(),
-            halve(xor_parts([proj_mid[k] for k in range(n_z)], at_z), swap_z),
-            trade_seq([qkv_mid[i : i + rows] for i in range(0, n_s * rows, rows)]),
-        )
+            proj_rest(),
+            qkv_rest(),
+            resume(widen_chain, widen_came),
+        )
+        widen_sum = jnp.stack(widen_back).reshape(n_f, CORES, rows, n_z, ub)
+        widen_sum = widen_sum.transpose(2, 0, 3, 1, 4).reshape(rows, FF).astype(f32)
         qkv_sum = jnp.stack(qkv_sum).reshape(n_s, rows, 3, hd)
         qkv_sum = qkv_sum.transpose(1, 2, 0, 3).reshape(rows, 3 * D)
         d_cond = d_cond.reshape(n_s, images_group, n_f, rows)

time: 351 us -> 364 us (1.037)
  waiting for transfers between devices: 104 us -> 134 us
  matrix products: 33.1 us -> 22.8 us
  local copies, waits for them, and re-layouts: 44 us -> 33.7 us
  Pallas kernels: 12.5 us -> 18.5 us
  other arithmetic: 58.3 us -> 54.5 us
    ppermute x87, waiting for transfers between devices: 104 us -> 125 us  [swap(): return lax.ppermute(values, axis, [(i, i ^ k) for i in range(size)])]
    dot_general x4 -> x2, matrix products: 11 us -> 2.01 us  [the longest x1 1.28 us: shards(): jnp.einsum('td,te->de', after(h_a, d_ha_part), d_qkv, preferred_element_t...]
    all_gather x1, waiting for transfers between devices: 0.01 us -> 8.81 us  [shards(): lax.all_gather(jnp.concatenate(widen_mine), 'z', axis=0, tiled=False)]
    pallas_call x0 -> x1, Pallas kernels: none -> 6.24 us  [attention(): pl.pallas_call(attention_forward, grid=(images, SEQ_LEN // QUERIES), in_s...]
    slice x4 -> x0, local copies, waits for them, and re-layouts: 5.62 us -> none  [the longest x2 2.72 us: shards(): keys = by_image(qkv[:, hd:2 * hd])]
    dot_general x1 -> x0, local copies, waits for them, and re-layouts: 4.02 us -> none  [shards(): grad_qkv = jnp.einsum('td,te->de', h_a, d_qkv, preferred_element_type=f32)]
    unnamed x247 -> x239, local copies, waits for them, and re-layouts: 15.4 us -> 17.5 us
  transfers between devices with their start and end apart: 92 -> 92, of which waited for: 39 -> 36; matrix products, arithmetic and copies ran while one was open for 31% -> 26% of each run, Pallas kernels for 4% -> 5%
where the time goes in v5:
time: 364 us; the launch traced here: 359 us
  waiting for transfers between devices  134 us (37%)
  starting transfers between devices  78.6 us (22%)
  other arithmetic  54.5 us (15%)
  local copies, waits for them, and re-layouts  33.7 us (9%)
  matrix products  22.8 us (6%)
  Pallas kernels  18.5 us (5%)
  between operations  17.5 us (5%)
    ppermute x87, waiting for transfers between devices, swap(): return lax.ppermute(values, axis, [(i, i ^ k) for i in range(size)])  125 us
    ppermute x87, starting transfers between devices, swap(): return lax.ppermute(values, axis, [(i, i ^ k) for i in range(size)])  77.8 us
    unnamed x239, local copies, waits for them, and re-layouts  17.5 us
    pallas_call x1, Pallas kernels, attention_grads(): pl.pallas_call(attention_back, grid=(images, SEQ_LEN // QUERIES), in_spec...  12.3 us
    sub x6, other arithmetic, adam_step(): weight - rate * (first / fix_first / (jnp.sqrt(second / fix_second) + ada...  10.9 us
    all_gather x1, waiting for transfers between devices, shards(): lax.all_gather(jnp.concatenate(widen_mine), 'z', axis=0, tiled=False)  8.81 us
  transfers between devices with their start and end apart: 92, of which 36 were waited for; matrix products, arithmetic and copies ran while one was open for 26% of the time, Pallas kernels for 5%

profile of v5, /device:TPU:0, one launch (start us, length us, event | category | flops | bytes accessed | tf_op | source)
XLA Modules:
  0.0 359.4 jit_solution(2330412421189844882)
XLA Ops:
  10.8 3.0 collective-permute-start
  22.6 2.6 collective-permute-start.7
  30.2 2.7 collective-permute-done.6
  32.9 14.0 %collective-permute-done.7 = bf16[128,1024]{1,0:T(8,128)(2,1)S(1)} collective-permute-done((bf16[128,1024]{1,0:T(8,128)(2,1)S(1)}, bf16[128,1024]{1,0:T(8,128)(2,1)S(1)}, u32[]{:S(2)}, u32[]{:S(2)}) %collective-permute-start.7) | collective-permute-done | bytes 262176 | tf_op jit(solution)/shard_map/ppermute | solution.py:191
  47.2 3.8 %collective-permute-done.9 = f32[2,1,6144]{2,1,0:T(1,128)S(1)} collective-permute-done((f32[2,1,6144]{2,1,0:T(1,128)S(1)}, f32[2,1,6144]{2,1,0:T(1,128)S(1)}, u32[]{:S(2)}, u32[]{:S(2)}) %collective-permute-start.9) | collective-permute-done | bytes 49184 | tf_op jit(solution)/shard_map/ppermute | solution.py:191
  72.7 3.6 %collective-permute-start.14 = (f32[14336]{0:T(1024)S(1)}, f32[14336]{0:T(1024)S(1)}, u32[]{:S(2)}, u32[]{:S(2)}) collective-permute-start(f32[14336]{0:T(1024)S(1)} %fusion.103), channel_id=1, source_target_pairs={{0,2},{2,0},{4,6},{6,4},{1,3},{3,1},{5,7},{7,5},{8,10},{10,8},{12,... | collective-permute-start | bytes 172040 | tf_op jit(solution)/shard_map/ppermute | solution.py:191
  79.3 5.7 %collective-permute-done.16 = bf16[8,32,384]{2,1,0:T(8,128)(2,1)S(1)} collective-permute-done((bf16[8,32,384]{2,1,0:T(8,128)(2,1)S(1)}, bf16[8,32,384]{2,1,0:T(8,128)(2,1)S(1)}, u32[]{:S(2)}, u32[]{:S(2)}) %collective-permute-start.16) | collective-permute-done | bytes 196640 | tf_op jit(solution)/shard_map/ppermute | solution.py:191
  85.0 4.5 %collective-permute-start.18 = (f32[14336]{0:T(1024)S(1)}, f32[14336]{0:T(1024)S(1)}, u32[]{:S(2)}, u32[]{:S(2)}) collective-permute-start(f32[14336]{0:T(1024)S(1)} %add.453), channel_id=1, source_target_pairs={{0,4},{2,6},{4,0},{6,2},{1,5},{3,7},{5,1},{7,3},{8,12},{10,14},{12... | collective-permute-start | bytes 172040 | tf_op jit(solution)/shard_map/ppermute | solution.py:191
  89.8 3.6 collective-permute-done.18
  98.0 6.2 %shard_map.373 = bf16[1,1024,128]{2,1,0:T(8,128)(2,1)S(1)} custom-call(bf16[1,1024,384]{2,1,0:T(8,128)(2,1)S(1)} %fusion.13.qkv_ref), custom_call_target="tpu_custom_call" | custom-call | flops 536870912 | bytes 1048576 | tf_op jit(solution)/shard_map/pallas_call | solution.py:143
  111.0 7.5 %collective-permute-done.35 = bf16[2,128,1024]{2,1,0:T(8,128)(2,1)} collective-permute-done((bf16[2,128,1024]{2,1,0:T(8,128)(2,1)S(1)}, bf16[2,128,1024]{2,1,0:T(8,128)(2,1)}, u32[]{:S(2)}, u32[]{:S(2)}) %collective-permute-start.35) | collective-permute-done | bytes 524320 | tf_op jit(solution)/shard_map/ppermute | solution.py:191
  119.7 8.8 %all-gather.12.cloned.1.call-done = bf16[1024,512]{1,0:T(8,128)(2,1)} async-done(((bf16[256,512]{1,0:T(8,128)(2,1)}), bf16[1024,512]{1,0:T(8,128)(2,1)}) %all-gather.12.cloned.1.call-update) | async-done | bytes 1048592 | tf_op jit(solution)/shard_map/all_gather | solution.py:438
  145.8 5.4 %collective-permute-done.30 = bf16[128,1024]{1,0:T(8,128)(2,1)} collective-permute-done((bf16[128,1024]{1,0:T(8,128)(2,1)}, bf16[128,1024]{1,0:T(8,128)(2,1)}, u32[]{:S(2)}, u32[]{:S(2)}) %collective-permute-start.30) | collective-permute-done | bytes 262176 | tf_op jit(solution)/shard_map/ppermute | solution.py:191
  157.4 2.6 fusion.131
  160.0 5.1 %convert_reduce_fusion.1 = (f32[512]{0:T(512)S(1)}, bf16[1024,512]{1,0:T(8,128)(2,1)S(1)}) fusion(f32[1024,512]{1,0:T(8,128)} %fusion.131, f32[512]{0:T(512)S(1)} %bitcast.757, bf16[1024,1024]{1,0:T(8,128)(2,1)} %copy-done.70, bf16[512,1024]{1,0:T(8,128)(2,1)} %all-gather.8.cloned.1.call-done), kind=kOutput, calls=%fused_computation.21 | convolution fusion | flops 1085799936 | bytes 6295552 | tf_op jit(solution)/shard_map/td,fd->tf/dot_general | solution.py:517
  179.4 7.0 %collective-permute-done.47 = bf16[128,1024]{1,0:T(8,128)(2,1)S(1)} collective-permute-done((bf16[128,1024]{1,0:T(8,128)(2,1)S(1)}, bf16[128,1024]{1,0:T(8,128)(2,1)S(1)}, u32[]{:S(2)}, u32[]{:S(2)}) %collective-permute-start.47) | collective-permute-done | bytes 262176 | tf_op jit(solution)/shard_map/ppermute | solution.py:191
  186.4 8.3 %collective-permute-done.46 = bf16[128,1024]{1,0:T(8,128)(2,1)S(1)} collective-permute-done((bf16[128,1024]{1,0:T(8,128)(2,1)S(1)}, bf16[128,1024]{1,0:T(8,128)(2,1)S(1)}, u32[]{:S(2)}, u32[]{:S(2)}) %collective-permute-start.46) | collective-permute-done | bytes 262176 | tf_op jit(solution)/shard_map/ppermute | solution.py:191
  194.7 2.9 collective-permute-done.42
  207.8 3.3 collective-permute-done.52
  211.1 8.9 %collective-permute-start.50 = (bf16[2,128,128]{2,1,0:T(8,128)(2,1)S(1)}, bf16[2,128,128]{2,1,0:T(8,128)(2,1)S(1)}, u32[]{:S(2)}, u32[]{:S(2)}) collective-permute-start(bf16[2,128,128]{2,1,0:T(8,128)(2,1)S(1)} %pad_maximum_fusion.38), channel_id=1, source_target_pairs={{0,2},{2,0},{4,6},{6,4},{1,3},{3,1},{5,7},{7,5},{8,10},{10,8},{12,... | collective-permute-start | bytes 196616 | tf_op jit(solution)/shard_map/ppermute | solution.py:191
  223.9 12.3 %shard_map.374 = bf16[1,1024,384]{2,1,0:T(8,128)(2,1)S(1)} custom-call(bf16[1,1024,384]{2,1,0:T(8,128)(2,1)S(1)} %fusion.13.qkv_ref, bf16[1,1024,128]{2,1,0:T(8,128)(2,1)S(1)} %bitcast.650), custom_call_target="tpu_custom_call" | custom-call | flops 1342177280 | bytes 1835008 | tf_op jit(solution)/shard_map/pallas_call | solution.py:160
  240.0 2.9 copy-done.17
  252.4 4.0 %collective-permute-done.65 = bf16[128,1024]{1,0:T(8,128)(2,1)S(1)} collective-permute-done((bf16[128,1024]{1,0:T(8,128)(2,1)S(1)}, bf16[128,1024]{1,0:T(8,128)(2,1)S(1)}, u32[]{:S(2)}, u32[]{:S(2)}) %collective-permute-start.65) | collective-permute-done | bytes 262176 | tf_op jit(solution)/shard_map/ppermute | solution.py:191
  256.4 15.5 %collective-permute-done.63 = bf16[128,1024]{1,0:T(8,128)(2,1)S(1)} collective-permute-done((bf16[128,1024]{1,0:T(8,128)(2,1)S(1)}, bf16[128,1024]{1,0:T(8,128)(2,1)S(1)}, u32[]{:S(2)}, u32[]{:S(2)}) %collective-permute-start.63) | collective-permute-done | bytes 262176 | tf_op jit(solution)/shard_map/ppermute | solution.py:191
  275.8 3.4 collective-permute-done.67
  286.1 3.1 bitcast_add_fusion
  290.1 2.7 fusion.133
  293.9 7.6 %collective-permute-done.72 = bf16[2,4,32,1024]{3,2,1,0:T(8,128)(2,1)} collective-permute-done((bf16[2,4,32,1024]{3,2,1,0:T(8,128)(2,1)S(1)}, bf16[2,4,32,1024]{3,2,1,0:T(8,128)(2,1)}, u32[]{:S(2)}, u32[]{:S(2)}) %collective-permute-start.72) | collective-permute-done | bytes 524320 | tf_op jit(solution)/shard_map/ppermute | solution.py:191
  306.3 3.0 collective-permute-done.73
  318.5 2.5 multiply_subtract_fusion.1
  331.2 2.8 multiply_subtract_fusion.2
  341.5 8.7 %collective-permute-done.86 = f32[2,2,32,384]{3,2,1,0:T(8,128)S(1)} collective-permute-done((f32[2,2,32,384]{3,2,1,0:T(8,128)S(1)}, f32[2,2,32,384]{3,2,1,0:T(8,128)S(1)}, u32[]{:S(2)}, u32[]{:S(2)}) %collective-permute-start.86) | collective-permute-done | bytes 196640 | tf_op jit(solution)/shard_map/ppermute | solution.py:191
  (659 shorter events, 164.0 us)
Async XLA Ops:
  7.2 98.0 %all-gather.6.cloned.1.call-start = ((), (), s32[]{:S(2)}) async-start(), calls=%async_computation.1 | async-start | bytes 2162688 | tf_op jit(solution)/shard_map/all_gather | solution.py:381
  22.6 24.3 %collective-permute-start.7 = (bf16[128,1024]{1,0:T(8,128)(2,1)S(1)}, bf16[128,1024]{1,0:T(8,128)(2,1)S(1)}, u32[]{:S(2)}, u32[]{:S(2)}) collective-permute-start(bf16[128,1024]{1,0:T(8,128)(2,1)S(1)} %copy-done.4), channel_id=1, source_target_pairs={{0,4},{2,6},{4,0},{6,2},{1,5},{3,7},{5,1},{7,3},{8,12},{10,14},{12... | collective-permute-start | bytes 786440 | tf_op jit(solution)/shard_map/ppermute | solution.py:191
  25.8 102.7 %all-gather.12.cloned.1.call-start = ((), (), s32[]{:S(2)}) async-start(), calls=%async_computation.5 | async-start | bytes 1310720 | tf_op jit(solution)/shard_map/all_gather | solution.py:438
  26.0 20.8 %collective-permute-start.8 = (bf16[128,1024]{1,0:T(8,128)(2,1)S(1)}, bf16[128,1024]{1,0:T(8,128)(2,1)S(1)}, u32[]{:S(2)}, u32[]{:S(2)}) collective-permute-start(bf16[128,1024]{1,0:T(8,128)(2,1)S(1)} %copy-done.4), channel_id=1, source_target_pairs={{0,6},{2,4},{4,2},{6,0},{1,7},{3,5},{5,3},{7,1},{8,14},{10,12},{12... | collective-permute-start | bytes 786440 | tf_op jit(solution)/shard_map/ppermute | solution.py:191
  27.5 24.8 %collective-permute-start.10 = (bf16[2,2,32,384]{3,2,1,0:T(8,128)(2,1)S(1)}, bf16[2,2,32,384]{3,2,1,0:T(8,128)(2,1)S(1)}, u32[]{:S(2)}, u32[]{:S(2)}) collective-permute-start(bf16[2,2,32,384]{3,2,1,0:T(8,128)(2,1)S(1)} %pad_maximum_fusion.25), channel_id=1, source_target_pairs={{0,4},{2,6},{4,0},{6,2},{1,5},{3,7},{5,1},{7,3},{8,12},{10,14},{12... | collective-permute-start | bytes 294920 | tf_op jit(solution)/shard_map/ppermute | solution.py:191
  29.3 23.0 %collective-permute-start.11 = (bf16[2,2,32,512]{3,2,1,0:T(8,128)(2,1)S(1)}, bf16[2,2,32,512]{3,2,1,0:T(8,128)(2,1)S(1)}, u32[]{:S(2)}, u32[]{:S(2)}) collective-permute-start(bf16[2,2,32,512]{3,2,1,0:T(8,128)(2,1)S(1)} %pad_maximum_fusion.16), channel_id=1, source_target_pairs={{0,16},{8,24},{16,0},{24,8},{1,17},{9,25},{17,1},{25,9},{2,18},{10... | collective-permute-start | bytes 393224 | tf_op jit(solution)/shard_map/ppermute | solution.py:191
  53.2 106.8 %all-gather.8.cloned.1.call-start = ((), (), s32[]{:S(2)}) async-start(), calls=%async_computation.2 | async-start | bytes 1310720 | tf_op jit(solution)/shard_map/all_gather | solution.py:442
  54.1 236.0 %all-gather.10.cloned.1.call-start = ((), (), s32[]{:S(2)}) async-start(), calls=%async_computation.3 | async-start | bytes 1966080 | tf_op jit(solution)/shard_map/all_gather | solution.py:509
  61.7 14.7 %collective-permute-start.22 = (bf16[128,1024]{1,0:T(8,128)(2,1)}, bf16[128,1024]{1,0:T(8,128)(2,1)S(1)}, u32[]{:S(2)}, u32[]{:S(2)}) collective-permute-start(bf16[128,1024]{1,0:T(8,128)(2,1)} %copy-done.47), channel_id=1, source_target_pairs={{0,1},{1,0},{2,3},{3,2},{4,5},{5,4},{6,7},{7,6},{8,9},{9,8},{10,11... | collective-permute-start | bytes 786440 | tf_op jit(solution)/shard_map/ppermute | solution.py:191
  70.1 14.9 %collective-permute-start.16 = (bf16[8,32,384]{2,1,0:T(8,128)(2,1)S(1)}, bf16[8,32,384]{2,1,0:T(8,128)(2,1)S(1)}, u32[]{:S(2)}, u32[]{:S(2)}) collective-permute-start(bf16[8,32,384]{2,1,0:T(8,128)(2,1)S(1)} %pad_maximum_fusion.8), channel_id=1, source_target_pairs={{0,16},{8,24},{16,0},{24,8},{1,17},{9,25},{17,1},{25,9},{2,18},{10... | collective-permute-start | bytes 589832 | tf_op jit(solution)/shard_map/ppermute | solution.py:191
  70.7 14.3 %collective-permute-start.17 = (bf16[8,32,384]{2,1,0:T(8,128)(2,1)S(1)}, bf16[8,32,384]{2,1,0:T(8,128)(2,1)S(1)}, u32[]{:S(2)}, u32[]{:S(2)}) collective-permute-start(bf16[8,32,384]{2,1,0:T(8,128)(2,1)S(1)} %pad_maximum_fusion.8), channel_id=1, source_target_pairs={{0,24},{8,16},{16,8},{24,0},{1,25},{9,17},{17,9},{25,1},{2,26},{10... | collective-permute-start | bytes 589832 | tf_op jit(solution)/shard_map/ppermute | solution.py:191
  104.9 13.6 %collective-permute-start.35 = (bf16[2,128,1024]{2,1,0:T(8,128)(2,1)S(1)}, bf16[2,128,1024]{2,1,0:T(8,128)(2,1)}, u32[]{:S(2)}, u32[]{:S(2)}) collective-permute-start(bf16[2,128,1024]{2,1,0:T(8,128)(2,1)S(1)} %pad_maximum_fusion.2), channel_id=1, source_target_pairs={{0,16},{8,24},{16,0},{24,8},{1,17},{9,25},{17,1},{25,9},{2,18},{10... | collective-permute-start | bytes 1572872 | tf_op jit(solution)/shard_map/ppermute | solution.py:191
  107.3 23.7 %collective-permute-start.25 = (bf16[2,128,128]{2,1,0:T(8,128)(2,1)S(1)}, bf16[2,128,128]{2,1,0:T(8,128)(2,1)S(1)}, u32[]{:S(2)}, u32[]{:S(2)}) collective-permute-start(bf16[2,128,128]{2,1,0:T(8,128)(2,1)S(1)} %pad_maximum_fusion.35), channel_id=1, source_target_pairs={{0,4},{2,6},{4,0},{6,2},{1,5},{3,7},{5,1},{7,3},{8,12},{10,14},{12... | collective-permute-start | bytes 196616 | tf_op jit(solution)/shard_map/ppermute | solution.py:191
  108.4 22.6 %collective-permute-start.24 = (bf16[2,128,128]{2,1,0:T(8,128)(2,1)S(1)}, bf16[2,128,128]{2,1,0:T(8,128)(2,1)}, u32[]{:S(2)}, u32[]{:S(2)}) collective-permute-start(bf16[2,128,128]{2,1,0:T(8,128)(2,1)S(1)} %pad_maximum_fusion.34), channel_id=1, source_target_pairs={{0,6},{2,4},{4,2},{6,0},{1,7},{3,5},{5,3},{7,1},{8,14},{10,12},{12... | collective-permute-start | bytes 196616 | tf_op jit(solution)/shard_map/ppermute | solution.py:191
  110.0 21.0 %collective-permute-start.26 = (bf16[2,128,128]{2,1,0:T(8,128)(2,1)S(1)}, bf16[2,128,128]{2,1,0:T(8,128)(2,1)}, u32[]{:S(2)}, u32[]{:S(2)}) collective-permute-start(bf16[2,128,128]{2,1,0:T(8,128)(2,1)S(1)} %pad_maximum_fusion.36), channel_id=1, source_target_pairs={{0,2},{2,0},{4,6},{6,4},{1,3},{3,1},{5,7},{7,5},{8,10},{10,8},{12,... | collective-permute-start | bytes 196616 | tf_op jit(solution)/shard_map/ppermute | solution.py:191
  135.3 16.4 %collective-permute-start.27 = (bf16[128,1024]{1,0:T(8,128)(2,1)}, bf16[128,1024]{1,0:T(8,128)(2,1)}, u32[]{:S(2)}, u32[]{:S(2)}) collective-permute-start(bf16[128,1024]{1,0:T(8,128)(2,1)} %get-tuple-element.167), channel_id=1, source_target_pairs={{0,1},{1,0},{2,3},{3,2},{4,5},{5,4},{6,7},{7,6},{8,9},{9,8},{10,11... | collective-permute-start | bytes 786440 | tf_op jit(solution)/shard_map/ppermute | solution.py:191
  136.8 14.4 %collective-permute-start.30 = (bf16[128,1024]{1,0:T(8,128)(2,1)}, bf16[128,1024]{1,0:T(8,128)(2,1)}, u32[]{:S(2)}, u32[]{:S(2)}) collective-permute-start(bf16[128,1024]{1,0:T(8,128)(2,1)} %get-tuple-element.167), channel_id=1, source_target_pairs={{0,16},{8,24},{16,0},{24,8},{1,17},{9,25},{17,1},{25,9},{2,18},{10... | collective-permute-start | bytes 786440 | tf_op jit(solution)/shard_map/ppermute | solution.py:191
  140.3 152.5 %reduce-scatter.2.cloned.1.call-start = ((), (), s32[]{:S(2)}) async-start(), calls=%async_computation.4 | async-start | bytes 1310720 | tf_op jit(solution)/shard_map/reduce_scatter | solution.py:564
  170.2 16.2 %collective-permute-start.45 = (bf16[2,128,1024]{2,1,0:T(8,128)(2,1)S(1)}, bf16[2,128,1024]{2,1,0:T(8,128)(2,1)S(1)}, u32[]{:S(2)}, u32[]{:S(2)}) collective-permute-start(bf16[2,128,1024]{2,1,0:T(8,128)(2,1)S(1)} %pad_maximum_fusion.3), channel_id=1, source_target_pairs={{0,2},{2,0},{4,6},{6,4},{1,3},{3,1},{5,7},{7,5},{8,10},{10,8},{12,... | collective-permute-start | bytes 1572872 | tf_op jit(solution)/shard_map/ppermute | solution.py:191
  175.8 18.9 %collective-permute-start.46 = (bf16[128,1024]{1,0:T(8,128)(2,1)S(1)}, bf16[128,1024]{1,0:T(8,128)(2,1)S(1)}, u32[]{:S(2)}, u32[]{:S(2)}) collective-permute-start(bf16[128,1024]{1,0:T(8,128)(2,1)S(1)} %get-tuple-element.178), channel_id=1, source_target_pairs={{0,16},{8,24},{16,0},{24,8},{1,17},{9,25},{17,1},{25,9},{2,18},{10... | collective-permute-start | bytes 786440 | tf_op jit(solution)/shard_map/ppermute | solution.py:191
  176.5 21.1 %collective-permute-start.42 = (bf16[128,1024]{1,0:T(8,128)(2,1)S(1)}, bf16[128,1024]{1,0:T(8,128)(2,1)S(1)}, u32[]{:S(2)}, u32[]{:S(2)}) collective-permute-start(bf16[128,1024]{1,0:T(8,128)(2,1)S(1)} %get-tuple-element.180), channel_id=1, source_target_pairs={{0,8},{8,0},{16,24},{24,16},{1,9},{9,1},{17,25},{25,17},{2,10},{10... | collective-permute-start | bytes 786440 | tf_op jit(solution)/shard_map/ppermute | solution.py:191
  201.3 21.0 %collective-permute-start.53 = (bf16[1,128,1024]{2,1,0:T(8,128)(2,1)S(1)}, bf16[1,128,1024]{2,1,0:T(8,128)(2,1)S(1)}, u32[]{:S(2)}, u32[]{:S(2)}) collective-permute-start(bf16[1,128,1024]{2,1,0:T(8,128)(2,1)S(1)} %add_convert_fusion.3), channel_id=1, source_target_pairs={{0,4},{2,6},{4,0},{6,2},{1,5},{3,7},{5,1},{7,3},{8,12},{10,14},{12... | collective-permute-start | bytes 786440 | tf_op jit(solution)/shard_map/ppermute | solution.py:191
  203.1 19.2 %collective-permute-start.57 = (bf16[128,1024]{1,0:T(8,128)(2,1)S(1)}, bf16[128,1024]{1,0:T(8,128)(2,1)S(1)}, u32[]{:S(2)}, u32[]{:S(2)}) collective-permute-start(bf16[128,1024]{1,0:T(8,128)(2,1)S(1)} %get-tuple-element.188), channel_id=1, source_target_pairs={{0,1},{1,0},{2,3},{3,2},{4,5},{5,4},{6,7},{7,6},{8,9},{9,8},{10,11... | collective-permute-start | bytes 786440 | tf_op jit(solution)/shard_map/ppermute | solution.py:191
  204.8 17.5 %collective-permute-start.56 = (bf16[2,128,1024]{2,1,0:T(8,128)(2,1)S(1)}, bf16[2,128,1024]{2,1,0:T(8,128)(2,1)S(1)}, u32[]{:S(2)}, u32[]{:S(2)}) collective-permute-start(bf16[2,128,1024]{2,1,0:T(8,128)(2,1)S(1)} %pad_maximum_fusion.4), channel_id=1, source_target_pairs={{0,16},{8,24},{16,0},{24,8},{1,17},{9,25},{17,1},{25,9},{2,18},{10... | collective-permute-start | bytes 1572872 | tf_op jit(solution)/shard_map/ppermute | solution.py:191
  206.3 14.5 %collective-permute-start.51 = (bf16[2,128,128]{2,1,0:T(8,128)(2,1)S(1)}, bf16[2,128,128]{2,1,0:T(8,128)(2,1)S(1)}, u32[]{:S(2)}, u32[]{:S(2)}) collective-permute-start(bf16[2,128,128]{2,1,0:T(8,128)(2,1)S(1)} %pad_maximum_fusion.39), channel_id=1, source_target_pairs={{0,4},{2,6},{4,0},{6,2},{1,5},{3,7},{5,1},{7,3},{8,12},{10,14},{12... | collective-permute-start | bytes 196616 | tf_op jit(solution)/shard_map/ppermute | solution.py:191
  223.8 24.9 %collective-permute-start.48 = (bf16[128,1024]{1,0:T(8,128)(2,1)}, bf16[128,1024]{1,0:T(8,128)(2,1)}, u32[]{:S(2)}, u32[]{:S(2)}) collective-permute-start(bf16[128,1024]{1,0:T(8,128)(2,1)} %get-tuple-element.187), channel_id=1, source_target_pairs={{0,1},{1,0},{2,3},{3,2},{4,5},{5,4},{6,7},{7,6},{8,9},{9,8},{10,11... | collective-permute-start | bytes 786440 | tf_op jit(solution)/shard_map/ppermute | solution.py:191
  244.4 41.6 %collective-permute-start.71 = (bf16[4,4,32,1024]{3,2,1,0:T(8,128)(2,1)S(1)}, bf16[4,4,32,1024]{3,2,1,0:T(8,128)(2,1)}, u32[]{:S(2)}, u32[]{:S(2)}) collective-permute-start(bf16[4,4,32,1024]{3,2,1,0:T(8,128)(2,1)S(1)} %fusion.14), channel_id=1, source_target_pairs={{0,1},{1,0},{2,3},{3,2},{4,5},{5,4},{6,7},{7,6},{8,9},{9,8},{10,11... | collective-permute-start | bytes 3145736 | tf_op jit(solution)/shard_map/ppermute | solution.py:191
  246.2 25.6 %collective-permute-start.63 = (bf16[128,1024]{1,0:T(8,128)(2,1)S(1)}, bf16[128,1024]{1,0:T(8,128)(2,1)S(1)}, u32[]{:S(2)}, u32[]{:S(2)}) collective-permute-start(bf16[128,1024]{1,0:T(8,128)(2,1)S(1)} %get-tuple-element.175), channel_id=1, source_target_pairs={{0,4},{2,6},{4,0},{6,2},{1,5},{3,7},{5,1},{7,3},{8,12},{10,14},{12... | collective-permute-start | bytes 786440 | tf_op jit(solution)/shard_map/ppermute | solution.py:191
  248.7 23.1 %collective-permute-start.61 = (bf16[128,1024]{1,0:T(8,128)(2,1)S(1)}, bf16[128,1024]{1,0:T(8,128)(2,1)S(1)}, u32[]{:S(2)}, u32[]{:S(2)}) collective-permute-start(bf16[128,1024]{1,0:T(8,128)(2,1)S(1)} %get-tuple-element.173), channel_id=1, source_target_pairs={{0,2},{2,0},{4,6},{6,4},{1,3},{3,1},{5,7},{7,5},{8,10},{10,8},{12,... | collective-permute-start | bytes 786440 | tf_op jit(solution)/shard_map/ppermute | solution.py:191
  252.0 27.2 %collective-permute-start.74 = (bf16[2,256,384]{2,1,0:T(8,128)(2,1)S(1)}, bf16[2,256,384]{2,1,0:T(8,128)(2,1)S(1)}, u32[]{:S(2)}, u32[]{:S(2)}) collective-permute-start(bf16[2,256,384]{2,1,0:T(8,128)(2,1)S(1)} %pad_maximum_fusion.6), channel_id=1, source_target_pairs={{0,16},{8,24},{16,0},{24,8},{1,17},{9,25},{17,1},{25,9},{2,18},{10... | collective-permute-start | bytes 1179656 | tf_op jit(solution)/shard_map/ppermute | solution.py:191
  281.1 25.1 %collective-permute-start.75 = (bf16[1,256,384]{2,1,0:T(8,128)(2,1)}, bf16[1,256,384]{2,1,0:T(8,128)(2,1)}, u32[]{:S(2)}, u32[]{:S(2)}) collective-permute-start(bf16[1,256,384]{2,1,0:T(8,128)(2,1)} %add_convert_fusion.5), channel_id=1, source_target_pairs={{0,8},{8,0},{16,24},{24,16},{1,9},{9,1},{17,25},{25,17},{2,10},{10... | collective-permute-start | bytes 589832 | tf_op jit(solution)/shard_map/ppermute | solution.py:191
  284.4 21.8 %collective-permute-start.69 = (f32[1,14336]{1,0:T(1,128)S(1)}, f32[1,14336]{1,0:T(1,128)S(1)}, u32[]{:S(2)}, u32[]{:S(2)}) collective-permute-start(f32[1,14336]{1,0:T(1,128)S(1)} %bitcast.669), channel_id=1, source_target_pairs={{0,8},{8,0},{16,24},{24,16},{1,9},{9,1},{17,25},{25,17},{2,10},{10... | collective-permute-start | bytes 172040 | tf_op jit(solution)/shard_map/ppermute | solution.py:191
  (164 other events, 1290.5 us)
Sparse Core Ops, SparseCore 0:
  25.9 65.1 all-gather.5
  93.3 35.2 all-gather.11
  130.7 26.7 all-gather.7
  159.8 38.0 all-gather.9
  224.0 26.0 reduce-scatter.1
